TPU v7x, 32 devices: a whole 2x2x4 slice. The times are simulated.
32 devices in a mesh: ctx: 16 (over z, x, core), head: 2 (over y).
Axes of the slice: x: 2, y: 2, z: 4, core: 2. Of those that a mesh axis runs over, the one named last changes fastest.
Arguments:
- query: bfloat16 [3072, 1024], P('ctx', 'head'), may hold values from -16 to 16
- key: bfloat16 [3072, 256], P('ctx', 'head'), may hold values from -4 to 4
- value: bfloat16 [3072, 256], P('ctx', 'head'), may hold values from -6 to 6
- tangent_query: bfloat16 [3072, 1024], P('ctx', 'head'), may hold values from -6 to 6
- tangent_key: bfloat16 [3072, 256], P('ctx', 'head'), may hold values from -6 to 6
- tangent_value: bfloat16 [3072, 256], P('ctx', 'head'), may hold values from -6 to 6
- out_weight: bfloat16 [1024, 4096], P('head'), may hold values from -1.5 to 1.5
- block_order: int32 [32], replicated, may hold values from 0 to 31, as said below
Outputs:
- output: bfloat16 [3072, 4096], P(('ctx', 'head'))
- tangent_output: bfloat16 [3072, 4096], P(('ctx', 'head'))
Inputs may be any that keep to these rules, and one draw needn't show every extreme that they name: block_order is a permutation in mirrored pairs: entries 2c and 2c + 1 sum to 2 * 16 - 1, so every stored pair of runs holds one early and one late run.
All inputs are finite; a program needn't handle non-finite values.
Results may differ from a plain program's by a relative error of at most 0.014.
Values may be sent and summed in bfloat16 or wider, within the bound.
No kernel may reach another device: no remote copies, remote signals or barrier semaphores. Data moves between devices by JAX's collectives and lax.ppermute only.
A program may use at most 64 MiB of HBM per device.

v0:
```python
import jax
import jax.numpy as jnp
from jax import lax
from jax.sharding import PartitionSpec as P

HD = 128


def positions(rows, block_order, run_length):
    slots = jnp.arange(block_order.shape[0], dtype=jnp.int32)
    match = (rows // run_length)[:, None] == slots[None, :]
    picked = jnp.sum(jnp.where(match, block_order[None, :], 0), axis=1)
    return picked * run_length + rows % run_length


def block_size(count):
    for size in (1024, 512, 256):
        return size
    return count


def per_device(
    query, key, value, tangent_query, tangent_key, tangent_value, out_weight, block_order
):
    rows_local = query.shape[0]
    run_length = rows_local // 2
    local_heads = key.shape[1] // HD
    group = query.shape[1] // key.shape[1]
    scale = HD ** (-0.5)
    first_row = lax.axis_index("ctx") * rows_local
    query_place = positions(
        first_row + jnp.arange(rows_local, dtype=jnp.int32), block_order, run_length
    )
    queries = query.reshape(rows_local, local_heads, group, HD)
    tangent_queries = tangent_query.reshape(rows_local, local_heads, group, HD)

    def scores_of(left, keys):
        return jnp.einsum("tkgd,skd->kgts", left, keys, preferred_element_type=jnp.float32) * scale

    def visible_of(key_place):
        return key_place[None, None, None, :] <= query_place[None, None, :, None]

    def combine(weights_b, values):
        return jnp.einsum("kgts,skd->kgtd", weights_b, values, preferred_element_type=jnp.float32)

    stat_shape = (local_heads, group, rows_local)
    field_shape = (local_heads, group, rows_local, HD)
    lowest = jnp.full(stat_shape, -1e30, jnp.float32)
    zero_stat = jnp.zeros(stat_shape, jnp.float32)
    zero_field = jnp.zeros(field_shape, jnp.float32)

    def joint_update(state, parts, key_place):
        peak, total, shift, context, mixed_values, mixed_tangent = state
        keys, values, tangent_keys, tangent_values = parts
        visible = visible_of(key_place)
        scores = scores_of(queries, keys)
        new_peak = jnp.maximum(peak, jnp.max(jnp.where(visible, scores, -1e30), axis=-1))
        factor = jnp.exp(peak - new_peak)
        weights = jnp.where(visible, jnp.exp(scores - new_peak[..., None]), 0.0)
        weights_b = weights.astype(jnp.bfloat16)
        slopes = scores_of(tangent_queries, keys) + scores_of(queries, tangent_keys)
        product = weights * slopes
        total = total * factor + jnp.sum(weights, axis=-1)
        shift = shift * factor + jnp.sum(product, axis=-1)
        context = context * factor[..., None] + combine(weights_b, values)
        mixed_values = mixed_values * factor[..., None] + combine(
            product.astype(jnp.bfloat16), values
        )
        mixed_tangent = mixed_tangent * factor[..., None] + combine(weights_b, tangent_values)
        return (new_peak, total, shift, context, mixed_values, mixed_tangent)

    initial = (lowest, zero_stat, zero_stat, zero_field, zero_field, zero_field)
    piece = (
        lax.all_gather(key, "ctx", axis=0, tiled=True),
        lax.all_gather(value, "ctx", axis=0, tiled=True),
        lax.all_gather(tangent_key, "ctx", axis=0, tiled=True),
        lax.all_gather(tangent_value, "ctx", axis=0, tiled=True),
    )
    count = piece[0].shape[0]
    size = block_size(count)
    piece_rows = jnp.arange(count, dtype=jnp.int32)

    def visit(index, state):
        offset = index * size
        parts = tuple(
            (
                lax.dynamic_slice_in_dim(field, offset, size, 0).reshape(size, local_heads, HD)
                for field in piece
            )
        )
        key_place = positions(
            lax.dynamic_slice_in_dim(piece_rows, offset, size, 0), block_order, run_length
        )
        return joint_update(state, parts, key_place)

    peak, total, shift, context, mixed_values, mixed_tangent = lax.fori_loop(
        0, count // size, visit, initial
    )
    context = context / total[..., None]
    tangent_context = (mixed_values + mixed_tangent) / total[..., None] - (shift / total)[
        ..., None
    ] * context
    attn = context.astype(jnp.bfloat16).transpose(2, 0, 1, 3).reshape(rows_local, -1)
    tangent_attn = (
        tangent_context.astype(jnp.bfloat16).transpose(2, 0, 1, 3).reshape(rows_local, -1)
    )
    width = out_weight.shape[1]
    left = attn
    summed = lax.psum_scatter(
        jnp.concatenate(
            [
                jnp.dot(left, out_weight, preferred_element_type=jnp.float32),
                jnp.dot(tangent_attn, out_weight, preferred_element_type=jnp.float32),
            ],
            axis=1,
        ).astype(jnp.bfloat16),
        "head",
        scatter_dimension=0,
        tiled=True,
    ).astype(jnp.float32)
    return (summed[:, :width].astype(jnp.bfloat16), summed[:, width:].astype(jnp.bfloat16))


def solution(mesh):
    in_specs = (
        P("ctx", "head"),
        P("ctx", "head"),
        P("ctx", "head"),
        P("ctx", "head"),
        P("ctx", "head"),
        P("ctx", "head"),
        P("head", None),
        P(),
    )
    out_specs = (P(("ctx", "head"), None), P(("ctx", "head"), None))
    return jax.shard_map(
        per_device, mesh=mesh, in_specs=in_specs, out_specs=out_specs, check_vma=False
    )
```

profile of v0, /device:TPU:0, one launch (start us, length us, event | category | flops | bytes accessed | tf_op | source)
XLA Modules:
  0.0 188.3 jit_solution(16077859561106010599)
XLA Ops:
  7.2 0.0 reduce-scatter.2.cloned.1.call-start
  7.3 0.7 select_reduce_fusion.1
  8.0 0.6 fusion.50
  8.6 1.0 reshape.215
  9.6 1.0 reshape.216
  10.7 25.7 %all_gather.12 = bf16[3072,128]{1,0:T(8,128)(2,1)S(1)} all-gather(bf16[192,128]{1,0:T(8,128)(2,1)} %param.11), channel_id=1, replica_groups=mesh['ctx'=16,'head'=2] {'ctx'}, dimensions={0}, use_global_device_ids=true | all-gather | bytes 835584 | tf_op jit(solution)/shard_map/all_gather | solution.py:74
  36.4 19.8 %all_gather.14 = bf16[3072,128]{1,0:T(8,128)(2,1)S(1)} all-gather(bf16[192,128]{1,0:T(8,128)(2,1)} %param.12), channel_id=1, replica_groups=mesh['ctx'=16,'head'=2] {'ctx'}, dimensions={0}, use_global_device_ids=true | all-gather | bytes 835584 | tf_op jit(solution)/shard_map/all_gather | solution.py:75
  56.2 21.3 %all_gather.13 = bf16[3072,128]{1,0:T(8,128)(2,1)S(1)} all-gather(bf16[192,128]{1,0:T(8,128)(2,1)} %param.14), channel_id=1, replica_groups=mesh['ctx'=16,'head'=2] {'ctx'}, dimensions={0}, use_global_device_ids=true | all-gather | bytes 835584 | tf_op jit(solution)/shard_map/all_gather | solution.py:76
  77.5 21.2 %all_gather.15 = bf16[3072,128]{1,0:T(8,128)(2,1)} all-gather(bf16[192,128]{1,0:T(8,128)(2,1)} %param.15), channel_id=1, replica_groups=mesh['ctx'=16,'head'=2] {'ctx'}, dimensions={0}, use_global_device_ids=true | all-gather | bytes 835584 | tf_op jit(solution)/shard_map/all_gather | solution.py:77
  98.7 29.4 %while.26 = (s32[]{:T(128)}, f32[1,4,192]{2,1,0:T(4,128)S(1)}, f32[1,4,192]{2,1,0:T(4,128)}, f32[1,4,192]{2,1,0:T(4,128)}, f32[1,4,192,128]{3,2,1,0:T(8,128)}, /...) while((s32[]{:T(128)}, f32[1,4,192]{2,1,0:T(4,128)S(1)}, ...), condition=%wide.region_6.7_spmd.clone, body=%wide.region_1.6_spmd.clone.sunk | while | flops 1227248640 | bytes 34174268 | solution.py:96
  98.7 0.7 select_reduce_fusion.3
  99.5 0.8 broadcast_compare_fusion.2
  100.4 0.6 fusion.85
  100.9 0.8 fusion.83
  101.8 1.5 fusion.86
  103.3 1.0 fusion.87
  104.3 0.0 copy-done.3
  104.3 0.0 copy-start.4
  104.4 0.6 fusion.89
  105.0 0.0 copy-start.1
  105.0 1.9 fusion.90
  106.9 0.9 fusion.88
  107.8 0.0 copy-start.2
  107.8 0.7 copy-done.2
  108.5 0.7 select_reduce_fusion.3
  109.3 0.8 broadcast_compare_fusion.2
  110.1 0.6 fusion.85
  110.7 0.8 fusion.83
  111.6 1.5 fusion.86
  113.1 1.0 fusion.87
  114.1 0.0 copy-done.3
  114.1 0.0 copy-done.5
  114.1 0.0 copy-start.4
  114.2 0.6 fusion.89
  114.8 0.0 copy-start.1
  114.8 1.9 fusion.90
  116.7 0.9 fusion.88
  117.5 0.0 copy-start.2
  117.6 0.7 copy-done.2
  118.3 0.7 select_reduce_fusion.3
  119.1 0.8 broadcast_compare_fusion.2
  119.9 0.6 fusion.85
  120.5 0.8 fusion.83
  121.3 1.5 fusion.86
  122.9 1.0 fusion.87
  123.9 0.0 copy-done.5
  123.9 0.0 copy-start.4
  123.9 0.6 fusion.89
  124.5 0.0 copy-start.1
  124.5 1.9 fusion.90
  126.5 0.9 fusion.88
  127.3 0.0 copy-start.2
  127.3 0.7 copy-done.2
  128.1 0.7 divide_bitcast_fusion
  128.8 1.3 convert_bitcast_fusion
  130.1 0.2 copy.16
  130.2 0.0 copy-start
  130.2 0.2 copy.17
  130.4 3.3 %convolution_convert_fusion = bf16[192,4096]{1,0:T(8,128)(2,1)S(1)} fusion(bf16[512,4096]{1,0:T(8,128)(2,1)} %param.16, bf16[24,8,4,128]{3,2,1,0:T(4,128)(2,1)S(1)} %bitcast.160), kind=kOutput, calls=%fused_computation.60 | convolution fusion | flops 806092800 | bytes 5963776 | tf_op jit(solution)/shard_map/dot_general | solution.py:113
  133.7 1.0 convolution_convert_fusion.1
  134.8 2.0 %pad_maximum_fusion = bf16[192,8192]{1,0:T(8,128)(2,1)} fusion(bf16[192,4096]{1,0:T(8,128)(2,1)S(1)} %convolution_convert_fusion, bf16[192,4096]{1,0:T(8,128)(2,1)S(1)} %convolution_convert_fusion.1), kind=kLoop, calls=%fused_computation.62 | loop fusion | flops 6291456 | bytes 6291456 | tf_op jit(solution)/shard_map/concatenate | solution.py:110
  136.7 0.0 reduce-scatter.2.cloned.1.call-update
  136.7 42.0 %reduce-scatter.2.cloned.1.call-done = bf16[96,8192]{1,0:T(8,128)(2,1)} async-done(((bf16[192,8192]{1,0:T(8,128)(2,1)}), bf16[96,8192]{1,0:T(8,128)(2,1)}) %reduce-scatter.2.cloned.1.call-update) | async-done | bytes 1572880 | tf_op jit(solution)/shard_map/reduce_scatter | solution.py:109
  178.8 2.7 %fusion.54 = (bf16[96,4096]{1,0:T(8,128)(2,1)}, bf16[96,4096]{1,0:T(8,128)(2,1)}) fusion(bf16[96,8192]{1,0:T(8,128)(2,1)} %reduce-scatter.2.cloned.1.call-done), kind=kLoop, calls=%fused_computation.81 | loop fusion | bytes 3145728 | tf_op jit(solution)/shard_map/slice | solution.py:121
  (46 shorter events, 0.3 us)
Async XLA Ops:
  7.2 171.6 %reduce-scatter.2.cloned.1.call-start = ((), (), s32[]{:S(2)}) async-start(), calls=%async_computation.1 | async-start | bytes 4718592 | tf_op jit(solution)/shard_map/reduce_scatter | solution.py:109
  103.3 1.0 copy-start.3
  103.3 1.0 copy-start.5
  104.3 2.5 %copy-start.4 = (f32[1,4,192]{2,1,0:T(4,128)}, f32[1,4,192]{2,1,0:T(4,128)S(1)}, u32[]{:S(2)}) copy-start(f32[1,4,192]{2,1,0:T(4,128)S(1)} %get-tuple-element.672) | copy-start | bytes 9220 | tf_op jit(solution)/shard_map/while
  104.4 2.5 %copy-start.6 = (f32[1,4,192]{2,1,0:T(4,128)}, f32[1,4,192]{2,1,0:T(4,128)S(1)}, u32[]{:S(2)}) copy-start(f32[1,4,192]{2,1,0:T(4,128)S(1)} %get-tuple-element.673) | copy-start | bytes 9220 | tf_op jit(solution)/shard_map/while
  105.0 1.9 %copy-start.1 = (f32[1,4,192,128]{3,2,1,0:T(8,128)S(1)}, f32[1,4,192,128]{3,2,1,0:T(8,128)}, u32[]{:S(2)}) copy-start(f32[1,4,192,128]{3,2,1,0:T(8,128)} %get-tuple-element.654) | copy-start | bytes 1179652 | tf_op jit(solution)/shard_map/while
  107.8 0.7 copy-start.2
  113.1 1.0 copy-start.3
  113.1 1.0 copy-start.5
  114.1 2.5 %copy-start.4 = (f32[1,4,192]{2,1,0:T(4,128)}, f32[1,4,192]{2,1,0:T(4,128)S(1)}, u32[]{:S(2)}) copy-start(f32[1,4,192]{2,1,0:T(4,128)S(1)} %get-tuple-element.672) | copy-start | bytes 9220 | tf_op jit(solution)/shard_map/while
  114.1 2.5 %copy-start.6 = (f32[1,4,192]{2,1,0:T(4,128)}, f32[1,4,192]{2,1,0:T(4,128)S(1)}, u32[]{:S(2)}) copy-start(f32[1,4,192]{2,1,0:T(4,128)S(1)} %get-tuple-element.673) | copy-start | bytes 9220 | tf_op jit(solution)/shard_map/while
  114.8 1.9 %copy-start.1 = (f32[1,4,192,128]{3,2,1,0:T(8,128)S(1)}, f32[1,4,192,128]{3,2,1,0:T(8,128)}, u32[]{:S(2)}) copy-start(f32[1,4,192,128]{3,2,1,0:T(8,128)} %get-tuple-element.654) | copy-start | bytes 1179652 | tf_op jit(solution)/shard_map/while
  117.5 0.7 copy-start.2
  122.9 1.0 copy-start.3
  122.9 1.0 copy-start.5
  123.9 2.5 %copy-start.4 = (f32[1,4,192]{2,1,0:T(4,128)}, f32[1,4,192]{2,1,0:T(4,128)S(1)}, u32[]{:S(2)}) copy-start(f32[1,4,192]{2,1,0:T(4,128)S(1)} %get-tuple-element.672) | copy-start | bytes 9220 | tf_op jit(solution)/shard_map/while
  123.9 2.5 %copy-start.6 = (f32[1,4,192]{2,1,0:T(4,128)}, f32[1,4,192]{2,1,0:T(4,128)S(1)}, u32[]{:S(2)}) copy-start(f32[1,4,192]{2,1,0:T(4,128)S(1)} %get-tuple-element.673) | copy-start | bytes 9220 | tf_op jit(solution)/shard_map/while
  124.5 1.9 %copy-start.1 = (f32[1,4,192,128]{3,2,1,0:T(8,128)S(1)}, f32[1,4,192,128]{3,2,1,0:T(8,128)}, u32[]{:S(2)}) copy-start(f32[1,4,192,128]{3,2,1,0:T(8,128)} %get-tuple-element.654) | copy-start | bytes 1179652 | tf_op jit(solution)/shard_map/while
  127.3 0.7 copy-start.2
  130.2 3.5 %copy-start = (bf16[512,4096]{1,0:T(8,128)(2,1)S(1)}, bf16[512,4096]{1,0:T(8,128)(2,1)}, u32[]{:S(2)}) copy-start(bf16[512,4096]{1,0:T(8,128)(2,1)} %param.16) | copy-start | bytes 12582916
Sparse Core Ops, SparseCore 0:
  136.9 41.8 reduce-scatter.1
where the time goes:
time: 189 us; the launch traced here: 188 us
  blocking collectives  88.1 us (47%)
  waiting for transfers between devices  42 us (22%)
  matrix products  23.1 us (12%)
  between operations  14.2 us (8%)
  other arithmetic  13.2 us (7%)
  local copies, waits for them, and re-layouts  7.3 us (4%)
    reduce_scatter x1, waiting for transfers between devices, per_device(): lax.psum_scatter(jnp.concatenate([jnp.dot(left, out_weight, preferred_ele...  42 us
    all_gather x1, blocking collectives, per_device(): lax.all_gather(key, 'ctx', axis=0, tiled=True)  25.7 us
    all_gather x1, blocking collectives, per_device(): lax.all_gather(tangent_key, 'ctx', axis=0, tiled=True)  21.3 us
    all_gather x1, blocking collectives, per_device(): lax.all_gather(tangent_value, 'ctx', axis=0, tiled=True)  21.2 us
    all_gather x1, blocking collectives, per_device(): lax.all_gather(value, 'ctx', axis=0, tiled=True)  19.8 us
    dot_general x9, matrix products, combine(): jnp.einsum('kgts,skd->kgtd', weights_b, values, preferred_element_type=jn...  9.98 us
    dot_general x9, matrix products, scores_of(): jnp.einsum('tkgd,skd->kgts', left, keys, preferred_element_type=jnp.float32)  8.8 us
  transfers between devices with their start and end apart: 1, of which 1 were waited for; matrix products, arithmetic and copies ran while one was open for 0% of the time, Pallas kernels for 0%

commit v1 on v0

v1 whole, which is shorter than its diff:
```python
import functools

import jax
import jax.numpy as jnp
from jax import lax
from jax.experimental import pallas as pl
from jax.experimental.pallas import tpu as pltpu
from jax.sharding import PartitionSpec as P

HD = 128
LOG2E = 1.4426950408889634
LOWEST = -1e30
VMEM = pl.BlockSpec(memory_space=pltpu.VMEM)
SMEM = pl.BlockSpec(memory_space=pltpu.SMEM)


def lanes(column, width):
    return jnp.broadcast_to(column, (column.shape[0], width))


def attend_kernel(
    sizes, meta, order, query, tangent_query, *refs
):
    packs, run, group, chunk = sizes
    pack_refs = refs[:packs]
    first_ref, second_ref = refs[packs : packs + 2]
    line, top, total, shift, both, mixed = refs[packs + 2 :]
    scale = HD ** (-0.5)

    at = 2
    for ref in pack_refs:
        for block in range(ref.shape[0] // (2 * run)):
            source = meta[at]
            at += 1
            for half in range(2):
                place = order[2 * source + half]
                rows = pl.ds(pl.multiple_of(place * run, run), run)
                begin = (2 * block + half) * run
                line[rows, :] = ref[begin : begin + run, :]

    me = meta[0]
    for step, out in enumerate((first_ref, second_ref)):
        half = meta[1] if step == 0 else 1 - meta[1]
        place = order[2 * me + half]
        rows = pl.ds(pl.multiple_of(half * run, run), run)
        q = [query[rows, h * HD : (h + 1) * HD] for h in range(group)]
        tq = [tangent_query[rows, h * HD : (h + 1) * HD] for h in range(group)]
        q = jnp.concatenate(q, axis=0)
        tq_q = jnp.concatenate([jnp.concatenate(tq, axis=0), q], axis=1)
        height = group * run
        top[...] = jnp.full(top.shape, LOWEST, jnp.float32)
        total[...] = jnp.zeros(total.shape, jnp.float32)
        shift[...] = jnp.zeros(shift.shape, jnp.float32)
        both[...] = jnp.zeros(both.shape, jnp.float32)
        mixed[...] = jnp.zeros(mixed.shape, jnp.float32)

        def visit(index, masked):
            cols = pl.ds(pl.multiple_of(index * chunk, chunk), chunk)
            keys = line[cols, 0:HD]
            keys_both = line[cols, 0 : 2 * HD]
            values = line[cols, 2 * HD : 3 * HD]
            values_both = line[cols, 2 * HD : 4 * HD]
            nt = (((1,), (1,)), ((), ()))
            scores = lax.dot_general(q, keys, nt, preferred_element_type=jnp.float32)
            scores = scores * (scale * LOG2E)
            if masked:
                col = index * chunk + lax.broadcasted_iota(jnp.int32, (height, chunk), 1)
                row = lax.rem(lax.broadcasted_iota(jnp.int32, (height, chunk), 0), run)
                scores = jnp.where(col <= place * run + row, scores, LOWEST)
            old = top[...]
            new = jnp.maximum(old, lanes(jnp.max(scores, axis=1, keepdims=True), HD))
            factor = jnp.exp2(old - new)
            top[...] = new
            weights = jnp.exp2(scores - jnp.tile(new, (1, chunk // HD)))
            slopes = lax.dot_general(tq_q, keys_both, nt, preferred_element_type=jnp.float32)
            product = weights * slopes
            weights_b = weights.astype(jnp.bfloat16)
            product_b = product.astype(jnp.bfloat16)
            part = weights[:, 0:HD]
            part_shift = product[:, 0:HD]
            for k in range(1, chunk // HD):
                part = part + weights[:, k * HD : (k + 1) * HD]
                part_shift = part_shift + product[:, k * HD : (k + 1) * HD]
            total[...] = total[...] * factor + part
            shift[...] = shift[...] * factor + part_shift
            both[...] = both[...] * jnp.tile(factor, (1, 2)) + jnp.dot(
                weights_b, values_both, preferred_element_type=jnp.float32
            )
            mixed[...] = mixed[...] * factor + jnp.dot(
                product_b, values, preferred_element_type=jnp.float32
            )

        whole = place * run // chunk

        @pl.loop(0, whole)
        def _(index):
            visit(index, False)

        visit(whole, True)
        inverse = lanes(1.0 / jnp.sum(total[...], axis=1, keepdims=True), HD)
        shifted = lanes(jnp.sum(shift[...], axis=1, keepdims=True), HD) * (scale * inverse)
        context = both[:, 0:HD] * inverse
        tangent = (mixed[...] * scale + both[:, HD : 2 * HD]) * inverse - shifted * context
        for h in range(group):
            out[0:run, h * HD : (h + 1) * HD] = context[h * run : (h + 1) * run].astype(out.dtype)
            out[run : 2 * run, h * HD : (h + 1) * HD] = tangent[h * run : (h + 1) * run].astype(
                out.dtype
            )


def attend(meta, order, query, tangent_query, packs):
    rows, width = query.shape
    run, group = rows // 2, width // HD
    count = sum(pack.shape[0] for pack in packs)
    chunk = 4 * run
    height = group * run
    out = jax.ShapeDtypeStruct((rows, width), jnp.bfloat16)
    sizes = (len(packs), run, group, chunk)
    flops = 2 * height * count * HD * 6
    return pl.pallas_call(
        functools.partial(attend_kernel, sizes),
        out_shape=(out, out),
        in_specs=[SMEM, SMEM] + [VMEM] * (2 + len(packs)),
        out_specs=(VMEM, VMEM),
        scratch_shapes=[
            pltpu.VMEM((count, 4 * HD), jnp.bfloat16),
            pltpu.VMEM((height, HD), jnp.float32),
            pltpu.VMEM((height, HD), jnp.float32),
            pltpu.VMEM((height, HD), jnp.float32),
            pltpu.VMEM((height, 2 * HD), jnp.float32),
            pltpu.VMEM((height, HD), jnp.float32),
        ],
        compiler_params=pltpu.CompilerParams(vmem_limit_bytes=40 * 2**20),
        cost_estimate=pl.CostEstimate(
            flops=flops, bytes_accessed=count * 8 * HD, transcendentals=height * count
        ),
        name="attend",
    )(meta, order, query, tangent_query, *packs)


def project_own_kernel(left, weight, out):
    out[...] = jnp.dot(left[...], weight[...], preferred_element_type=jnp.float32).astype(out.dtype)


def project_own(left, weight, tile=512):
    rows, depth = left.shape
    width = weight.shape[1]
    return pl.pallas_call(
        project_own_kernel,
        out_shape=jax.ShapeDtypeStruct((rows, width), jnp.bfloat16),
        grid=(width // tile,),
        in_specs=[
            pl.BlockSpec((rows, depth), lambda k: (0, 0)),
            pl.BlockSpec((depth, tile), lambda k: (0, k)),
        ],
        out_specs=pl.BlockSpec((rows, tile), lambda k: (0, k)),
        compiler_params=pltpu.CompilerParams(vmem_limit_bytes=20 * 2**20),
        cost_estimate=pl.CostEstimate(
            flops=2 * rows * depth * width, bytes_accessed=2 * depth * width, transcendentals=0
        ),
        name="project_own",
    )(left, weight)


def project_other_kernel(starts, left, partial, *refs):
    pieces, (out, tangent_out) = refs[:-2], refs[-2:]
    run = left.shape[0] // 2
    left = left[...]
    for n, piece in enumerate(pieces):
        width = piece.shape[1]
        cols = pl.ds(pl.multiple_of(starts[n], HD), width)
        other = jnp.dot(left, piece[...], preferred_element_type=jnp.float32)
        other = other.astype(jnp.bfloat16).astype(jnp.float32)
        sums = (partial[:, cols].astype(jnp.float32) + other).astype(out.dtype)
        out[:, cols] = sums[0:run]
        tangent_out[:, cols] = sums[run : 2 * run]


def project_other(starts, left, partial, pieces):
    rows = left.shape[0]
    width = partial.shape[1]
    out = jax.ShapeDtypeStruct((rows // 2, width), jnp.bfloat16)
    return pl.pallas_call(
        project_other_kernel,
        out_shape=(out, out),
        in_specs=[SMEM] + [VMEM] * (2 + len(pieces)),
        out_specs=(VMEM, VMEM),
        compiler_params=pltpu.CompilerParams(vmem_limit_bytes=40 * 2**20),
        cost_estimate=pl.CostEstimate(
            flops=2 * rows * left.shape[1] * width,
            bytes_accessed=2 * left.shape[1] * width,
            transcendentals=0,
        ),
        name="project_other",
    )(starts, left, partial, *pieces)


def whole_program(
    query, key, value, tangent_query, tangent_key, tangent_value, out_weight, block_order, axes
):
    run = query.shape[0] // 2
    pack = jnp.concatenate([key, tangent_key, value, tangent_value], axis=1)
    gathered = lax.all_gather(pack, "ctx", axis=0, tiled=True)
    me = lax.axis_index("ctx").astype(jnp.int32)
    meta = jnp.concatenate(
        [jnp.stack([me, jnp.int32(0)]), jnp.arange(axes["ctx"], dtype=jnp.int32)]
    )
    first, second = attend(meta, block_order, query, tangent_query, [gathered])
    left = jnp.concatenate([first[:run], second[:run], first[run:], second[run:]], axis=0)
    partial = project_own(left, out_weight)
    both = jnp.concatenate([partial[: 2 * run], partial[2 * run :]], axis=1)
    summed = lax.psum_scatter(both, "head", scatter_dimension=0, tiled=True)
    width = out_weight.shape[1]
    return summed[:, :width], summed[:, width:]


def paired_program(
    query, key, value, tangent_query, tangent_key, tangent_value, out_weight, block_order, axes
):
    count = axes["ctx"]
    width = out_weight.shape[1]
    me = lax.axis_index("ctx").astype(jnp.int32)
    side = lax.axis_index("head").astype(jnp.int32)

    def swap(array, bits):
        return lax.ppermute(array, "ctx", [(i, i ^ bits) for i in range(count)])

    def cross(array):
        return lax.ppermute(array, "head", [(0, 1), (1, 0)])

    core, level = me & 1, (me >> 2) & 1
    quarter, eighth = width // 4, width // 8
    direct_start = core * quarter
    shared_start = width // 2 + (2 * level + core) * eighth
    shared = cross(lax.dynamic_slice_in_dim(out_weight, shared_start, eighth, 1))
    direct = cross(lax.dynamic_slice_in_dim(out_weight, direct_start, quarter, 1))

    pack = jnp.concatenate([key, tangent_key, value, tangent_value], axis=1)
    bits, packs = [0], [pack]
    for step in (4, 8, 12):
        bits.append(step)
        packs.append(swap(pack, step))
    for n in range(4):
        bits.append(bits[n] ^ 2)
        packs.append(swap(packs[n], 2))
    for n in range(8):
        bits.append(bits[n] ^ 1)
        packs.append(swap(packs[n], 1))
    meta = jnp.stack([me, 1 - side] + [me ^ b for b in bits])
    theirs, mine = attend(meta, block_order, query, tangent_query, packs)

    shared_z = swap(shared, 4)
    pieces = [direct, swap(direct, 1), shared, shared_z, swap(shared, 1), swap(shared_z, 1)]
    half = width // 2
    starts = jnp.stack(
        [
            direct_start,
            (1 - core) * quarter,
            half + (2 * level + core) * eighth,
            half + (2 * (1 - level) + core) * eighth,
            half + (2 * level + 1 - core) * eighth,
            half + (2 * (1 - level) + 1 - core) * eighth,
        ]
    )
    other = cross(theirs)
    partial = project_own(mine, out_weight)
    return project_other(starts, other, partial, pieces)


def solution(mesh):
    axes = dict(mesh.shape)
    program = paired_program if axes == {"ctx": 16, "head": 2} else whole_program
    in_specs = (
        P("ctx", "head"),
        P("ctx", "head"),
        P("ctx", "head"),
        P("ctx", "head"),
        P("ctx", "head"),
        P("ctx", "head"),
        P("head", None),
        P(),
    )
    out_specs = (P(("ctx", "head"), None), P(("ctx", "head"), None))
    return jax.shard_map(
        functools.partial(program, axes=axes),
        mesh=mesh,
        in_specs=in_specs,
        out_specs=out_specs,
        check_vma=False,
    )
```

time: 189 us -> 91.3 us (0.48)
  blocking collectives: 88.1 us -> 0 us
  matrix products: 23.1 us -> 0 us
  local copies, waits for them, and re-layouts: 7.3 us -> 29.7 us
  starting transfers between devices: 0.04 us -> 18.7 us
  waiting for transfers between devices: 42 us -> 27.8 us
  between operations: 14.2 us -> 0.75 us
  Pallas kernels: 0 us -> 13.4 us
  other arithmetic: 13.2 us -> 0 us
    all_gather x4 -> x0, blocking collectives: 88.1 us -> none  [the longest x1 25.7 us: per_device(): lax.all_gather(key, 'ctx', axis=0, tiled=True)]
    reduce_scatter x1 -> x0, waiting for transfers between devices: 42 us -> none  [per_device(): lax.psum_scatter(jnp.concatenate([jnp.dot(left, out_weight, preferred_ele...]
    ppermute x0 -> x22, waiting for transfers between devices: none -> 27.8 us  [the longest x19 19.8 us: swap(): return lax.ppermute(array, 'ctx', [(i, i ^ bits) for i in range(count)])]
    unnamed x4 -> x59, local copies, waits for them, and re-layouts: 0.06 us -> 26.4 us
    dot_general x20 -> x0, matrix products: 23.1 us -> none  [the longest x9 9.98 us: combine(): jnp.einsum('kgts,skd->kgtd', weights_b, values, preferred_element_type=jn...]
    ppermute x0 -> x22, starting transfers between devices: none -> 18.7 us  [the longest x19 14.1 us: swap(): return lax.ppermute(array, 'ctx', [(i, i ^ bits) for i in range(count)])]
    pallas_call x0 -> x3, Pallas kernels: none -> 13.4 us  [the longest x1 7.42 us: attend(): pl.pallas_call(functools.partial(attend_kernel, sizes), out_shape=(out, o...]
    reduce_sum x7 -> x0, other arithmetic: 5.9 us -> none  [the longest x4 2.98 us: positions(): picked = jnp.sum(jnp.where(match, block_order[None, :], 0), axis=1)]
  transfers between devices with their start and end apart: 1 -> 22, of which waited for: 1 -> 9; matrix products, arithmetic and copies ran while one was open for 0% -> 5% of each run, Pallas kernels for 0% -> 11%
where the time goes in v1:
time: 91.3 us; the launch traced here: 90.4 us
  local copies, waits for them, and re-layouts  29.7 us (33%)
  waiting for transfers between devices  27.8 us (30%)
  starting transfers between devices  18.7 us (20%)
  Pallas kernels  13.4 us (15%)
    unnamed x59, local copies, waits for them, and re-layouts  26.4 us
    ppermute x19, waiting for transfers between devices, swap(): return lax.ppermute(array, 'ctx', [(i, i ^ bits) for i in range(count)])  19.8 us
    ppermute x19, starting transfers between devices, swap(): return lax.ppermute(array, 'ctx', [(i, i ^ bits) for i in range(count)])  14.1 us
    ppermute x3, waiting for transfers between devices, cross(): return lax.ppermute(array, 'head', [(0, 1), (1, 0)])  7.99 us
    pallas_call x1, Pallas kernels, attend(): pl.pallas_call(functools.partial(attend_kernel, sizes), out_shape=(out, o...  7.42 us
    ppermute x3, starting transfers between devices, cross(): return lax.ppermute(array, 'head', [(0, 1), (1, 0)])  4.62 us
    pallas_call x1, Pallas kernels, project_other(): pl.pallas_call(project_other_kernel, out_shape=(out, out), in_specs=[SMEM...  3.35 us
    pallas_call x1, Pallas kernels, project_own(): pl.pallas_call(project_own_kernel, out_shape=jax.ShapeDtypeStruct((rows,...  2.6 us
  transfers between devices with their start and end apart: 22, of which 9 were waited for; matrix products, arithmetic and copies ran while one was open for 5% of the time, Pallas kernels for 11%

profile of v1, /device:TPU:0, one launch (start us, length us, event | category | flops | bytes accessed | tf_op | source)
XLA Modules:
  0.0 90.4 jit_solution(1313531411789721897)
XLA Ops:
  0.6 1.3 %constant_dynamic-slice_fusion.1 = bf16[512,1024]{1,0:T(8,128)(2,1)S(1)} fusion(bf16[512,4096]{1,0:T(8,128)(2,1)} %weight.1, s32[]{:T(128)S(6)} %select_n.6), kind=kLoop, calls=%fused_computation.5 | loop fusion | bytes 2097156 | tf_op jit(solution)/shard_map/dynamic_slice | solution.py:236
  1.9 3.0 %collective-permute-start.16 = (bf16[512,1024]{1,0:T(8,128)(2,1)S(1)}, bf16[512,1024]{1,0:T(8,128)(2,1)S(1)}, u32[]{:S(2)}, u32[]{:S(2)}) collective-permute-start(bf16[512,1024]{1,0:T(8,128)(2,1)S(1)} %constant_dynamic-slice_fusion.1), channel_id=1, source_target_pairs={{0,1},{1,0},{2,3},{3,2},{4,5},{5,4},{6,7},{7,6},{8,9},{9,8},{10,11... | collective-permute-start | bytes 3145736 | tf_op jit(solution)/shard_map/ppermute | solution.py:229
  5.0 1.1 %constant_dynamic-slice_fusion = bf16[512,512]{1,0:T(8,128)(2,1)S(1)} fusion(bf16[512,4096]{1,0:T(8,128)(2,1)} %weight.1, s32[]{:T(128)S(6)} %select_n.7), kind=kLoop, calls=%fused_computation.4 | loop fusion | bytes 1048580 | tf_op jit(solution)/shard_map/dynamic_slice | solution.py:235
  6.0 0.1 collective-permute-start.18
  6.1 0.8 constant_dynamic-update-slice_fusion.3
  7.0 0.8 constant_dynamic-update-slice_fusion.2
  7.8 0.8 constant_dynamic-update-slice_fusion.1
  8.6 0.8 constant_dynamic-update-slice_fusion.refs_0_
  9.4 0.1 collective-permute-start.7
  9.5 2.0 %collective-permute-start.3 = (bf16[192,512]{1,0:T(8,128)(2,1)S(1)}, bf16[192,512]{1,0:T(8,128)(2,1)S(1)}, u32[]{:S(2)}, u32[]{:S(2)}) collective-permute-start(bf16[192,512]{1,0:T(8,128)(2,1)S(1)} %constant_dynamic-update-slice_fusion.refs_0_), channel_id=1, source_target_pairs={{0,4},{2,6},{4,0},{6,2},{8,12},{10,14},{12,8},{14,10},{16,20},{18,... | collective-permute-start | bytes 589832 | tf_op jit(solution)/shard_map/ppermute | solution.py:226
  11.5 3.6 %collective-permute-start.2 = (bf16[192,512]{1,0:T(8,128)(2,1)S(1)}, bf16[192,512]{1,0:T(8,128)(2,1)S(1)}, u32[]{:S(2)}, u32[]{:S(2)}) collective-permute-start(bf16[192,512]{1,0:T(8,128)(2,1)S(1)} %constant_dynamic-update-slice_fusion.refs_0_), channel_id=1, source_target_pairs={{0,24},{2,26},{4,28},{6,30},{8,16},{10,18},{12,20},{14,22},{16,8},... | collective-permute-start | bytes 589832 | tf_op jit(solution)/shard_map/ppermute | solution.py:226
  15.1 0.7 copy-done.3
  15.8 1.2 %collective-permute-done.3.refs_4_ = bf16[192,512]{1,0:T(8,128)(2,1)S(1)} collective-permute-done((bf16[192,512]{1,0:T(8,128)(2,1)S(1)}, bf16[192,512]{1,0:T(8,128)(2,1)S(1)}, u32[]{:S(2)}, u32[]{:S(2)}) %collective-permute-start.3) | collective-permute-done | bytes 196640 | tf_op jit(solution)/shard_map/ppermute | solution.py:226
  17.0 1.8 %collective-permute-start = (bf16[192,512]{1,0:T(8,128)(2,1)S(1)}, bf16[192,512]{1,0:T(8,128)(2,1)S(1)}, u32[]{:S(2)}, u32[]{:S(2)}) collective-permute-start(bf16[192,512]{1,0:T(8,128)(2,1)S(1)} %constant_dynamic-update-slice_fusion.refs_0_), channel_id=1, source_target_pairs={{0,8},{2,10},{4,12},{6,14},{8,0},{10,2},{12,4},{14,6},{16,24},{18,... | collective-permute-start | bytes 589832 | tf_op jit(solution)/shard_map/ppermute | solution.py:226
  18.9 2.3 %collective-permute-done.2.refs_3_ = bf16[192,512]{1,0:T(8,128)(2,1)S(1)} collective-permute-done((bf16[192,512]{1,0:T(8,128)(2,1)S(1)}, bf16[192,512]{1,0:T(8,128)(2,1)S(1)}, u32[]{:S(2)}, u32[]{:S(2)}) %collective-permute-start.2) | collective-permute-done | bytes 196640 | tf_op jit(solution)/shard_map/ppermute | solution.py:226
  21.2 0.0 collective-permute-start.11
  21.2 0.7 copy-done.5
  21.8 10.3 %collective-permute-done.1.refs_2_ = bf16[192,512]{1,0:T(8,128)(2,1)S(1)} collective-permute-done((bf16[192,512]{1,0:T(8,128)(2,1)S(1)}, bf16[192,512]{1,0:T(8,128)(2,1)S(1)}, u32[]{:S(2)}, u32[]{:S(2)}) %collective-permute-start.1) | collective-permute-done | bytes 196640 | tf_op jit(solution)/shard_map/ppermute | solution.py:226
  32.2 7.2 %collective-permute-done.18.refs_2_ = bf16[512,512]{1,0:T(8,128)(2,1)S(1)} collective-permute-done((bf16[512,512]{1,0:T(8,128)(2,1)S(1)}, bf16[512,512]{1,0:T(8,128)(2,1)S(1)}, u32[]{:S(2)}, u32[]{:S(2)}) %collective-permute-start.18) | collective-permute-done | bytes 524320 | tf_op jit(solution)/shard_map/ppermute | solution.py:229
  39.4 1.8 %collective-permute-start.19 = (bf16[512,512]{1,0:T(8,128)(2,1)S(1)}, bf16[512,512]{1,0:T(8,128)(2,1)S(1)}, u32[]{:S(2)}, u32[]{:S(2)}) collective-permute-start(bf16[512,512]{1,0:T(8,128)(2,1)S(1)} %collective-permute-done.18.refs_2_), channel_id=1, source_target_pairs={{0,8},{2,10},{4,12},{6,14},{8,0},{10,2},{12,4},{14,6},{16,24},{18,... | collective-permute-start | bytes 1572872 | tf_op jit(solution)/shard_map/ppermute | solution.py:226
  41.2 1.6 %collective-permute-start.6 = (bf16[192,512]{1,0:T(8,128)(2,1)S(1)}, bf16[192,512]{1,0:T(8,128)(2,1)S(1)}, u32[]{:S(2)}, u32[]{:S(2)}) collective-permute-start(bf16[192,512]{1,0:T(8,128)(2,1)S(1)} %collective-permute-done.2.refs_3_), channel_id=1, source_target_pairs={{0,4},{2,6},{4,0},{6,2},{8,12},{10,14},{12,8},{14,10},{16,20},{18,... | collective-permute-start | bytes 589832 | tf_op jit(solution)/shard_map/ppermute | solution.py:226
  42.7 0.7 copy-done.7
  43.4 0.7 copy-done.13
  44.1 0.2 collective-permute-start.9
  44.3 0.7 copy-done.15
  45.0 0.5 collective-permute-start.5
  45.5 0.7 copy-done.9
  46.2 2.8 %collective-permute-done.6.refs_7_ = bf16[192,512]{1,0:T(8,128)(2,1)S(1)} collective-permute-done((bf16[192,512]{1,0:T(8,128)(2,1)S(1)}, bf16[192,512]{1,0:T(8,128)(2,1)S(1)}, u32[]{:S(2)}, u32[]{:S(2)}) %collective-permute-start.6) | collective-permute-done | bytes 196640 | tf_op jit(solution)/shard_map/ppermute | solution.py:226
  49.0 0.7 copy-done.19
  49.6 1.5 %collective-permute-start.4 = (bf16[192,512]{1,0:T(8,128)(2,1)S(1)}, bf16[192,512]{1,0:T(8,128)(2,1)}, u32[]{:S(2)}, u32[]{:S(2)}) collective-permute-start(bf16[192,512]{1,0:T(8,128)(2,1)S(1)} %collective-permute-done.refs_1_), channel_id=1, source_target_pairs={{0,4},{2,6},{4,0},{6,2},{8,12},{10,14},{12,8},{14,10},{16,20},{18,... | collective-permute-start | bytes 589832 | tf_op jit(solution)/shard_map/ppermute | solution.py:226
  51.1 0.7 copy-done.11
  51.8 0.9 collective-permute-done.5.refs_6_
  52.7 0.7 copy-done.17
  53.4 0.7 copy-done.23
  54.0 0.5 collective-permute-start.13
  54.6 0.7 copy-done.21
  55.2 1.8 %collective-permute-done.4.refs_5_ = bf16[192,512]{1,0:T(8,128)(2,1)} collective-permute-done((bf16[192,512]{1,0:T(8,128)(2,1)S(1)}, bf16[192,512]{1,0:T(8,128)(2,1)}, u32[]{:S(2)}, u32[]{:S(2)}) %collective-permute-start.4) | collective-permute-done | bytes 196640 | tf_op jit(solution)/shard_map/ppermute | solution.py:226
  57.1 0.7 copy-done.25
  57.7 0.5 collective-permute-start.20
  58.2 0.0 collective-permute-start.21
  58.2 0.1 stack.100.meta
  58.3 0.5 collective-permute-done.12.refs_13_
  58.8 0.9 %copy-done.1 = bf16[192,512]{1,0:T(8,128)(2,1)S(1)} copy-done((bf16[192,512]{1,0:T(8,128)(2,1)S(1)}, bf16[192,512]{1,0:T(8,128)(2,1)}, u32[]{:S(2)}) %copy-start.1) | copy-done | bytes 196632
  59.8 0.9 %copy-done.2 = bf16[192,512]{1,0:T(8,128)(2,1)S(1)} copy-done((bf16[192,512]{1,0:T(8,128)(2,1)S(1)}, bf16[192,512]{1,0:T(8,128)(2,1)}, u32[]{:S(2)}) %copy-start.2) | copy-done | bytes 196632
  60.7 0.9 %copy-done.4 = bf16[192,512]{1,0:T(8,128)(2,1)S(1)} copy-done((bf16[192,512]{1,0:T(8,128)(2,1)S(1)}, bf16[192,512]{1,0:T(8,128)(2,1)}, u32[]{:S(2)}) %copy-start.4) | copy-done | bytes 196632
  61.6 0.9 %copy-done.6 = bf16[192,512]{1,0:T(8,128)(2,1)S(1)} copy-done((bf16[192,512]{1,0:T(8,128)(2,1)S(1)}, bf16[192,512]{1,0:T(8,128)(2,1)}, u32[]{:S(2)}) %copy-start.6) | copy-done | bytes 196632
  62.5 0.9 %copy-done.8 = bf16[192,512]{1,0:T(8,128)(2,1)S(1)} copy-done((bf16[192,512]{1,0:T(8,128)(2,1)S(1)}, bf16[192,512]{1,0:T(8,128)(2,1)}, u32[]{:S(2)}) %copy-start.8) | copy-done | bytes 196632
  63.5 0.9 %copy-done.10 = bf16[192,512]{1,0:T(8,128)(2,1)S(1)} copy-done((bf16[192,512]{1,0:T(8,128)(2,1)S(1)}, bf16[192,512]{1,0:T(8,128)(2,1)}, u32[]{:S(2)}) %copy-start.10) | copy-done | bytes 196632
  64.4 0.9 %copy-done.12 = bf16[192,512]{1,0:T(8,128)(2,1)S(1)} copy-done((bf16[192,512]{1,0:T(8,128)(2,1)S(1)}, bf16[192,512]{1,0:T(8,128)(2,1)}, u32[]{:S(2)}) %copy-start.12) | copy-done | bytes 196632
  65.3 0.9 %copy-done.14 = bf16[192,512]{1,0:T(8,128)(2,1)S(1)} copy-done((bf16[192,512]{1,0:T(8,128)(2,1)S(1)}, bf16[192,512]{1,0:T(8,128)(2,1)}, u32[]{:S(2)}) %copy-start.14) | copy-done | bytes 196632
  66.3 0.9 %copy-done.16 = bf16[192,512]{1,0:T(8,128)(2,1)S(1)} copy-done((bf16[192,512]{1,0:T(8,128)(2,1)S(1)}, bf16[192,512]{1,0:T(8,128)(2,1)}, u32[]{:S(2)}) %copy-start.16) | copy-done | bytes 196632
  67.2 0.9 %copy-done.18 = bf16[192,512]{1,0:T(8,128)(2,1)S(1)} copy-done((bf16[192,512]{1,0:T(8,128)(2,1)S(1)}, bf16[192,512]{1,0:T(8,128)(2,1)}, u32[]{:S(2)}) %copy-start.18) | copy-done | bytes 196632
  68.1 0.9 %copy-done.20 = bf16[192,512]{1,0:T(8,128)(2,1)S(1)} copy-done((bf16[192,512]{1,0:T(8,128)(2,1)S(1)}, bf16[192,512]{1,0:T(8,128)(2,1)}, u32[]{:S(2)}) %copy-start.20) | copy-done | bytes 196632
  69.0 0.9 %copy-done.22 = bf16[192,512]{1,0:T(8,128)(2,1)S(1)} copy-done((bf16[192,512]{1,0:T(8,128)(2,1)S(1)}, bf16[192,512]{1,0:T(8,128)(2,1)}, u32[]{:S(2)}) %copy-start.22) | copy-done | bytes 196632
  70.0 0.9 %copy-done.24 = bf16[192,512]{1,0:T(8,128)(2,1)S(1)} copy-done((bf16[192,512]{1,0:T(8,128)(2,1)S(1)}, bf16[192,512]{1,0:T(8,128)(2,1)}, u32[]{:S(2)}) %copy-start.24) | copy-done | bytes 196632
  70.9 0.9 %copy-done.26 = bf16[192,512]{1,0:T(8,128)(2,1)S(1)} copy-done((bf16[192,512]{1,0:T(8,128)(2,1)S(1)}, bf16[192,512]{1,0:T(8,128)(2,1)}, u32[]{:S(2)}) %copy-start.26) | copy-done | bytes 196632
  71.8 0.7 copy-done.27
  72.5 7.4 %attend.1 = (bf16[192,512]{1,0:T(8,128)(2,1)}, bf16[192,512]{1,0:T(8,128)(2,1)S(1)}) custom-call(s32[18]{0:T(128)S(1)} %stack.100.meta, s32[32]{0:T(128)S(1)} %copy-done.27, bf16[192,512]{1,0:T(8,128)(2,1)S(1)} %copy-done.1, bf16[192,512]{1,0:T(8,128)(2,1)S(1)} %copy-done.2, bf16[192,512]{1,0:T(8,128)(2,1)S(1)} %constant_dynamic-update-slice_fusion.refs_0_, ...), custom_call_target="tpu_custom_call" | custom-call | flops 1811939328 | bytes 3145728 | tf_op jit(solution)/shard_map/attend/pallas_call | solution.py:120
  79.9 1.5 %collective-permute-start.15 = (bf16[192,512]{1,0:T(8,128)(2,1)}, bf16[192,512]{1,0:T(8,128)(2,1)S(1)}, u32[]{:S(2)}, u32[]{:S(2)}) collective-permute-start(bf16[192,512]{1,0:T(8,128)(2,1)} %get-tuple-element.4), channel_id=1, source_target_pairs={{0,1},{1,0},{2,3},{3,2},{4,5},{5,4},{6,7},{7,6},{8,9},{9,8},{10,11... | collective-permute-start | bytes 589832 | tf_op jit(solution)/shard_map/ppermute | solution.py:229
  81.4 0.1 stack.82.starts
  81.5 2.2 %copy-done = bf16[512,4096]{1,0:T(8,128)(2,1)S(1)} copy-done((bf16[512,4096]{1,0:T(8,128)(2,1)S(1)}, bf16[512,4096]{1,0:T(8,128)(2,1)}, u32[]{:S(2)}) %copy-start) | copy-done | bytes 4194328
  83.7 2.6 %project_own.1.partial = bf16[192,4096]{1,0:T(8,128)(2,1)S(1)} custom-call(bf16[192,512]{1,0:T(8,128)(2,1)S(1)} %get-tuple-element.5.left, bf16[512,4096]{1,0:T(8,128)(2,1)S(1)} %copy-done), custom_call_target="tpu_custom_call" | custom-call | flops 805306368 | bytes 4194304 | tf_op jit(solution)/shard_map/project_own/pallas_call | solution.py:148
  86.3 0.8 collective-permute-done.15.left
  87.1 3.3 %project_other.1 = (bf16[96,4096]{1,0:T(8,128)(2,1)}, bf16[96,4096]{1,0:T(8,128)(2,1)}) custom-call(s32[6]{0:T(128)S(1)} %stack.82.starts, bf16[192,512]{1,0:T(8,128)(2,1)S(1)} %collective-permute-done.15.left, bf16[192,4096]{1,0:T(8,128)(2,1)S(1)} %project_own.1.partial, bf16[512,1024]{1,0:T(8,128)(2,1)S(1)} %collective-permute-done.16.refs_0_, ...), custom_call_target="tpu_custom_call" | custom-call | flops 805306368 | bytes 4194304 | tf_op jit(solution)/shard_map/project_other/pallas_call | solution.py:183
  (47 shorter events, 0.1 us)
Async XLA Ops:
  1.9 39.2 %collective-permute-start.16 = (bf16[512,1024]{1,0:T(8,128)(2,1)S(1)}, bf16[512,1024]{1,0:T(8,128)(2,1)S(1)}, u32[]{:S(2)}, u32[]{:S(2)}) collective-permute-start(bf16[512,1024]{1,0:T(8,128)(2,1)S(1)} %constant_dynamic-slice_fusion.1), channel_id=1, source_target_pairs={{0,1},{1,0},{2,3},{3,2},{4,5},{5,4},{6,7},{7,6},{8,9},{9,8},{10,11... | collective-permute-start | bytes 3145736 | tf_op jit(solution)/shard_map/ppermute | solution.py:229
  6.0 33.3 %collective-permute-start.18 = (bf16[512,512]{1,0:T(8,128)(2,1)S(1)}, bf16[512,512]{1,0:T(8,128)(2,1)S(1)}, u32[]{:S(2)}, u32[]{:S(2)}) collective-permute-start(bf16[512,512]{1,0:T(8,128)(2,1)S(1)} %constant_dynamic-slice_fusion), channel_id=1, source_target_pairs={{0,1},{1,0},{2,3},{3,2},{4,5},{5,4},{6,7},{7,6},{8,9},{9,8},{10,11... | collective-permute-start | bytes 1572872 | tf_op jit(solution)/shard_map/ppermute | solution.py:229
  9.4 5.7 %collective-permute-start.7 = (bf16[192,512]{1,0:T(8,128)(2,1)S(1)}, bf16[192,512]{1,0:T(8,128)(2,1)S(1)}, u32[]{:S(2)}, u32[]{:S(2)}) collective-permute-start(bf16[192,512]{1,0:T(8,128)(2,1)S(1)} %constant_dynamic-update-slice_fusion.refs_0_), channel_id=1, source_target_pairs={{0,2},{2,0},{4,6},{6,4},{8,10},{10,8},{12,14},{14,12},{16,18},{18,... | collective-permute-start | bytes 589832 | tf_op jit(solution)/shard_map/ppermute | solution.py:226
  9.5 7.5 %collective-permute-start.3 = (bf16[192,512]{1,0:T(8,128)(2,1)S(1)}, bf16[192,512]{1,0:T(8,128)(2,1)S(1)}, u32[]{:S(2)}, u32[]{:S(2)}) collective-permute-start(bf16[192,512]{1,0:T(8,128)(2,1)S(1)} %constant_dynamic-update-slice_fusion.refs_0_), channel_id=1, source_target_pairs={{0,4},{2,6},{4,0},{6,2},{8,12},{10,14},{12,8},{14,10},{16,20},{18,... | collective-permute-start | bytes 589832 | tf_op jit(solution)/shard_map/ppermute | solution.py:226
  11.5 9.6 %collective-permute-start.2 = (bf16[192,512]{1,0:T(8,128)(2,1)S(1)}, bf16[192,512]{1,0:T(8,128)(2,1)S(1)}, u32[]{:S(2)}, u32[]{:S(2)}) collective-permute-start(bf16[192,512]{1,0:T(8,128)(2,1)S(1)} %constant_dynamic-update-slice_fusion.refs_0_), channel_id=1, source_target_pairs={{0,24},{2,26},{4,28},{6,30},{8,16},{10,18},{12,20},{14,22},{16,8},... | collective-permute-start | bytes 589832 | tf_op jit(solution)/shard_map/ppermute | solution.py:226
  15.1 0.7 copy-start.3
  15.8 16.3 %collective-permute-start.1 = (bf16[192,512]{1,0:T(8,128)(2,1)S(1)}, bf16[192,512]{1,0:T(8,128)(2,1)S(1)}, u32[]{:S(2)}, u32[]{:S(2)}) collective-permute-start(bf16[192,512]{1,0:T(8,128)(2,1)S(1)} %constant_dynamic-update-slice_fusion.refs_0_), channel_id=1, source_target_pairs={{0,16},{2,18},{4,20},{6,22},{8,24},{10,26},{12,28},{14,30},{16,0},... | collective-permute-start | bytes 589832 | tf_op jit(solution)/shard_map/ppermute | solution.py:226
  17.0 24.2 %collective-permute-start = (bf16[192,512]{1,0:T(8,128)(2,1)S(1)}, bf16[192,512]{1,0:T(8,128)(2,1)S(1)}, u32[]{:S(2)}, u32[]{:S(2)}) collective-permute-start(bf16[192,512]{1,0:T(8,128)(2,1)S(1)} %constant_dynamic-update-slice_fusion.refs_0_), channel_id=1, source_target_pairs={{0,8},{2,10},{4,12},{6,14},{8,0},{10,2},{12,4},{14,6},{16,24},{18,... | collective-permute-start | bytes 589832 | tf_op jit(solution)/shard_map/ppermute | solution.py:226
  21.2 22.3 %collective-permute-start.11 = (bf16[192,512]{1,0:T(8,128)(2,1)S(1)}, bf16[192,512]{1,0:T(8,128)(2,1)S(1)}, u32[]{:S(2)}, u32[]{:S(2)}) collective-permute-start(bf16[192,512]{1,0:T(8,128)(2,1)S(1)} %collective-permute-done.3.refs_4_), channel_id=1, source_target_pairs={{0,2},{2,0},{4,6},{6,4},{8,10},{10,8},{12,14},{14,12},{16,18},{18,... | collective-permute-start | bytes 589832 | tf_op jit(solution)/shard_map/ppermute | solution.py:226
  21.2 0.7 copy-start.5
  32.1 12.1 %collective-permute-start.10 = (bf16[192,512]{1,0:T(8,128)(2,1)S(1)}, bf16[192,512]{1,0:T(8,128)(2,1)S(1)}, u32[]{:S(2)}, u32[]{:S(2)}) collective-permute-start(bf16[192,512]{1,0:T(8,128)(2,1)S(1)} %collective-permute-done.2.refs_3_), channel_id=1, source_target_pairs={{0,2},{2,0},{4,6},{6,4},{8,10},{10,8},{12,14},{14,12},{16,18},{18,... | collective-permute-start | bytes 589832 | tf_op jit(solution)/shard_map/ppermute | solution.py:226
  39.4 18.9 %collective-permute-start.19 = (bf16[512,512]{1,0:T(8,128)(2,1)S(1)}, bf16[512,512]{1,0:T(8,128)(2,1)S(1)}, u32[]{:S(2)}, u32[]{:S(2)}) collective-permute-start(bf16[512,512]{1,0:T(8,128)(2,1)S(1)} %collective-permute-done.18.refs_2_), channel_id=1, source_target_pairs={{0,8},{2,10},{4,12},{6,14},{8,0},{10,2},{12,4},{14,6},{16,24},{18,... | collective-permute-start | bytes 1572872 | tf_op jit(solution)/shard_map/ppermute | solution.py:226
  41.2 45.9 %collective-permute-start.17 = (bf16[512,1024]{1,0:T(8,128)(2,1)S(1)}, bf16[512,1024]{1,0:T(8,128)(2,1)S(1)}, u32[]{:S(2)}, u32[]{:S(2)}) collective-permute-start(bf16[512,1024]{1,0:T(8,128)(2,1)S(1)} %collective-permute-done.16.refs_0_), channel_id=1, source_target_pairs={{0,2},{2,0},{4,6},{6,4},{8,10},{10,8},{12,14},{14,12},{16,18},{18,... | collective-permute-start | bytes 3145736 | tf_op jit(solution)/shard_map/ppermute | solution.py:226
  41.2 7.8 %collective-permute-start.6 = (bf16[192,512]{1,0:T(8,128)(2,1)S(1)}, bf16[192,512]{1,0:T(8,128)(2,1)S(1)}, u32[]{:S(2)}, u32[]{:S(2)}) collective-permute-start(bf16[192,512]{1,0:T(8,128)(2,1)S(1)} %collective-permute-done.2.refs_3_), channel_id=1, source_target_pairs={{0,4},{2,6},{4,0},{6,2},{8,12},{10,14},{12,8},{14,10},{16,20},{18,... | collective-permute-start | bytes 589832 | tf_op jit(solution)/shard_map/ppermute | solution.py:226
  42.7 0.7 copy-start.7
  43.4 0.7 copy-start.13
  44.1 4.8 %collective-permute-start.9 = (bf16[192,512]{1,0:T(8,128)(2,1)S(1)}, bf16[192,512]{1,0:T(8,128)(2,1)S(1)}, u32[]{:S(2)}, u32[]{:S(2)}) collective-permute-start(bf16[192,512]{1,0:T(8,128)(2,1)S(1)} %collective-permute-done.1.refs_2_), channel_id=1, source_target_pairs={{0,2},{2,0},{4,6},{6,4},{8,10},{10,8},{12,14},{14,12},{16,18},{18,... | collective-permute-start | bytes 589832 | tf_op jit(solution)/shard_map/ppermute | solution.py:226
  44.3 0.7 copy-start.15
  45.0 7.7 %collective-permute-start.5 = (bf16[192,512]{1,0:T(8,128)(2,1)S(1)}, bf16[192,512]{1,0:T(8,128)(2,1)S(1)}, u32[]{:S(2)}, u32[]{:S(2)}) collective-permute-start(bf16[192,512]{1,0:T(8,128)(2,1)S(1)} %collective-permute-done.1.refs_2_), channel_id=1, source_target_pairs={{0,4},{2,6},{4,0},{6,2},{8,12},{10,14},{12,8},{14,10},{16,20},{18,... | collective-permute-start | bytes 589832 | tf_op jit(solution)/shard_map/ppermute | solution.py:226
  45.5 0.7 copy-start.9
  48.9 4.4 %collective-permute-start.8 = (bf16[192,512]{1,0:T(8,128)(2,1)S(1)}, bf16[192,512]{1,0:T(8,128)(2,1)S(1)}, u32[]{:S(2)}, u32[]{:S(2)}) collective-permute-start(bf16[192,512]{1,0:T(8,128)(2,1)S(1)} %collective-permute-done.refs_1_), channel_id=1, source_target_pairs={{0,2},{2,0},{4,6},{6,4},{8,10},{10,8},{12,14},{14,12},{16,18},{18,... | collective-permute-start | bytes 589832 | tf_op jit(solution)/shard_map/ppermute | solution.py:226
  49.0 0.7 copy-start.19
  49.6 7.4 %collective-permute-start.4 = (bf16[192,512]{1,0:T(8,128)(2,1)S(1)}, bf16[192,512]{1,0:T(8,128)(2,1)}, u32[]{:S(2)}, u32[]{:S(2)}) collective-permute-start(bf16[192,512]{1,0:T(8,128)(2,1)S(1)} %collective-permute-done.refs_1_), channel_id=1, source_target_pairs={{0,4},{2,6},{4,0},{6,2},{8,12},{10,14},{12,8},{14,10},{16,20},{18,... | collective-permute-start | bytes 589832 | tf_op jit(solution)/shard_map/ppermute | solution.py:226
  51.1 0.7 copy-start.11
  52.7 4.4 %collective-permute-start.14 = (bf16[192,512]{1,0:T(8,128)(2,1)S(1)}, bf16[192,512]{1,0:T(8,128)(2,1)S(1)}, u32[]{:S(2)}, u32[]{:S(2)}) collective-permute-start(bf16[192,512]{1,0:T(8,128)(2,1)S(1)} %collective-permute-done.6.refs_7_), channel_id=1, source_target_pairs={{0,2},{2,0},{4,6},{6,4},{8,10},{10,8},{12,14},{14,12},{16,18},{18,... | collective-permute-start | bytes 589832 | tf_op jit(solution)/shard_map/ppermute | solution.py:226
  52.7 0.7 copy-start.17
  53.4 0.7 copy-start.23
  54.0 4.3 %collective-permute-start.13 = (bf16[192,512]{1,0:T(8,128)(2,1)S(1)}, bf16[192,512]{1,0:T(8,128)(2,1)}, u32[]{:S(2)}, u32[]{:S(2)}) collective-permute-start(bf16[192,512]{1,0:T(8,128)(2,1)S(1)} %collective-permute-done.5.refs_6_), channel_id=1, source_target_pairs={{0,2},{2,0},{4,6},{6,4},{8,10},{10,8},{12,14},{14,12},{16,18},{18,... | collective-permute-start | bytes 589832 | tf_op jit(solution)/shard_map/ppermute | solution.py:226
  54.6 0.7 copy-start.21
  57.1 1.8 %collective-permute-start.12 = (bf16[192,512]{1,0:T(8,128)(2,1)}, bf16[192,512]{1,0:T(8,128)(2,1)}, u32[]{:S(2)}, u32[]{:S(2)}) collective-permute-start(bf16[192,512]{1,0:T(8,128)(2,1)} %collective-permute-done.4.refs_5_), channel_id=1, source_target_pairs={{0,2},{2,0},{4,6},{6,4},{8,10},{10,8},{12,14},{14,12},{16,18},{18,... | collective-permute-start | bytes 589832 | tf_op jit(solution)/shard_map/ppermute | solution.py:226
  57.1 0.7 copy-start.25
  57.7 29.3 %collective-permute-start.20 = (bf16[512,512]{1,0:T(8,128)(2,1)S(1)}, bf16[512,512]{1,0:T(8,128)(2,1)}, u32[]{:S(2)}, u32[]{:S(2)}) collective-permute-start(bf16[512,512]{1,0:T(8,128)(2,1)S(1)} %collective-permute-done.18.refs_2_), channel_id=1, source_target_pairs={{0,2},{2,0},{4,6},{6,4},{8,10},{10,8},{12,14},{14,12},{16,18},{18,... | collective-permute-start | bytes 1572872 | tf_op jit(solution)/shard_map/ppermute | solution.py:226
  58.2 28.8 %collective-permute-start.21 = (bf16[512,512]{1,0:T(8,128)(2,1)S(1)}, bf16[512,512]{1,0:T(8,128)(2,1)}, u32[]{:S(2)}, u32[]{:S(2)}) collective-permute-start(bf16[512,512]{1,0:T(8,128)(2,1)S(1)} %collective-permute-done.19.refs_3_), channel_id=1, source_target_pairs={{0,2},{2,0},{4,6},{6,4},{8,10},{10,8},{12,14},{14,12},{16,18},{18,... | collective-permute-start | bytes 1572872 | tf_op jit(solution)/shard_map/ppermute | solution.py:226
  58.8 0.9 %copy-start.1 = (bf16[192,512]{1,0:T(8,128)(2,1)S(1)}, bf16[192,512]{1,0:T(8,128)(2,1)}, u32[]{:S(2)}) copy-start(bf16[192,512]{1,0:T(8,128)(2,1)} %query.1) | copy-start | bytes 589828
  59.8 0.9 %copy-start.2 = (bf16[192,512]{1,0:T(8,128)(2,1)S(1)}, bf16[192,512]{1,0:T(8,128)(2,1)}, u32[]{:S(2)}) copy-start(bf16[192,512]{1,0:T(8,128)(2,1)} %tangent_query.1) | copy-start | bytes 589828
  60.7 0.9 %copy-start.4 = (bf16[192,512]{1,0:T(8,128)(2,1)S(1)}, bf16[192,512]{1,0:T(8,128)(2,1)}, u32[]{:S(2)}) copy-start(bf16[192,512]{1,0:T(8,128)(2,1)} %copy-done.3) | copy-start | bytes 589828
  61.6 0.9 %copy-start.6 = (bf16[192,512]{1,0:T(8,128)(2,1)S(1)}, bf16[192,512]{1,0:T(8,128)(2,1)}, u32[]{:S(2)}) copy-start(bf16[192,512]{1,0:T(8,128)(2,1)} %copy-done.5) | copy-start | bytes 589828
  62.5 0.9 %copy-start.8 = (bf16[192,512]{1,0:T(8,128)(2,1)S(1)}, bf16[192,512]{1,0:T(8,128)(2,1)}, u32[]{:S(2)}) copy-start(bf16[192,512]{1,0:T(8,128)(2,1)} %copy-done.7) | copy-start | bytes 589828
  63.5 0.9 %copy-start.10 = (bf16[192,512]{1,0:T(8,128)(2,1)S(1)}, bf16[192,512]{1,0:T(8,128)(2,1)}, u32[]{:S(2)}) copy-start(bf16[192,512]{1,0:T(8,128)(2,1)} %copy-done.9) | copy-start | bytes 589828
  64.4 0.9 %copy-start.12 = (bf16[192,512]{1,0:T(8,128)(2,1)S(1)}, bf16[192,512]{1,0:T(8,128)(2,1)}, u32[]{:S(2)}) copy-start(bf16[192,512]{1,0:T(8,128)(2,1)} %copy-done.11) | copy-start | bytes 589828
  65.3 0.9 %copy-start.14 = (bf16[192,512]{1,0:T(8,128)(2,1)S(1)}, bf16[192,512]{1,0:T(8,128)(2,1)}, u32[]{:S(2)}) copy-start(bf16[192,512]{1,0:T(8,128)(2,1)} %copy-done.13) | copy-start | bytes 589828
  66.3 0.9 %copy-start.16 = (bf16[192,512]{1,0:T(8,128)(2,1)S(1)}, bf16[192,512]{1,0:T(8,128)(2,1)}, u32[]{:S(2)}) copy-start(bf16[192,512]{1,0:T(8,128)(2,1)} %copy-done.15) | copy-start | bytes 589828
  67.2 0.9 %copy-start.18 = (bf16[192,512]{1,0:T(8,128)(2,1)S(1)}, bf16[192,512]{1,0:T(8,128)(2,1)}, u32[]{:S(2)}) copy-start(bf16[192,512]{1,0:T(8,128)(2,1)} %copy-done.17) | copy-start | bytes 589828
  68.1 0.9 %copy-start.20 = (bf16[192,512]{1,0:T(8,128)(2,1)S(1)}, bf16[192,512]{1,0:T(8,128)(2,1)}, u32[]{:S(2)}) copy-start(bf16[192,512]{1,0:T(8,128)(2,1)} %copy-done.19) | copy-start | bytes 589828
  69.0 0.9 %copy-start.22 = (bf16[192,512]{1,0:T(8,128)(2,1)S(1)}, bf16[192,512]{1,0:T(8,128)(2,1)}, u32[]{:S(2)}) copy-start(bf16[192,512]{1,0:T(8,128)(2,1)} %copy-done.21) | copy-start | bytes 589828
  70.0 0.9 %copy-start.24 = (bf16[192,512]{1,0:T(8,128)(2,1)S(1)}, bf16[192,512]{1,0:T(8,128)(2,1)}, u32[]{:S(2)}) copy-start(bf16[192,512]{1,0:T(8,128)(2,1)} %copy-done.23) | copy-start | bytes 589828
  70.9 0.9 %copy-start.26 = (bf16[192,512]{1,0:T(8,128)(2,1)S(1)}, bf16[192,512]{1,0:T(8,128)(2,1)}, u32[]{:S(2)}) copy-start(bf16[192,512]{1,0:T(8,128)(2,1)} %copy-done.25) | copy-start | bytes 589828
  71.8 0.7 copy-start.27
  79.9 7.2 %collective-permute-start.15 = (bf16[192,512]{1,0:T(8,128)(2,1)}, bf16[192,512]{1,0:T(8,128)(2,1)S(1)}, u32[]{:S(2)}, u32[]{:S(2)}) collective-permute-start(bf16[192,512]{1,0:T(8,128)(2,1)} %get-tuple-element.4), channel_id=1, source_target_pairs={{0,1},{1,0},{2,3},{3,2},{4,5},{5,4},{6,7},{7,6},{8,9},{9,8},{10,11... | collective-permute-start | bytes 589832 | tf_op jit(solution)/shard_map/ppermute | solution.py:229
  81.5 2.2 %copy-start = (bf16[512,4096]{1,0:T(8,128)(2,1)S(1)}, bf16[512,4096]{1,0:T(8,128)(2,1)}, u32[]{:S(2)}) copy-start(bf16[512,4096]{1,0:T(8,128)(2,1)} %weight.1) | copy-start | bytes 12582916

commit v2 on v1

v2 whole, which is shorter than its diff:
```python
import functools

import jax
import jax.numpy as jnp
from jax import lax
from jax.experimental import pallas as pl
from jax.experimental.pallas import tpu as pltpu
from jax.sharding import PartitionSpec as P

HD = 128
LOG2E = 1.4426950408889634
LOWEST = -1e30
VMEM = pl.BlockSpec(memory_space=pltpu.VMEM)
SMEM = pl.BlockSpec(memory_space=pltpu.SMEM)
ANY = pl.BlockSpec(memory_space=pl.ANY)
HBM = pl.BlockSpec(memory_space=pltpu.HBM)


def in_hbm(arrays):
    return [pltpu.with_memory_space_constraint(array, pltpu.HBM) for array in arrays]


def lanes(column, width):
    return jnp.broadcast_to(column, (column.shape[0], width))


SMALL = pl.CostEstimate(flops=1, bytes_accessed=1, transcendentals=0)
NT = (((1,), (1,)), ((), ()))


def attend_kernel(sizes, meta, query, tangent_query, *refs):
    packs, carried, last, held, run, group, chunk = sizes
    height = group * run
    pack_refs, refs = refs[:packs], refs[packs:]
    before, refs = refs[: 5 * carried], refs[5 * carried :]
    outs, refs = (refs[:2], refs[2:]) if last else (refs[:5], refs[5:])
    line, top, total, shift, both, mixed, sems = refs
    state = (top, total, shift, both, mixed)
    scale = HD ** (-0.5)

    copies = []
    blocks = [(ref, begin) for ref in pack_refs for begin in range(0, ref.shape[0], run)]
    for n, (ref, begin) in enumerate(blocks):
        rows = pl.ds(pl.multiple_of(meta[4 + n] * run, run), run)
        block = ref.at[begin : begin + run, :]
        if held:
            line[rows, :] = block[...]
        else:
            copies.append(pltpu.make_async_copy(block, line.at[rows, :], sems.at[n]))
            copies[-1].start()
    for copy in copies:
        copy.wait()

    own = meta[1]
    for step in range(2):
        half = meta[0] if step == 0 else 1 - meta[0]
        ahead = meta[2 + half]
        mine = slice(step * height, (step + 1) * height)
        rows = pl.ds(pl.multiple_of(half * run, run), run)
        q = [query[rows, h * HD : (h + 1) * HD] for h in range(group)]
        tq = [tangent_query[rows, h * HD : (h + 1) * HD] for h in range(group)]
        q = jnp.concatenate(q, axis=0)
        tq_q = jnp.concatenate([jnp.concatenate(tq, axis=0), q], axis=1)
        if carried:
            for now, then in zip(state, before):
                now[...] = then[mine, :]
        else:
            top[...] = jnp.full(top.shape, LOWEST, jnp.float32)
            for now in state[1:]:
                now[...] = jnp.zeros(now.shape, jnp.float32)

        def visit(index, masked):
            cols = pl.ds(pl.multiple_of(index * chunk, chunk), chunk)
            keys = line[cols, 0:HD]
            keys_both = line[cols, 0 : 2 * HD]
            values = line[cols, 2 * HD : 3 * HD]
            values_both = line[cols, 2 * HD : 4 * HD]
            scores = lax.dot_general(q, keys, NT, preferred_element_type=jnp.float32)
            scores = scores * (scale * LOG2E)
            if masked:
                col = index * chunk + lax.broadcasted_iota(jnp.int32, (height, chunk), 1)
                row = lax.rem(lax.broadcasted_iota(jnp.int32, (height, chunk), 0), run)
                scores = jnp.where(col < ahead * run + (row + 1) * own, scores, LOWEST)
            old = top[...]
            new = jnp.maximum(old, lanes(jnp.max(scores, axis=1, keepdims=True), HD))
            factor = jnp.exp2(old - new)
            top[...] = new
            weights = jnp.exp2(scores - jnp.tile(new, (1, chunk // HD)))
            slopes = lax.dot_general(tq_q, keys_both, NT, preferred_element_type=jnp.float32)
            product = weights * slopes
            weights_b = weights.astype(jnp.bfloat16)
            product_b = product.astype(jnp.bfloat16)
            part = weights[:, 0:HD]
            part_shift = product[:, 0:HD]
            for k in range(1, chunk // HD):
                part = part + weights[:, k * HD : (k + 1) * HD]
                part_shift = part_shift + product[:, k * HD : (k + 1) * HD]
            total[...] = total[...] * factor + part
            shift[...] = shift[...] * factor + part_shift
            both[...] = both[...] * jnp.tile(factor, (1, 2)) + jnp.dot(
                weights_b, values_both, preferred_element_type=jnp.float32
            )
            mixed[...] = mixed[...] * factor + jnp.dot(
                product_b, values, preferred_element_type=jnp.float32
            )

        whole = ahead * run // chunk

        @pl.loop(0, whole)
        def _(index):
            visit(index, False)

        @pl.when((ahead + own) * run > whole * chunk)
        def _():
            visit(whole, True)

        if not last:
            for now, out in zip(state, outs):
                out[mine, :] = now[...]
            continue
        inverse = lanes(1.0 / jnp.sum(total[...], axis=1, keepdims=True), HD)
        shifted = lanes(jnp.sum(shift[...], axis=1, keepdims=True), HD) * (scale * inverse)
        context = both[:, 0:HD] * inverse
        tangent = (mixed[...] * scale + both[:, HD : 2 * HD]) * inverse - shifted * context
        out = outs[step]
        for h in range(group):
            cols = slice(h * HD, (h + 1) * HD)
            head = slice(h * run, (h + 1) * run)
            out[0:run, cols] = context[head].astype(out.dtype)
            out[run : 2 * run, cols] = tangent[head].astype(out.dtype)


def ranks(order, first, me, sources, own):
    place = order.reshape(-1, 2)[sources].reshape(-1)
    rank = jnp.sum(place[None, :] < place[:, None], axis=1, dtype=jnp.int32)
    ours = lax.dynamic_slice_in_dim(order, 2 * me, 2)
    ahead = jnp.sum(place[None, :] < ours[:, None], axis=1, dtype=jnp.int32)
    return jnp.concatenate([jnp.stack([first, jnp.int32(own)]), ahead, rank])


def attend(meta, query, tangent_query, packs, before=(), last=True, held=False):
    rows, width = query.shape
    run, group = rows // 2, width // HD
    count = sum(pack.shape[0] for pack in packs)
    height = group * run
    chunk = 4 * run
    widths = (HD, HD, HD, 2 * HD, HD)
    if last:
        outs = (jax.ShapeDtypeStruct((rows, width), jnp.bfloat16),) * 2
    else:
        outs = tuple(jax.ShapeDtypeStruct((2 * height, w), jnp.float32) for w in widths)
    sizes = (len(packs), len(before) // 5, last, held, run, group, chunk)
    return pl.pallas_call(
        functools.partial(attend_kernel, sizes),
        out_shape=outs,
        in_specs=[SMEM, VMEM, VMEM] + [VMEM if held else ANY] * len(packs) + [VMEM] * len(before),
        out_specs=(VMEM,) * len(outs),
        scratch_shapes=[pltpu.VMEM((count, 4 * HD), jnp.bfloat16)]
        + [pltpu.VMEM((height, w), jnp.float32) for w in widths]
        + [pltpu.SemaphoreType.DMA((count // run,))],
        compiler_params=pltpu.CompilerParams(vmem_limit_bytes=16 * 2**20),
        cost_estimate=SMALL,
        name="attend_last" if last else "attend_early",
    )(meta, query, tangent_query, *(packs if held else in_hbm(packs)), *before)


def project_own_kernel(tile, left, weight, out, held, sems):
    count = weight.shape[1] // tile
    copies = []
    for n in range(count):
        cols = slice(n * tile, (n + 1) * tile)
        copies.append(pltpu.make_async_copy(weight.at[:, cols], held.at[n], sems.at[n]))
        copies[-1].start()
    rows = left[...]
    for n in range(count):
        copies[n].wait()
        out[:, n * tile : (n + 1) * tile] = jnp.dot(
            rows, held[n], preferred_element_type=jnp.float32
        ).astype(out.dtype)


def project_own(left, weight, tile=512):
    rows, depth = left.shape
    width = weight.shape[1]
    return pl.pallas_call(
        functools.partial(project_own_kernel, tile),
        out_shape=jax.ShapeDtypeStruct((rows, width), jnp.bfloat16),
        in_specs=[VMEM, HBM],
        out_specs=VMEM,
        scratch_shapes=[
            pltpu.VMEM((width // tile, depth, tile), jnp.bfloat16),
            pltpu.SemaphoreType.DMA((width // tile,)),
        ],
        compiler_params=pltpu.CompilerParams(vmem_limit_bytes=8 * 2**20),
        cost_estimate=SMALL,
        name="project_own",
    )(left, *in_hbm([weight]))


def project_other_kernel(counts, early, ours, starts, left, partial, *refs):
    pieces, refs = refs[: len(counts)], refs[len(counts) + 2 * ours :]
    outs, held, sums, (sems, out_sems) = refs[:2], refs[2 : 2 + early], refs[2 + early : -2], refs[-2:]
    copies = []
    for n in range(early):
        copies.append(pltpu.make_async_copy(pieces[n], held[n], sems.at[n]))
        copies[-1].start()
    run = left.shape[0] // 2
    rows = left[...]
    stores = []
    for n in list(range(early, len(counts))) + list(range(early)):
        piece = pieces[n]
        if n < early:
            copies[n].wait()
            piece = held[n]
        other = jnp.dot(rows, piece[...], preferred_element_type=jnp.float32)
        other = other.astype(jnp.bfloat16).astype(jnp.float32)
        width = piece.shape[1] // counts[n]
        for m in range(counts[n]):
            cols = pl.ds(pl.multiple_of(starts[sum(counts[:n]) + m], HD), width)
            here = slice(m * width, (m + 1) * width)
            sums[n][:, here] = (partial[:, cols].astype(jnp.float32) + other[:, here]).astype(
                jnp.bfloat16
            )
            for k in range(2):
                stores.append(
                    pltpu.make_async_copy(
                        sums[n].at[k * run : (k + 1) * run, here],
                        outs[k].at[:, cols],
                        out_sems.at[sum(counts[:n]) + m, k],
                    )
                )
                stores[-1].start()
    for store in stores:
        store.wait()


def project_other(starts, left, partial, early, late, outs=()):
    rows = left.shape[0]
    width = partial.shape[1]
    out = jax.ShapeDtypeStruct((rows // 2, width), jnp.bfloat16)
    pieces = early + late
    counts = tuple(len(some) for some in starts)
    starts = jnp.stack([start for some in starts for start in some])
    return pl.pallas_call(
        functools.partial(project_other_kernel, counts, len(early), int(bool(outs))),
        out_shape=(out, out),
        in_specs=[SMEM, VMEM, VMEM] + [ANY] * len(early) + [VMEM] * len(late) + [HBM] * len(outs),
        out_specs=(HBM, HBM),
        input_output_aliases={3 + len(pieces) + n: n for n in range(len(outs))},
        scratch_shapes=[pltpu.VMEM(piece.shape, piece.dtype) for piece in early]
        + [pltpu.VMEM((rows, piece.shape[1]), jnp.bfloat16) for piece in pieces]
        + [pltpu.SemaphoreType.DMA((max(len(early), 1),))]
        + [pltpu.SemaphoreType.DMA((sum(counts), 2))],
        compiler_params=pltpu.CompilerParams(vmem_limit_bytes=16 * 2**20),
        cost_estimate=SMALL,
        name="project_other",
    )(starts, left, partial, *in_hbm(early), *late, *outs)


def whole_program(
    query, key, value, tangent_query, tangent_key, tangent_value, out_weight, block_order, axes
):
    run = query.shape[0] // 2
    pack = jnp.concatenate([key, tangent_key, value, tangent_value], axis=1)
    gathered = lax.all_gather(pack, "ctx", axis=0, tiled=True)
    me = lax.axis_index("ctx").astype(jnp.int32)
    meta = ranks(block_order, jnp.int32(0), me, jnp.arange(axes["ctx"], dtype=jnp.int32), 1)
    first, second = attend(meta, query, tangent_query, [gathered])
    left = jnp.concatenate([first[:run], second[:run], first[run:], second[run:]], axis=0)
    partial = project_own(left, out_weight)
    both = jnp.concatenate([partial[: 2 * run], partial[2 * run :]], axis=1)
    summed = lax.psum_scatter(both, "head", scatter_dimension=0, tiled=True)
    width = out_weight.shape[1]
    return summed[:, :width], summed[:, width:]


def stage_kernel(widths, starts, key, tangent_key, value, tangent_value, weight, pack, *refs):
    parts, sems = refs[:-1], refs[-1]
    moves = []
    for part, some in zip(parts, widths):
        at = 0
        for width in some:
            source = weight.at[:, pl.ds(pl.multiple_of(starts[len(moves)], HD), width)]
            moves.append((source, part.at[:, at : at + width]))
            at += width
    for n, field in enumerate((key, tangent_key, value, tangent_value)):
        moves.append((field, pack.at[:, n * HD : (n + 1) * HD]))
    copies = [pltpu.make_async_copy(*move, sems.at[n]) for n, move in enumerate(moves)]
    for copy in copies:
        copy.start()
    for copy in copies:
        copy.wait()


def stage(starts, fields, weight, widths):
    rows, depth = fields[0].shape[0], weight.shape[0]
    return pl.pallas_call(
        functools.partial(stage_kernel, widths),
        out_shape=[jax.ShapeDtypeStruct((rows, 4 * HD), jnp.bfloat16)]
        + [jax.ShapeDtypeStruct((depth, sum(some)), jnp.bfloat16) for some in widths],
        in_specs=[SMEM] + [HBM] * 5,
        out_specs=[VMEM] * (1 + len(widths)),
        scratch_shapes=[pltpu.SemaphoreType.DMA((4 + sum(len(some) for some in widths),))],
        compiler_params=pltpu.CompilerParams(vmem_limit_bytes=4 * 2**20),
        name="stage",
    )(starts, *in_hbm((*fields, weight)))


def paired_program(
    query, key, value, tangent_query, tangent_key, tangent_value, out_weight, block_order, axes
):
    count = axes["ctx"]
    width = out_weight.shape[1]
    me = lax.axis_index("ctx").astype(jnp.int32)
    side = lax.axis_index("head").astype(jnp.int32)

    def swap(array, bits, *after):
        if after:
            array = lax.optimization_barrier((array,) + after)[0]
        return lax.ppermute(array, "ctx", [(i, i ^ bits) for i in range(count)])

    def cross(array):
        return lax.ppermute(array, "head", [(0, 1), (1, 0)])

    core, column, level = me & 1, (me >> 1) & 1, (me >> 2) & 1
    part = width // 16

    def by_level(level, core):
        return (2 * level + core) * part

    def by_column(column, core):
        return (4 + 2 * column + core) * part

    def by_core(core):
        return (8 + 4 * core) * part

    pack, shared, direct = stage(
        jnp.stack([by_level(level, core), by_column(column, core), by_core(core)]),
        (key, tangent_key, value, tangent_value),
        out_weight,
        ((part, part), (4 * part,)),
    )
    tie = lax.optimization_barrier
    bits = ([0, 1, 2, 4, 8, 3, 5, 9], [6, 12, 10, 7, 13, 11], [14, 15])
    metas = [
        ranks(block_order, 1 - side, me, me ^ jnp.array(some, jnp.int32), int(0 in some))
        for some in bits
    ]

    shared = cross(shared)
    c0, x0, z1, z2 = swap(pack, 1), swap(pack, 2), swap(pack, 4), swap(pack, 8)
    metas, pack, c0, x0, z1, z2, direct = tie((metas, pack, c0, x0, z1, z2, direct))
    direct = cross(direct)
    cx0, cz1, cz2 = swap(x0, 1), swap(z1, 1), swap(z2, 1)
    x1, z3, x2 = swap(z1, 2), swap(z2, 4), swap(z2, 2)
    packs = [pack, c0, x0, z1, z2, cx0, cz1, cz2]
    state = attend(metas[0], query, tangent_query, packs, last=False)
    level_part, column_part = shared[:, :part], shared[:, part:]
    x1, x2, z3, shared, level_part, column_part, state = tie(
        (x1, x2, z3, shared, level_part, column_part, state)
    )
    x3 = swap(z3, 2)
    cx1, cz3, cx2 = swap(x1, 1), swap(z3, 1), swap(x2, 1)
    packs = [x1, z3, x2, cx1, cz3, cx2]
    state = attend(metas[1], query, tangent_query, packs, state, last=False, held=True)
    x3, shared, level_part, column_part, state = tie((x3, shared, level_part, column_part, state))
    level_part, column_part = swap(level_part, 4), swap(column_part, 2)
    cx3, shared_core = tie((swap(x3, 1), swap(shared, 1)))
    theirs, mine = attend(metas[2], query, tangent_query, [x3, cx3], state, held=True)

    other, partial, level_part, column_part, direct = tie(
        (cross(theirs), project_own(mine, out_weight), level_part, column_part, direct)
    )
    far = [swap(p, 1) for p in (direct, level_part, column_part)]
    outs = project_other(
        [
            [by_level(level, core), by_column(column, core)],
            [by_level(1 - level, core)],
            [by_column(1 - column, core)],
            [by_core(core)],
            [by_level(level, 1 - core), by_column(column, 1 - core)],
        ],
        other,
        partial,
        [shared, level_part, column_part, direct],
        [shared_core],
    )
    return project_other(
        [[by_core(1 - core)], [by_level(1 - level, 1 - core)], [by_column(1 - column, 1 - core)]],
        other,
        partial,
        [],
        far,
        outs,
    )


def solution(mesh):
    axes = dict(mesh.shape)
    program = paired_program if axes == {"ctx": 16, "head": 2} else whole_program
    in_specs = (
        P("ctx", "head"),
        P("ctx", "head"),
        P("ctx", "head"),
        P("ctx", "head"),
        P("ctx", "head"),
        P("ctx", "head"),
        P("head", None),
        P(),
    )
    out_specs = (P(("ctx", "head"), None), P(("ctx", "head"), None))
    return jax.shard_map(
        functools.partial(program, axes=axes),
        mesh=mesh,
        in_specs=in_specs,
        out_specs=out_specs,
        check_vma=False,
    )
```

time: 91.3 us -> 58.2 us (0.64)
  local copies, waits for them, and re-layouts: 29.7 us -> 2.26 us
  waiting for transfers between devices: 27.8 us -> 8.03 us
  Pallas kernels: 13.4 us -> 22.6 us
  starting transfers between devices: 18.7 us -> 22.3 us
  other arithmetic: 0 us -> 1.51 us
    unnamed x59 -> x30, local copies, waits for them, and re-layouts: 26.4 us -> 0.07 us
    ppermute x19 -> x21, waiting for transfers between devices: 19.8 us -> 4.32 us  [swap(): return lax.ppermute(array, 'ctx', [(i, i ^ bits) for i in range(count)])]
    pallas_call x3 -> x7, Pallas kernels: 13.4 us -> 22.6 us  [the longest x3 11.3 us: attend(): pl.pallas_call(functools.partial(attend_kernel, sizes), out_shape=outs, i...]
    ppermute x3, waiting for transfers between devices: 7.99 us -> 3.71 us  [cross(): return lax.ppermute(array, 'head', [(0, 1), (1, 0)])]
    ppermute x19 -> x21, starting transfers between devices: 14.1 us -> 17.7 us  [swap(): return lax.ppermute(array, 'ctx', [(i, i ^ bits) for i in range(count)])]
    dynamic_slice x2 -> x1, local copies, waits for them, and re-layouts: 2.37 us -> 0.08 us  [ranks(): ours = lax.dynamic_slice_in_dim(order, 2 * me, 2)]
    gather x0 -> x3, local copies, waits for them, and re-layouts: none -> 1.67 us  [ranks(): place = order.reshape(-1, 2)[sources].reshape(-1)]
    reduce_sum x0 -> x6, other arithmetic: none -> 1.1 us  [the longest x3 0.55 us: ranks(): ahead = jnp.sum(place[None, :] < ours[:, None], axis=1, dtype=jnp.int32)]
  transfers between devices with their start and end apart: 22 -> 24, of which waited for: 9 -> 5; matrix products, arithmetic and copies ran while one was open for 5% -> 6% of each run, Pallas kernels for 11% -> 32%
where the time goes in v2:
time: 58.2 us; the launch traced here: 57.9 us
  Pallas kernels  22.6 us (39%)
  starting transfers between devices  22.3 us (38%)
  waiting for transfers between devices  8.03 us (14%)
  local copies, waits for them, and re-layouts  2.26 us (4%)
  other arithmetic  1.51 us (3%)
  between operations  1.17 us (2%)
    ppermute x21, starting transfers between devices, swap(): return lax.ppermute(array, 'ctx', [(i, i ^ bits) for i in range(count)])  17.7 us
    pallas_call x3, Pallas kernels, attend(): pl.pallas_call(functools.partial(attend_kernel, sizes), out_shape=outs, i...  11.3 us
    pallas_call x2, Pallas kernels, project_other(): pl.pallas_call(functools.partial(project_other_kernel, counts, len(early)...  5.97 us
    ppermute x3, starting transfers between devices, cross(): return lax.ppermute(array, 'head', [(0, 1), (1, 0)])  4.62 us
    ppermute x21, waiting for transfers between devices, swap(): return lax.ppermute(array, 'ctx', [(i, i ^ bits) for i in range(count)])  4.32 us
    ppermute x3, waiting for transfers between devices, cross(): return lax.ppermute(array, 'head', [(0, 1), (1, 0)])  3.71 us
    pallas_call x1, Pallas kernels, project_own(): pl.pallas_call(functools.partial(project_own_kernel, tile), out_shape=jax...  3.27 us
    pallas_call x1, Pallas kernels, stage(): pl.pallas_call(functools.partial(stage_kernel, widths), out_shape=[jax.Sh...  2.01 us
  transfers between devices with their start and end apart: 24, of which 5 were waited for; matrix products, arithmetic and copies ran while one was open for 6% of the time, Pallas kernels for 32%

profile of v2, /device:TPU:0, one launch (start us, length us, event | category | flops | bytes accessed | tf_op | source)
XLA Modules:
  0.0 57.9 jit_solution(511910173855924031)
XLA Ops:
  0.6 0.0 copy-start.14
  0.6 0.0 copy-start.13
  0.7 0.0 copy-start.12
  0.7 0.1 pad_add_fusion.4.starts
  0.8 2.0 %stage.1 = (bf16[192,512]{1,0:T(8,128)(2,1)S(1)}, bf16[512,512]{1,0:T(8,128)(2,1)S(1)}, bf16[512,1024]{1,0:T(8,128)(2,1)S(1)}) custom-call(s32[3]{0:T(128)S(1)} %pad_add_fusion.4.starts, bf16[192,128]{1,0:T(8,128)(2,1)} %key.1, bf16[192,128]{1,0:T(8,128)(2,1)} %tangent_key.1, bf16[192,128]{1,0:T(8,128)(2,1)} %value.1, bf16[192,128]{1,0:T(8,128)(2,1)} %tangent_value.1, ...), custom_call_target="tpu_custom_call" | custom-call | tf_op jit(solution)/shard_map/stage/pallas_call | solution.py:297
  2.8 0.0 copy-start.2
  2.8 4.1 %collective-permute-start.3 = (bf16[192,512]{1,0:T(8,128)(2,1)S(1)}, bf16[192,512]{1,0:T(8,128)(2,1)S(1)}, u32[]{:S(2)}, u32[]{:S(2)}) collective-permute-start(bf16[192,512]{1,0:T(8,128)(2,1)S(1)} %get-tuple-element.62.refs_0_), channel_id=1, source_target_pairs={{0,16},{2,18},{4,20},{6,22},{8,24},{10,26},{12,28},{14,30},{16,0},... | collective-permute-start | bytes 589832 | tf_op jit(solution)/shard_map/ppermute | solution.py:320
  6.9 1.6 %collective-permute-start.2 = (bf16[192,512]{1,0:T(8,128)(2,1)S(1)}, bf16[192,512]{1,0:T(8,128)(2,1)S(1)}, u32[]{:S(2)}, u32[]{:S(2)}) collective-permute-start(bf16[192,512]{1,0:T(8,128)(2,1)S(1)} %get-tuple-element.62.refs_0_), channel_id=1, source_target_pairs={{0,8},{2,10},{4,12},{6,14},{8,0},{10,2},{12,4},{14,6},{16,24},{18,... | collective-permute-start | bytes 589832 | tf_op jit(solution)/shard_map/ppermute | solution.py:320
  8.5 1.5 %collective-permute-start.1 = (bf16[192,512]{1,0:T(8,128)(2,1)S(1)}, bf16[192,512]{1,0:T(8,128)(2,1)S(1)}, u32[]{:S(2)}, u32[]{:S(2)}) collective-permute-start(bf16[192,512]{1,0:T(8,128)(2,1)S(1)} %get-tuple-element.62.refs_0_), channel_id=1, source_target_pairs={{0,4},{2,6},{4,0},{6,2},{8,12},{10,14},{12,8},{14,10},{16,20},{18,... | collective-permute-start | bytes 589832 | tf_op jit(solution)/shard_map/ppermute | solution.py:320
  10.0 1.5 %collective-permute-start.7 = (bf16[512,512]{1,0:T(8,128)(2,1)S(1)}, bf16[512,512]{1,0:T(8,128)(2,1)S(1)}, u32[]{:S(2)}, u32[]{:S(2)}) collective-permute-start(bf16[512,512]{1,0:T(8,128)(2,1)S(1)} %get-tuple-element.60), channel_id=1, source_target_pairs={{0,1},{1,0},{2,3},{3,2},{4,5},{5,4},{6,7},{7,6},{8,9},{9,8},{10,11... | collective-permute-start | bytes 1572872 | tf_op jit(solution)/shard_map/ppermute | solution.py:323
  11.5 0.1 reshape.16
  11.6 0.1 dynamic_slice.2
  11.7 0.0 copy-done.13
  11.7 0.6 gather_fusion.1
  12.3 0.6 gather_fusion
  12.9 0.1 lt.99
  12.9 0.1 lt.108
  13.0 0.2 convert_reduce_fusion
  13.2 0.2 fusion.1
  13.4 0.2 convert_reduce_fusion.1
  13.6 0.2 fusion
  13.8 0.6 gather_fusion.2
  14.3 0.1 lt.116
  14.4 0.2 fusion.2
  14.6 0.2 convert_reduce_fusion.2
  14.8 0.1 pad_add_fusion.2.meta
  14.9 0.1 pad_add_fusion.3.meta
  14.9 0.1 pad_add_fusion.1.meta
  15.0 1.1 %collective-permute-done.3.refs_4_ = bf16[192,512]{1,0:T(8,128)(2,1)S(1)} collective-permute-done((bf16[192,512]{1,0:T(8,128)(2,1)S(1)}, bf16[192,512]{1,0:T(8,128)(2,1)S(1)}, u32[]{:S(2)}, u32[]{:S(2)}) %collective-permute-start.3) | collective-permute-done | bytes 196640 | tf_op jit(solution)/shard_map/ppermute | solution.py:320
  16.2 0.2 collective-permute-done.2.refs_3_
  16.3 0.0 collective-permute-done.1.refs_2_
  16.3 0.0 collective-permute-done.refs_1_
  16.4 0.0 copy-start.7
  16.4 0.1 collective-permute-start.8
  16.4 0.5 collective-permute-start.9
  16.9 0.1 collective-permute-start.10
  17.0 1.5 %collective-permute-start.4 = (bf16[192,512]{1,0:T(8,128)(2,1)S(1)}, bf16[192,512]{1,0:T(8,128)(2,1)S(1)}, u32[]{:S(2)}, u32[]{:S(2)}) collective-permute-start(bf16[192,512]{1,0:T(8,128)(2,1)S(1)} %collective-permute-done.2.refs_3_), channel_id=1, source_target_pairs={{0,4},{2,6},{4,0},{6,2},{8,12},{10,14},{12,8},{14,10},{16,20},{18,... | collective-permute-start | bytes 589832 | tf_op jit(solution)/shard_map/ppermute | solution.py:320
  18.6 0.0 collective-permute-done.8.refs_5_
  18.6 1.4 %collective-permute-start.6 = (bf16[192,512]{1,0:T(8,128)(2,1)S(1)}, bf16[192,512]{1,0:T(8,128)(2,1)S(1)}, u32[]{:S(2)}, u32[]{:S(2)}) collective-permute-start(bf16[192,512]{1,0:T(8,128)(2,1)S(1)} %collective-permute-done.3.refs_4_), channel_id=1, source_target_pairs={{0,8},{2,10},{4,12},{6,14},{8,0},{10,2},{12,4},{14,6},{16,24},{18,... | collective-permute-start | bytes 589832 | tf_op jit(solution)/shard_map/ppermute | solution.py:320
  20.0 0.8 %collective-permute-start.5 = (bf16[192,512]{1,0:T(8,128)(2,1)S(1)}, bf16[192,512]{1,0:T(8,128)(2,1)S(1)}, u32[]{:S(2)}, u32[]{:S(2)}) collective-permute-start(bf16[192,512]{1,0:T(8,128)(2,1)S(1)} %collective-permute-done.3.refs_4_), channel_id=1, source_target_pairs={{0,4},{2,6},{4,0},{6,2},{8,12},{10,14},{12,8},{14,10},{16,20},{18,... | collective-permute-start | bytes 589832 | tf_op jit(solution)/shard_map/ppermute | solution.py:320
  20.9 1.5 %collective-permute-start.20 = (bf16[512,1024]{1,0:T(8,128)(2,1)S(1)}, bf16[512,1024]{1,0:T(8,128)(2,1)}, u32[]{:S(2)}, u32[]{:S(2)}) collective-permute-start(bf16[512,1024]{1,0:T(8,128)(2,1)S(1)} %get-tuple-element.99), channel_id=1, source_target_pairs={{0,1},{1,0},{2,3},{3,2},{4,5},{5,4},{6,7},{7,6},{8,9},{9,8},{10,11... | collective-permute-start | bytes 3145736 | tf_op jit(solution)/shard_map/ppermute | solution.py:323
  22.5 5.7 %attend_early.2 = (f32[768,128]{1,0:T(8,128)S(1)}, f32[768,128]{1,0:T(8,128)S(1)}, f32[768,128]{1,0:T(8,128)S(1)}, f32[768,256]{1,0:T(8,128)S(1)}, f32[768,128]{1,0:T(8,128)S(1)}) custom-call(s32[20]{0:T(128)S(1)} %pad_add_fusion.1.meta, bf16[192,512]{1,0:T(8,128)(2,1)S(1)} %copy-done, bf16[192,512]{1,0:T(8,128)(2,1)S(1)} %copy-done.1, ...), custom_call_target="tpu_custom_call" | custom-call | flops 1 | bytes 1 | tf_op jit(solution)/shard_map/attend_early/pallas_call | solution.py:153
  28.3 0.0 collective-permute-done.6.refs_1_
  28.3 0.2 collective-permute-done.5.refs_2_
  28.5 0.0 collective-permute-start.12
  28.5 0.5 collective-permute-start.14
  29.0 0.0 collective-permute-start.13
  29.0 1.5 %collective-permute-start.11 = (bf16[192,512]{1,0:T(8,128)(2,1)S(1)}, bf16[192,512]{1,0:T(8,128)(2,1)S(1)}, u32[]{:S(2)}, u32[]{:S(2)}) collective-permute-start(bf16[192,512]{1,0:T(8,128)(2,1)S(1)} %collective-permute-done.6.refs_1_), channel_id=1, source_target_pairs={{0,4},{2,6},{4,0},{6,2},{8,12},{10,14},{12,8},{14,10},{16,20},{18,... | collective-permute-start | bytes 589832 | tf_op jit(solution)/shard_map/ppermute | solution.py:320
  30.6 3.0 %attend_early.3 = (f32[768,128]{1,0:T(8,128)S(1)}, f32[768,128]{1,0:T(8,128)S(1)}, f32[768,128]{1,0:T(8,128)S(1)}, f32[768,256]{1,0:T(8,128)S(1)}, f32[768,128]{1,0:T(8,128)S(1)}) custom-call(s32[16]{0:T(128)S(1)} %pad_add_fusion.2.meta, bf16[192,512]{1,0:T(8,128)(2,1)S(1)} %copy-done, bf16[192,512]{1,0:T(8,128)(2,1)S(1)} %copy-done.1, ...), custom_call_target="tpu_custom_call" | custom-call | flops 1 | bytes 1 | tf_op jit(solution)/shard_map/attend_early/pallas_call | solution.py:153
  33.6 2.7 %collective-permute-done.11.refs_0_ = bf16[192,512]{1,0:T(8,128)(2,1)S(1)} collective-permute-done((bf16[192,512]{1,0:T(8,128)(2,1)S(1)}, bf16[192,512]{1,0:T(8,128)(2,1)S(1)}, u32[]{:S(2)}, u32[]{:S(2)}) %collective-permute-start.11) | collective-permute-done | bytes 196640 | tf_op jit(solution)/shard_map/ppermute | solution.py:320
  36.3 0.5 collective-permute-start.15
  36.8 1.5 %collective-permute-start.18 = (bf16[512,256]{1,0:T(8,128)(2,1)S(1)}, bf16[512,256]{1,0:T(8,128)(2,1)}, u32[]{:S(2)}, u32[]{:S(2)}) collective-permute-start(bf16[512,256]{1,0:T(8,128)(2,1)S(1)} %get-tuple-element.97), channel_id=1, source_target_pairs={{0,8},{2,10},{4,12},{6,14},{8,0},{10,2},{12,4},{14,6},{16,24},{18,... | collective-permute-start | bytes 786440 | tf_op jit(solution)/shard_map/ppermute | solution.py:320
  38.3 1.5 %collective-permute-start.19 = (bf16[512,256]{1,0:T(8,128)(2,1)S(1)}, bf16[512,256]{1,0:T(8,128)(2,1)}, u32[]{:S(2)}, u32[]{:S(2)}) collective-permute-start(bf16[512,256]{1,0:T(8,128)(2,1)S(1)} %get-tuple-element.98), channel_id=1, source_target_pairs={{0,4},{2,6},{4,0},{6,2},{8,12},{10,14},{12,8},{14,10},{16,20},{18,... | collective-permute-start | bytes 786440 | tf_op jit(solution)/shard_map/ppermute | solution.py:320
  39.8 0.0 collective-permute-done.15.refs_1_
  39.8 2.6 %attend_last.1 = (bf16[192,512]{1,0:T(8,128)(2,1)S(1)}, bf16[192,512]{1,0:T(8,128)(2,1)S(1)}) custom-call(s32[8]{0:T(128)S(1)} %pad_add_fusion.3.meta, bf16[192,512]{1,0:T(8,128)(2,1)S(1)} %copy-done, bf16[192,512]{1,0:T(8,128)(2,1)S(1)} %copy-done.1, bf16[192,512]{1,0:T(8,128)(2,1)S(1)} %collective-permute-done.11.refs_0_, ...), custom_call_target="tpu_custom_call" | custom-call | flops 1 | bytes 1 | tf_op jit(solution)/shard_map/attend_last/pallas_call | solution.py:153
  42.4 1.6 %collective-permute-start.17 = (bf16[192,512]{1,0:T(8,128)(2,1)S(1)}, bf16[192,512]{1,0:T(8,128)(2,1)S(1)}, u32[]{:S(2)}, u32[]{:S(2)}) collective-permute-start(bf16[192,512]{1,0:T(8,128)(2,1)S(1)} %get-tuple-element.95), channel_id=1, source_target_pairs={{0,1},{1,0},{2,3},{3,2},{4,5},{5,4},{6,7},{7,6},{8,9},{9,8},{10,11... | collective-permute-start | bytes 589832 | tf_op jit(solution)/shard_map/ppermute | solution.py:323
  44.0 3.3 %project_own.1.partial = bf16[192,4096]{1,0:T(8,128)(2,1)S(1)} custom-call(bf16[192,512]{1,0:T(8,128)(2,1)S(1)} %get-tuple-element.96.left, bf16[512,4096]{1,0:T(8,128)(2,1)} %weight.3), custom_call_target="tpu_custom_call" | custom-call | flops 1 | bytes 1 | tf_op jit(solution)/shard_map/project_own/pallas_call | solution.py:185
  47.3 3.7 %collective-permute-done.17.left = bf16[192,512]{1,0:T(8,128)(2,1)S(1)} collective-permute-done((bf16[192,512]{1,0:T(8,128)(2,1)S(1)}, bf16[192,512]{1,0:T(8,128)(2,1)S(1)}, u32[]{:S(2)}, u32[]{:S(2)}) %collective-permute-start.17) | collective-permute-done | bytes 196640 | tf_op jit(solution)/shard_map/ppermute | solution.py:323
  51.0 0.5 collective-permute-start.22
  51.5 0.0 collective-permute-start.23
  51.5 0.1 stack.60.starts
  51.6 0.1 pad_add_fusion.starts
  51.7 3.7 %project_other.2 = (bf16[96,4096]{1,0:T(8,128)(2,1)}, bf16[96,4096]{1,0:T(8,128)(2,1)}) custom-call(s32[7]{0:T(128)S(1)} %stack.60.starts, bf16[192,512]{1,0:T(8,128)(2,1)S(1)} %collective-permute-done.17.left, bf16[192,4096]{1,0:T(8,128)(2,1)S(1)} %project_own.1.partial, bf16[512,512]{1,0:T(8,128)(2,1)} %copy-done.3, ...), custom_call_target="tpu_custom_call" | custom-call | flops 1 | bytes 1 | tf_op jit(solution)/shard_map/project_other/pallas_call | solution.py:244
  55.4 2.3 %project_other.3 = (bf16[96,4096]{1,0:T(8,128)(2,1)}, bf16[96,4096]{1,0:T(8,128)(2,1)}) custom-call(s32[3]{0:T(128)S(1)} %pad_add_fusion.starts, bf16[192,512]{1,0:T(8,128)(2,1)S(1)} %collective-permute-done.17.left, bf16[192,4096]{1,0:T(8,128)(2,1)S(1)} %project_own.1.partial, ...), custom_call_target="tpu_custom_call", output_to_operand_aliasing={{0}: (6, {}), {1}: (7, {})} | custom-call | flops 1 | bytes 1 | tf_op jit(solution)/shard_map/project_other/pallas_call | solution.py:244
  (48 shorter events, 0.2 us)
Async XLA Ops:
  0.6 11.1 %copy-start.14 = (s32[8]{0:T(128)S(1)}, s32[8]{0:T(128)}, u32[]{:S(2)}) copy-start(s32[8]{0:T(128)} %constant.12.clone) | copy-start | bytes 100
  0.6 11.1 %copy-start.13 = (s32[6]{0:T(128)S(1)}, s32[6]{0:T(128)}, u32[]{:S(2)}) copy-start(s32[6]{0:T(128)} %constant.13.clone) | copy-start | bytes 76
  0.7 13.1 %copy-start.12 = (s32[2]{0:T(128)S(1)}, s32[2]{0:T(128)}, u32[]{:S(2)}) copy-start(s32[2]{0:T(128)} %constant.14.clone) | copy-start | bytes 28
  0.7 10.9 %copy-start.11 = (s32[32]{0:T(128)S(1)}, s32[32]{0:T(128)}, u32[]{:S(2)}) copy-start(s32[32]{0:T(128)} %param.18) | copy-start | bytes 388
  0.7 21.8 %copy-start.1 = (bf16[192,512]{1,0:T(8,128)(2,1)S(1)}, bf16[192,512]{1,0:T(8,128)(2,1)}, u32[]{:S(2)}) copy-start(bf16[192,512]{1,0:T(8,128)(2,1)} %tangent_query.5) | copy-start | bytes 589828
  0.7 21.8 %copy-start = (bf16[192,512]{1,0:T(8,128)(2,1)S(1)}, bf16[192,512]{1,0:T(8,128)(2,1)}, u32[]{:S(2)}) copy-start(bf16[192,512]{1,0:T(8,128)(2,1)} %query.5) | copy-start | bytes 589828
  2.8 19.6 %copy-start.2 = (bf16[192,512]{1,0:T(8,128)(2,1)}, bf16[192,512]{1,0:T(8,128)(2,1)S(1)}, u32[]{:S(2)}) copy-start(bf16[192,512]{1,0:T(8,128)(2,1)S(1)} %get-tuple-element.62.refs_0_) | copy-start | bytes 589828
  2.8 13.3 %collective-permute-start.3 = (bf16[192,512]{1,0:T(8,128)(2,1)S(1)}, bf16[192,512]{1,0:T(8,128)(2,1)S(1)}, u32[]{:S(2)}, u32[]{:S(2)}) collective-permute-start(bf16[192,512]{1,0:T(8,128)(2,1)S(1)} %get-tuple-element.62.refs_0_), channel_id=1, source_target_pairs={{0,16},{2,18},{4,20},{6,22},{8,24},{10,26},{12,28},{14,30},{16,0},... | collective-permute-start | bytes 589832 | tf_op jit(solution)/shard_map/ppermute | solution.py:320
  6.9 9.4 %collective-permute-start.2 = (bf16[192,512]{1,0:T(8,128)(2,1)S(1)}, bf16[192,512]{1,0:T(8,128)(2,1)S(1)}, u32[]{:S(2)}, u32[]{:S(2)}) collective-permute-start(bf16[192,512]{1,0:T(8,128)(2,1)S(1)} %get-tuple-element.62.refs_0_), channel_id=1, source_target_pairs={{0,8},{2,10},{4,12},{6,14},{8,0},{10,2},{12,4},{14,6},{16,24},{18,... | collective-permute-start | bytes 589832 | tf_op jit(solution)/shard_map/ppermute | solution.py:320
  8.5 7.8 %collective-permute-start.1 = (bf16[192,512]{1,0:T(8,128)(2,1)S(1)}, bf16[192,512]{1,0:T(8,128)(2,1)S(1)}, u32[]{:S(2)}, u32[]{:S(2)}) collective-permute-start(bf16[192,512]{1,0:T(8,128)(2,1)S(1)} %get-tuple-element.62.refs_0_), channel_id=1, source_target_pairs={{0,4},{2,6},{4,0},{6,2},{8,12},{10,14},{12,8},{14,10},{16,20},{18,... | collective-permute-start | bytes 589832 | tf_op jit(solution)/shard_map/ppermute | solution.py:320
  10.0 6.4 %collective-permute-start = (bf16[192,512]{1,0:T(8,128)(2,1)S(1)}, bf16[192,512]{1,0:T(8,128)(2,1)S(1)}, u32[]{:S(2)}, u32[]{:S(2)}) collective-permute-start(bf16[192,512]{1,0:T(8,128)(2,1)S(1)} %get-tuple-element.62.refs_0_), channel_id=1, source_target_pairs={{0,2},{2,0},{4,6},{6,4},{8,10},{10,8},{12,14},{14,12},{16,18},{18,... | collective-permute-start | bytes 589832 | tf_op jit(solution)/shard_map/ppermute | solution.py:320
  10.0 18.2 %collective-permute-start.7 = (bf16[512,512]{1,0:T(8,128)(2,1)S(1)}, bf16[512,512]{1,0:T(8,128)(2,1)S(1)}, u32[]{:S(2)}, u32[]{:S(2)}) collective-permute-start(bf16[512,512]{1,0:T(8,128)(2,1)S(1)} %get-tuple-element.60), channel_id=1, source_target_pairs={{0,1},{1,0},{2,3},{3,2},{4,5},{5,4},{6,7},{7,6},{8,9},{9,8},{10,11... | collective-permute-start | bytes 1572872 | tf_op jit(solution)/shard_map/ppermute | solution.py:323
  16.1 6.2 %copy-start.4 = (bf16[192,512]{1,0:T(8,128)(2,1)}, bf16[192,512]{1,0:T(8,128)(2,1)S(1)}, u32[]{:S(2)}) copy-start(bf16[192,512]{1,0:T(8,128)(2,1)S(1)} %collective-permute-done.3.refs_4_) | copy-start | bytes 589828
  16.3 6.1 %copy-start.5 = (bf16[192,512]{1,0:T(8,128)(2,1)}, bf16[192,512]{1,0:T(8,128)(2,1)S(1)}, u32[]{:S(2)}) copy-start(bf16[192,512]{1,0:T(8,128)(2,1)S(1)} %collective-permute-done.2.refs_3_) | copy-start | bytes 589828
  16.3 6.0 %copy-start.6 = (bf16[192,512]{1,0:T(8,128)(2,1)}, bf16[192,512]{1,0:T(8,128)(2,1)S(1)}, u32[]{:S(2)}) copy-start(bf16[192,512]{1,0:T(8,128)(2,1)S(1)} %collective-permute-done.1.refs_2_) | copy-start | bytes 589828
  16.4 6.0 %copy-start.7 = (bf16[192,512]{1,0:T(8,128)(2,1)}, bf16[192,512]{1,0:T(8,128)(2,1)S(1)}, u32[]{:S(2)}) copy-start(bf16[192,512]{1,0:T(8,128)(2,1)S(1)} %collective-permute-done.refs_1_) | copy-start | bytes 589828
  16.4 2.2 %collective-permute-start.8 = (bf16[192,512]{1,0:T(8,128)(2,1)S(1)}, bf16[192,512]{1,0:T(8,128)(2,1)S(1)}, u32[]{:S(2)}, u32[]{:S(2)}) collective-permute-start(bf16[192,512]{1,0:T(8,128)(2,1)S(1)} %collective-permute-done.1.refs_2_), channel_id=1, source_target_pairs={{0,2},{2,0},{4,6},{6,4},{8,10},{10,8},{12,14},{14,12},{16,18},{18,... | collective-permute-start | bytes 589832 | tf_op jit(solution)/shard_map/ppermute | solution.py:320
  16.4 3.6 %collective-permute-start.9 = (bf16[192,512]{1,0:T(8,128)(2,1)S(1)}, bf16[192,512]{1,0:T(8,128)(2,1)S(1)}, u32[]{:S(2)}, u32[]{:S(2)}) collective-permute-start(bf16[192,512]{1,0:T(8,128)(2,1)S(1)} %collective-permute-done.2.refs_3_), channel_id=1, source_target_pairs={{0,2},{2,0},{4,6},{6,4},{8,10},{10,8},{12,14},{14,12},{16,18},{18,... | collective-permute-start | bytes 589832 | tf_op jit(solution)/shard_map/ppermute | solution.py:320
  16.9 3.9 %collective-permute-start.10 = (bf16[192,512]{1,0:T(8,128)(2,1)S(1)}, bf16[192,512]{1,0:T(8,128)(2,1)S(1)}, u32[]{:S(2)}, u32[]{:S(2)}) collective-permute-start(bf16[192,512]{1,0:T(8,128)(2,1)S(1)} %collective-permute-done.3.refs_4_), channel_id=1, source_target_pairs={{0,2},{2,0},{4,6},{6,4},{8,10},{10,8},{12,14},{14,12},{16,18},{18,... | collective-permute-start | bytes 589832 | tf_op jit(solution)/shard_map/ppermute | solution.py:320
  17.0 11.2 %collective-permute-start.4 = (bf16[192,512]{1,0:T(8,128)(2,1)S(1)}, bf16[192,512]{1,0:T(8,128)(2,1)S(1)}, u32[]{:S(2)}, u32[]{:S(2)}) collective-permute-start(bf16[192,512]{1,0:T(8,128)(2,1)S(1)} %collective-permute-done.2.refs_3_), channel_id=1, source_target_pairs={{0,4},{2,6},{4,0},{6,2},{8,12},{10,14},{12,8},{14,10},{16,20},{18,... | collective-permute-start | bytes 589832 | tf_op jit(solution)/shard_map/ppermute | solution.py:320
  18.6 3.8 %copy-start.8 = (bf16[192,512]{1,0:T(8,128)(2,1)}, bf16[192,512]{1,0:T(8,128)(2,1)S(1)}, u32[]{:S(2)}) copy-start(bf16[192,512]{1,0:T(8,128)(2,1)S(1)} %collective-permute-done.8.refs_5_) | copy-start | bytes 589828
  18.6 9.7 %collective-permute-start.6 = (bf16[192,512]{1,0:T(8,128)(2,1)S(1)}, bf16[192,512]{1,0:T(8,128)(2,1)S(1)}, u32[]{:S(2)}, u32[]{:S(2)}) collective-permute-start(bf16[192,512]{1,0:T(8,128)(2,1)S(1)} %collective-permute-done.3.refs_4_), channel_id=1, source_target_pairs={{0,8},{2,10},{4,12},{6,14},{8,0},{10,2},{12,4},{14,6},{16,24},{18,... | collective-permute-start | bytes 589832 | tf_op jit(solution)/shard_map/ppermute | solution.py:320
  20.0 2.4 %copy-start.9 = (bf16[192,512]{1,0:T(8,128)(2,1)}, bf16[192,512]{1,0:T(8,128)(2,1)S(1)}, u32[]{:S(2)}) copy-start(bf16[192,512]{1,0:T(8,128)(2,1)S(1)} %collective-permute-done.9.refs_6_) | copy-start | bytes 589828
  20.0 8.5 %collective-permute-start.5 = (bf16[192,512]{1,0:T(8,128)(2,1)S(1)}, bf16[192,512]{1,0:T(8,128)(2,1)S(1)}, u32[]{:S(2)}, u32[]{:S(2)}) collective-permute-start(bf16[192,512]{1,0:T(8,128)(2,1)S(1)} %collective-permute-done.3.refs_4_), channel_id=1, source_target_pairs={{0,4},{2,6},{4,0},{6,2},{8,12},{10,14},{12,8},{14,10},{16,20},{18,... | collective-permute-start | bytes 589832 | tf_op jit(solution)/shard_map/ppermute | solution.py:320
  20.9 1.6 %copy-start.10 = (bf16[192,512]{1,0:T(8,128)(2,1)}, bf16[192,512]{1,0:T(8,128)(2,1)S(1)}, u32[]{:S(2)}) copy-start(bf16[192,512]{1,0:T(8,128)(2,1)S(1)} %collective-permute-done.10.refs_7_) | copy-start | bytes 589828
  20.9 26.4 %collective-permute-start.20 = (bf16[512,1024]{1,0:T(8,128)(2,1)S(1)}, bf16[512,1024]{1,0:T(8,128)(2,1)}, u32[]{:S(2)}, u32[]{:S(2)}) collective-permute-start(bf16[512,1024]{1,0:T(8,128)(2,1)S(1)} %get-tuple-element.99), channel_id=1, source_target_pairs={{0,1},{1,0},{2,3},{3,2},{4,5},{5,4},{6,7},{7,6},{8,9},{9,8},{10,11... | collective-permute-start | bytes 3145736 | tf_op jit(solution)/shard_map/ppermute | solution.py:323
  28.2 15.8 %copy-start.3 = (bf16[512,512]{1,0:T(8,128)(2,1)}, bf16[512,512]{1,0:T(8,128)(2,1)S(1)}, u32[]{:S(2)}) copy-start(bf16[512,512]{1,0:T(8,128)(2,1)S(1)} %collective-permute-done.7.refs_0_) | copy-start | bytes 1572868
  28.5 2.1 %collective-permute-start.12 = (bf16[192,512]{1,0:T(8,128)(2,1)S(1)}, bf16[192,512]{1,0:T(8,128)(2,1)S(1)}, u32[]{:S(2)}, u32[]{:S(2)}) collective-permute-start(bf16[192,512]{1,0:T(8,128)(2,1)S(1)} %collective-permute-done.4.refs_0_), channel_id=1, source_target_pairs={{0,2},{2,0},{4,6},{6,4},{8,10},{10,8},{12,14},{14,12},{16,18},{18,... | collective-permute-start | bytes 589832 | tf_op jit(solution)/shard_map/ppermute | solution.py:320
  28.5 2.1 %collective-permute-start.14 = (bf16[192,512]{1,0:T(8,128)(2,1)S(1)}, bf16[192,512]{1,0:T(8,128)(2,1)S(1)}, u32[]{:S(2)}, u32[]{:S(2)}) collective-permute-start(bf16[192,512]{1,0:T(8,128)(2,1)S(1)} %collective-permute-done.5.refs_2_), channel_id=1, source_target_pairs={{0,2},{2,0},{4,6},{6,4},{8,10},{10,8},{12,14},{14,12},{16,18},{18,... | collective-permute-start | bytes 589832 | tf_op jit(solution)/shard_map/ppermute | solution.py:320
  29.0 1.6 %collective-permute-start.13 = (bf16[192,512]{1,0:T(8,128)(2,1)S(1)}, bf16[192,512]{1,0:T(8,128)(2,1)S(1)}, u32[]{:S(2)}, u32[]{:S(2)}) collective-permute-start(bf16[192,512]{1,0:T(8,128)(2,1)S(1)} %collective-permute-done.6.refs_1_), channel_id=1, source_target_pairs={{0,2},{2,0},{4,6},{6,4},{8,10},{10,8},{12,14},{14,12},{16,18},{18,... | collective-permute-start | bytes 589832 | tf_op jit(solution)/shard_map/ppermute | solution.py:320
  29.0 7.3 %collective-permute-start.11 = (bf16[192,512]{1,0:T(8,128)(2,1)S(1)}, bf16[192,512]{1,0:T(8,128)(2,1)S(1)}, u32[]{:S(2)}, u32[]{:S(2)}) collective-permute-start(bf16[192,512]{1,0:T(8,128)(2,1)S(1)} %collective-permute-done.6.refs_1_), channel_id=1, source_target_pairs={{0,4},{2,6},{4,0},{6,2},{8,12},{10,14},{12,8},{14,10},{16,20},{18,... | collective-permute-start | bytes 589832 | tf_op jit(solution)/shard_map/ppermute | solution.py:320
  36.3 3.5 %collective-permute-start.16 = (bf16[512,512]{1,0:T(8,128)(2,1)S(1)}, bf16[512,512]{1,0:T(8,128)(2,1)S(1)}, u32[]{:S(2)}, u32[]{:S(2)}) collective-permute-start(bf16[512,512]{1,0:T(8,128)(2,1)S(1)} %collective-permute-done.7.refs_0_), channel_id=1, source_target_pairs={{0,2},{2,0},{4,6},{6,4},{8,10},{10,8},{12,14},{14,12},{16,18},{18,... | collective-permute-start | bytes 1572872 | tf_op jit(solution)/shard_map/ppermute | solution.py:320
  36.3 3.5 %collective-permute-start.15 = (bf16[192,512]{1,0:T(8,128)(2,1)S(1)}, bf16[192,512]{1,0:T(8,128)(2,1)S(1)}, u32[]{:S(2)}, u32[]{:S(2)}) collective-permute-start(bf16[192,512]{1,0:T(8,128)(2,1)S(1)} %collective-permute-done.11.refs_0_), channel_id=1, source_target_pairs={{0,2},{2,0},{4,6},{6,4},{8,10},{10,8},{12,14},{14,12},{16,18},{18,... | collective-permute-start | bytes 589832 | tf_op jit(solution)/shard_map/ppermute | solution.py:320
  36.8 10.5 %collective-permute-start.18 = (bf16[512,256]{1,0:T(8,128)(2,1)S(1)}, bf16[512,256]{1,0:T(8,128)(2,1)}, u32[]{:S(2)}, u32[]{:S(2)}) collective-permute-start(bf16[512,256]{1,0:T(8,128)(2,1)S(1)} %get-tuple-element.97), channel_id=1, source_target_pairs={{0,8},{2,10},{4,12},{6,14},{8,0},{10,2},{12,4},{14,6},{16,24},{18,... | collective-permute-start | bytes 786440 | tf_op jit(solution)/shard_map/ppermute | solution.py:320
  38.3 9.0 %collective-permute-start.19 = (bf16[512,256]{1,0:T(8,128)(2,1)S(1)}, bf16[512,256]{1,0:T(8,128)(2,1)}, u32[]{:S(2)}, u32[]{:S(2)}) collective-permute-start(bf16[512,256]{1,0:T(8,128)(2,1)S(1)} %get-tuple-element.98), channel_id=1, source_target_pairs={{0,4},{2,6},{4,0},{6,2},{8,12},{10,14},{12,8},{14,10},{16,20},{18,... | collective-permute-start | bytes 786440 | tf_op jit(solution)/shard_map/ppermute | solution.py:320
  42.4 8.6 %collective-permute-start.17 = (bf16[192,512]{1,0:T(8,128)(2,1)S(1)}, bf16[192,512]{1,0:T(8,128)(2,1)S(1)}, u32[]{:S(2)}, u32[]{:S(2)}) collective-permute-start(bf16[192,512]{1,0:T(8,128)(2,1)S(1)} %get-tuple-element.95), channel_id=1, source_target_pairs={{0,1},{1,0},{2,3},{3,2},{4,5},{5,4},{6,7},{7,6},{8,9},{9,8},{10,11... | collective-permute-start | bytes 589832 | tf_op jit(solution)/shard_map/ppermute | solution.py:323
  51.0 4.4 %collective-permute-start.21 = (bf16[512,1024]{1,0:T(8,128)(2,1)}, bf16[512,1024]{1,0:T(8,128)(2,1)S(1)}, u32[]{:S(2)}, u32[]{:S(2)}) collective-permute-start(bf16[512,1024]{1,0:T(8,128)(2,1)} %collective-permute-done.20.refs_3_), channel_id=1, source_target_pairs={{0,2},{2,0},{4,6},{6,4},{8,10},{10,8},{12,14},{14,12},{16,18},{18,... | collective-permute-start | bytes 3145736 | tf_op jit(solution)/shard_map/ppermute | solution.py:320
  51.0 4.4 %collective-permute-start.22 = (bf16[512,256]{1,0:T(8,128)(2,1)}, bf16[512,256]{1,0:T(8,128)(2,1)}, u32[]{:S(2)}, u32[]{:S(2)}) collective-permute-start(bf16[512,256]{1,0:T(8,128)(2,1)} %collective-permute-done.18.refs_1_), channel_id=1, source_target_pairs={{0,2},{2,0},{4,6},{6,4},{8,10},{10,8},{12,14},{14,12},{16,18},{18,... | collective-permute-start | bytes 786440 | tf_op jit(solution)/shard_map/ppermute | solution.py:320
  51.5 3.9 %collective-permute-start.23 = (bf16[512,256]{1,0:T(8,128)(2,1)}, bf16[512,256]{1,0:T(8,128)(2,1)}, u32[]{:S(2)}, u32[]{:S(2)}) collective-permute-start(bf16[512,256]{1,0:T(8,128)(2,1)} %collective-permute-done.19.refs_2_), channel_id=1, source_target_pairs={{0,2},{2,0},{4,6},{6,4},{8,10},{10,8},{12,14},{14,12},{16,18},{18,... | collective-permute-start | bytes 786440 | tf_op jit(solution)/shard_map/ppermute | solution.py:320

commit v3 on v2

--- a/solution.py
+++ b/solution.py
@@ -25,6 +25,7 @@
 
 
 SMALL = pl.CostEstimate(flops=1, bytes_accessed=1, transcendentals=0)
+LARGE = pl.CostEstimate(flops=10**11, bytes_accessed=1, transcendentals=0)
 NT = (((1,), (1,)), ((), ()))
 
 
@@ -197,30 +198,35 @@
     )(left, *in_hbm([weight]))
 
 
-def project_other_kernel(counts, early, ours, starts, left, partial, *refs):
-    pieces, refs = refs[: len(counts)], refs[len(counts) + 2 * ours :]
-    outs, held, sums, (sems, out_sems) = refs[:2], refs[2 : 2 + early], refs[2 + early : -2], refs[-2:]
-    copies = []
-    for n in range(early):
-        copies.append(pltpu.make_async_copy(pieces[n], held[n], sems.at[n]))
-        copies[-1].start()
+def columns_at(starts, counts, n, width):
+    width = width // counts[n]
+    at = sum(counts[:n])
+    return [
+        (
+            slice(m * width, (m + 1) * width),
+            pl.ds(pl.multiple_of(starts[at + m], HD), width),
+        )
+        for m in range(counts[n])
+    ]
+
+
+def project_other_kernel(counts, early, done, starts, left, partial, *refs):
+    total = len(counts)
+    pieces, refs = refs[:total], refs[total:]
+    outs, refs = (refs[:2], refs[2:]) if done else ([], refs)
+    sums, refs = list(pieces[:done]) + list(refs[: total - done]), refs[total - done :]
+    held, (sems, out_sems) = refs[:early], refs[early:]
     run = left.shape[0] // 2
     rows = left[...]
-    stores = []
-    for n in list(range(early, len(counts))) + list(range(early)):
-        piece = pieces[n]
-        if n < early:
-            copies[n].wait()
-            piece = held[n]
-        other = jnp.dot(rows, piece[...], preferred_element_type=jnp.float32)
-        other = other.astype(jnp.bfloat16).astype(jnp.float32)
-        width = piece.shape[1] // counts[n]
-        for m in range(counts[n]):
-            cols = pl.ds(pl.multiple_of(starts[sum(counts[:n]) + m], HD), width)
-            here = slice(m * width, (m + 1) * width)
-            sums[n][:, here] = (partial[:, cols].astype(jnp.float32) + other[:, here]).astype(
-                jnp.bfloat16
-            )
+    copies, stores = [], []
+    for n in range(early):
+        copies.append(pltpu.make_async_copy(pieces[done + n], held[n], sems.at[n]))
+        copies[-1].start()
+
+    def store(n):
+        if not done:
+            return
+        for m, (here, cols) in enumerate(columns_at(starts, counts, n, sums[n].shape[1])):
             for k in range(2):
                 stores.append(
                     pltpu.make_async_copy(
@@ -230,31 +236,46 @@
                     )
                 )
                 stores[-1].start()
-    for store in stores:
-        store.wait()
-
-
-def project_other(starts, left, partial, early, late, outs=()):
-    rows = left.shape[0]
-    width = partial.shape[1]
+
+    for n in range(done):
+        store(n)
+    for n in list(range(done + early, total)) + list(range(done, done + early)):
+        piece = pieces[n]
+        if n < done + early:
+            copies[n - done].wait()
+            piece = held[n - done]
+        other = jnp.dot(rows, piece[...], preferred_element_type=jnp.float32)
+        other = other.astype(jnp.bfloat16).astype(jnp.float32)
+        for here, cols in columns_at(starts, counts, n, piece.shape[1]):
+            sums[n][:, here] = (partial[:, cols].astype(jnp.float32) + other[:, here]).astype(
+                jnp.bfloat16
+            )
+        store(n)
+    for copy in stores:
+        copy.wait()
+
+
+def project_other(places, left, partial, early, late, done=()):
+    rows, width = left.shape[0], partial.shape[1]
+    pieces = early + late
+    counts = tuple(len(some) for some in places)
+    starts = jnp.stack([start for some in places for start in some])
+    sums = [jax.ShapeDtypeStruct((rows, piece.shape[1]), jnp.bfloat16) for piece in pieces]
     out = jax.ShapeDtypeStruct((rows // 2, width), jnp.bfloat16)
-    pieces = early + late
-    counts = tuple(len(some) for some in starts)
-    starts = jnp.stack([start for some in starts for start in some])
+    scratch = [pltpu.VMEM(some.shape, some.dtype) for some in sums] if done else []
+    scratch = scratch + [pltpu.VMEM(piece.shape, piece.dtype) for piece in early]
     return pl.pallas_call(
-        functools.partial(project_other_kernel, counts, len(early), int(bool(outs))),
-        out_shape=(out, out),
-        in_specs=[SMEM, VMEM, VMEM] + [ANY] * len(early) + [VMEM] * len(late) + [HBM] * len(outs),
-        out_specs=(HBM, HBM),
-        input_output_aliases={3 + len(pieces) + n: n for n in range(len(outs))},
-        scratch_shapes=[pltpu.VMEM(piece.shape, piece.dtype) for piece in early]
-        + [pltpu.VMEM((rows, piece.shape[1]), jnp.bfloat16) for piece in pieces]
+        functools.partial(project_other_kernel, counts, len(early), len(done)),
+        out_shape=[out, out] if done else sums,
+        in_specs=[SMEM, VMEM, VMEM] + [VMEM] * len(done) + [ANY] * len(early) + [VMEM] * len(late),
+        out_specs=[HBM, HBM] if done else [VMEM] * len(sums),
+        scratch_shapes=scratch
         + [pltpu.SemaphoreType.DMA((max(len(early), 1),))]
-        + [pltpu.SemaphoreType.DMA((sum(counts), 2))],
+        + [pltpu.SemaphoreType.DMA((len(starts), 2))],
         compiler_params=pltpu.CompilerParams(vmem_limit_bytes=16 * 2**20),
-        cost_estimate=SMALL,
-        name="project_other",
-    )(starts, left, partial, *in_hbm(early), *late, *outs)
+        cost_estimate=SMALL if done else LARGE,
+        name="project_last" if done else "project_other",
+    )(starts, left, partial, *done, *in_hbm(early), *late)
 
 
 def whole_program(
@@ -274,17 +295,16 @@
     return summed[:, :width], summed[:, width:]
 
 
-def stage_kernel(widths, starts, key, tangent_key, value, tangent_value, weight, pack, *refs):
-    parts, sems = refs[:-1], refs[-1]
-    moves = []
+def stage_kernel(widths, count, starts, weight, *refs):
+    fields, outs, sems = refs[:count], refs[count:-1], refs[-1]
+    moves = [(field, outs[0].at[:, n * HD : (n + 1) * HD]) for n, field in enumerate(fields)]
+    parts = outs[1:] if fields else outs
     for part, some in zip(parts, widths):
         at = 0
         for width in some:
-            source = weight.at[:, pl.ds(pl.multiple_of(starts[len(moves)], HD), width)]
-            moves.append((source, part.at[:, at : at + width]))
+            cols = pl.ds(pl.multiple_of(starts[len(moves) - count], HD), width)
+            moves.append((weight.at[:, cols], part.at[:, at : at + width]))
             at += width
-    for n, field in enumerate((key, tangent_key, value, tangent_value)):
-        moves.append((field, pack.at[:, n * HD : (n + 1) * HD]))
     copies = [pltpu.make_async_copy(*move, sems.at[n]) for n, move in enumerate(moves)]
     for copy in copies:
         copy.start()
@@ -292,18 +312,20 @@
         copy.wait()
 
 
-def stage(starts, fields, weight, widths):
-    rows, depth = fields[0].shape[0], weight.shape[0]
+def stage(starts, weight, widths, fields=()):
+    shapes = [(weight.shape[0], sum(some)) for some in widths]
+    if fields:
+        shapes = [(fields[0].shape[0], HD * len(fields))] + shapes
     return pl.pallas_call(
-        functools.partial(stage_kernel, widths),
-        out_shape=[jax.ShapeDtypeStruct((rows, 4 * HD), jnp.bfloat16)]
-        + [jax.ShapeDtypeStruct((depth, sum(some)), jnp.bfloat16) for some in widths],
-        in_specs=[SMEM] + [HBM] * 5,
-        out_specs=[VMEM] * (1 + len(widths)),
-        scratch_shapes=[pltpu.SemaphoreType.DMA((4 + sum(len(some) for some in widths),))],
+        functools.partial(stage_kernel, widths, len(fields)),
+        out_shape=[jax.ShapeDtypeStruct(shape, jnp.bfloat16) for shape in shapes],
+        in_specs=[SMEM] + [HBM] * (1 + len(fields)),
+        out_specs=[VMEM] * len(shapes),
+        scratch_shapes=[pltpu.SemaphoreType.DMA((len(fields) + len(starts),))],
         compiler_params=pltpu.CompilerParams(vmem_limit_bytes=4 * 2**20),
+        cost_estimate=SMALL,
         name="stage",
-    )(starts, *in_hbm((*fields, weight)))
+    )(jnp.stack(starts), *in_hbm((weight, *fields)))
 
 
 def paired_program(
@@ -334,12 +356,10 @@
     def by_core(core):
         return (8 + 4 * core) * part
 
-    pack, shared, direct = stage(
-        jnp.stack([by_level(level, core), by_column(column, core), by_core(core)]),
-        (key, tangent_key, value, tangent_value),
-        out_weight,
-        ((part, part), (4 * part,)),
-    )
+    fields = (key, tangent_key, value, tangent_value)
+    places = [by_level(level, core), by_column(column, core)]
+    pack, shared = stage(places, out_weight, ((part, part),), fields)
+    (direct,) = stage([by_core(core)], out_weight, ((4 * part,),))
     tie = lax.optimization_barrier
     bits = ([0, 1, 2, 4, 8, 3, 5, 9], [6, 12, 10, 7, 13, 11], [14, 15])
     metas = [
@@ -347,8 +367,8 @@
         for some in bits
     ]
 
+    c0, x0, z1, z2 = swap(pack, 1), swap(pack, 2), swap(pack, 4), swap(pack, 8)
     shared = cross(shared)
-    c0, x0, z1, z2 = swap(pack, 1), swap(pack, 2), swap(pack, 4), swap(pack, 8)
     metas, pack, c0, x0, z1, z2, direct = tie((metas, pack, c0, x0, z1, z2, direct))
     direct = cross(direct)
     cx0, cz1, cz2 = swap(x0, 1), swap(z1, 1), swap(z2, 1)
@@ -368,31 +388,23 @@
     cx3, shared_core = tie((swap(x3, 1), swap(shared, 1)))
     theirs, mine = attend(metas[2], query, tangent_query, [x3, cx3], state, held=True)
 
-    other, partial, level_part, column_part, direct = tie(
-        (cross(theirs), project_own(mine, out_weight), level_part, column_part, direct)
+    other = cross(theirs)
+    partial, level_part, column_part, direct = tie(
+        (project_own(mine, out_weight), level_part, column_part, direct)
     )
     far = [swap(p, 1) for p in (direct, level_part, column_part)]
-    outs = project_other(
-        [
-            [by_level(level, core), by_column(column, core)],
-            [by_level(1 - level, core)],
-            [by_column(1 - column, core)],
-            [by_core(core)],
-            [by_level(level, 1 - core), by_column(column, 1 - core)],
-        ],
-        other,
-        partial,
-        [shared, level_part, column_part, direct],
-        [shared_core],
+    near = [
+        [by_level(level, core), by_column(column, core)],
+        [by_level(level, 1 - core), by_column(column, 1 - core)],
+        [by_level(1 - level, core)],
+        [by_column(1 - column, core)],
+        [by_core(core)],
+    ]
+    sums = project_other(
+        near, other, partial, [shared, shared_core], [level_part, column_part, direct]
     )
-    return project_other(
-        [[by_core(1 - core)], [by_level(1 - level, 1 - core)], [by_column(1 - column, 1 - core)]],
-        other,
-        partial,
-        [],
-        far,
-        outs,
-    )
+    rest = [[by_core(1 - core)], [by_level(1 - level, 1 - core)], [by_column(1 - column, 1 - core)]]
+    return tuple(project_other(near + rest, other, partial, [], far, sums))
 
 
 def solution(mesh):

time: 58.2 us -> 56 us (0.962)
  waiting for transfers between devices: 8.03 us -> 5.31 us
  local copies, waits for them, and re-layouts: 2.26 us -> 4.15 us
  starting transfers between devices: 22.3 us -> 20.7 us
    slice x1, local copies, waits for them, and re-layouts: 0.04 us -> 1.85 us  [paired_program(): level_part, column_part = (shared[:, :part], shared[:, part:])]
    ppermute x21, waiting for transfers between devices: 4.32 us -> 2.74 us  [swap(): return lax.ppermute(array, 'ctx', [(i, i ^ bits) for i in range(count)])]
    ppermute x21, starting transfers between devices: 17.7 us -> 16.4 us  [swap(): return lax.ppermute(array, 'ctx', [(i, i ^ bits) for i in range(count)])]
    pallas_call x2, Pallas kernels: 5.97 us -> 4.8 us  [project_other(): pl.pallas_call(functools.partial(project_other_kernel, counts, len(early)...]
    ppermute x3, waiting for transfers between devices: 3.71 us -> 2.58 us  [cross(): return lax.ppermute(array, 'head', [(0, 1), (1, 0)])]
    pallas_call x1 -> x2, Pallas kernels: 2.01 us -> 2.98 us  [stage(): pl.pallas_call(functools.partial(stage_kernel, widths, len(fields)), out_...]
    pallas_call x3, Pallas kernels: 11.3 us -> 11.9 us  [attend(): pl.pallas_call(functools.partial(attend_kernel, sizes), out_shape=outs, i...]
  transfers between devices with their start and end apart: 24 -> 24, of which waited for: 5 -> 5; matrix products, arithmetic and copies ran while one was open for 6% -> 10% of each run, Pallas kernels for 32% -> 34%
where the time goes in v3:
time: 56 us; the launch traced here: 55.7 us
  Pallas kernels  23 us (41%)
  starting transfers between devices  20.7 us (37%)
  waiting for transfers between devices  5.31 us (9%)
  local copies, waits for them, and re-layouts  4.15 us (7%)
  other arithmetic  1.43 us (3%)
  between operations  1.14 us (2%)
    ppermute x21, starting transfers between devices, swap(): return lax.ppermute(array, 'ctx', [(i, i ^ bits) for i in range(count)])  16.4 us
    pallas_call x3, Pallas kernels, attend(): pl.pallas_call(functools.partial(attend_kernel, sizes), out_shape=outs, i...  11.9 us
    pallas_call x2, Pallas kernels, project_other(): pl.pallas_call(functools.partial(project_other_kernel, counts, len(early)...  4.8 us
    ppermute x3, starting transfers between devices, cross(): return lax.ppermute(array, 'head', [(0, 1), (1, 0)])  4.31 us
    pallas_call x1, Pallas kernels, project_own(): pl.pallas_call(functools.partial(project_own_kernel, tile), out_shape=jax...  3.27 us
    pallas_call x2, Pallas kernels, stage(): pl.pallas_call(functools.partial(stage_kernel, widths, len(fields)), out_...  2.98 us
    ppermute x21, waiting for transfers between devices, swap(): return lax.ppermute(array, 'ctx', [(i, i ^ bits) for i in range(count)])  2.74 us
    ppermute x3, waiting for transfers between devices, cross(): return lax.ppermute(array, 'head', [(0, 1), (1, 0)])  2.58 us
  transfers between devices with their start and end apart: 24, of which 5 were waited for; matrix products, arithmetic and copies ran while one was open for 10% of the time, Pallas kernels for 34%

profile of v3, /device:TPU:0, one launch (start us, length us, event | category | flops | bytes accessed | tf_op | source)
XLA Modules:
  0.0 55.7 jit_solution(12773847743861201104)
XLA Ops:
  0.6 0.0 copy-start.13
  0.6 0.0 copy-start.12
  0.7 0.0 copy-start.11
  0.7 0.1 pad_add_fusion.3.starts
  0.8 1.7 %stage.2 = (bf16[192,512]{1,0:T(8,128)(2,1)S(1)}, bf16[512,512]{1,0:T(8,128)(2,1)S(1)}) custom-call(s32[2]{0:T(128)S(1)} %pad_add_fusion.3.starts, bf16[512,4096]{1,0:T(8,128)(2,1)} %weight.5, bf16[192,128]{1,0:T(8,128)(2,1)} %refs_0_.1, bf16[192,128]{1,0:T(8,128)(2,1)} %refs_1_.1, bf16[192,128]{1,0:T(8,128)(2,1)} %refs_2_.1, bf16[192,128]{1,0:T(8,128)(2,1)} %refs_3_.1), custom_call_target="tpu_custom_call" | custom-call | flops 1 | bytes 1 | tf_op jit(solution)/shard_map/stage/pallas_call | solution.py:319
  2.5 0.0 copy-start.2
  2.5 4.1 %collective-permute-start.3 = (bf16[192,512]{1,0:T(8,128)(2,1)S(1)}, bf16[192,512]{1,0:T(8,128)(2,1)S(1)}, u32[]{:S(2)}, u32[]{:S(2)}) collective-permute-start(bf16[192,512]{1,0:T(8,128)(2,1)S(1)} %get-tuple-element.62.refs_0_), channel_id=1, source_target_pairs={{0,16},{2,18},{4,20},{6,22},{8,24},{10,26},{12,28},{14,30},{16,0},... | collective-permute-start | bytes 589832 | tf_op jit(solution)/shard_map/ppermute | solution.py:342
  6.6 1.6 %collective-permute-start.2 = (bf16[192,512]{1,0:T(8,128)(2,1)S(1)}, bf16[192,512]{1,0:T(8,128)(2,1)}, u32[]{:S(2)}, u32[]{:S(2)}) collective-permute-start(bf16[192,512]{1,0:T(8,128)(2,1)S(1)} %get-tuple-element.62.refs_0_), channel_id=1, source_target_pairs={{0,8},{2,10},{4,12},{6,14},{8,0},{10,2},{12,4},{14,6},{16,24},{18,... | collective-permute-start | bytes 589832 | tf_op jit(solution)/shard_map/ppermute | solution.py:342
  8.2 1.5 %collective-permute-start.1 = (bf16[192,512]{1,0:T(8,128)(2,1)S(1)}, bf16[192,512]{1,0:T(8,128)(2,1)S(1)}, u32[]{:S(2)}, u32[]{:S(2)}) collective-permute-start(bf16[192,512]{1,0:T(8,128)(2,1)S(1)} %get-tuple-element.62.refs_0_), channel_id=1, source_target_pairs={{0,4},{2,6},{4,0},{6,2},{8,12},{10,14},{12,8},{14,10},{16,20},{18,... | collective-permute-start | bytes 589832 | tf_op jit(solution)/shard_map/ppermute | solution.py:342
  9.7 1.5 %collective-permute-start.7 = (bf16[512,512]{1,0:T(8,128)(2,1)S(1)}, bf16[512,512]{1,0:T(8,128)(2,1)}, u32[]{:S(2)}, u32[]{:S(2)}) collective-permute-start(bf16[512,512]{1,0:T(8,128)(2,1)S(1)} %get-tuple-element.60), channel_id=1, source_target_pairs={{0,1},{1,0},{2,3},{3,2},{4,5},{5,4},{6,7},{7,6},{8,9},{9,8},{10,11... | collective-permute-start | bytes 1572872 | tf_op jit(solution)/shard_map/ppermute | solution.py:345
  11.2 0.1 reshape.16
  11.3 0.1 dynamic_slice.2
  11.4 0.0 copy-done.12
  11.4 0.6 gather_fusion.1
  12.0 0.6 gather_fusion
  12.6 0.1 lt.99
  12.6 0.1 lt.108
  12.7 0.2 convert_reduce_fusion
  12.9 0.2 fusion.1
  13.1 0.2 convert_reduce_fusion.1
  13.3 0.2 fusion
  13.5 0.6 %gather_fusion.2 = s32[2,2]{1,0:T(2,128)S(1)} fusion(s32[16,2]{1,0:T(8,128)S(1)} %reshape.16, s32[1024]{0:T(1024)S(1)} %pad_clamp_fusion), kind=kCustom, calls=%fused_computation.2 | custom fusion | bytes 40 | tf_op jit(solution)/shard_map/gather | solution.py:135
  14.1 0.1 lt.116
  14.1 0.2 fusion.2
  14.3 0.2 convert_reduce_fusion.2
  14.5 1.2 %stage.3 = bf16[512,1024]{1,0:T(8,128)(2,1)S(1)} custom-call(s32[1]{0:T(128)} %bitcast.6.starts, bf16[512,4096]{1,0:T(8,128)(2,1)} %weight.5), custom_call_target="tpu_custom_call" | custom-call | flops 1 | bytes 1 | tf_op jit(solution)/shard_map/stage/pallas_call | solution.py:319
  15.8 0.1 pad_add_fusion.1.meta
  15.8 0.1 pad_add_fusion.2.meta
  15.9 0.1 pad_add_fusion.meta
  16.0 0.0 collective-permute-done.3.refs_4_
  16.0 0.2 collective-permute-done.2.refs_3_
  16.2 0.0 collective-permute-done.1.refs_2_
  16.2 0.0 copy-start.5
  16.2 0.2 collective-permute-start.8
  16.3 0.4 collective-permute-start.9
  16.8 0.1 collective-permute-start.10
  16.8 1.5 %collective-permute-start.4 = (bf16[192,512]{1,0:T(8,128)(2,1)}, bf16[192,512]{1,0:T(8,128)(2,1)S(1)}, u32[]{:S(2)}, u32[]{:S(2)}) collective-permute-start(bf16[192,512]{1,0:T(8,128)(2,1)} %collective-permute-done.2.refs_3_), channel_id=1, source_target_pairs={{0,4},{2,6},{4,0},{6,2},{8,12},{10,14},{12,8},{14,10},{16,20},{18,... | collective-permute-start | bytes 589832 | tf_op jit(solution)/shard_map/ppermute | solution.py:342
  18.4 1.4 %collective-permute-start.6 = (bf16[192,512]{1,0:T(8,128)(2,1)S(1)}, bf16[192,512]{1,0:T(8,128)(2,1)S(1)}, u32[]{:S(2)}, u32[]{:S(2)}) collective-permute-start(bf16[192,512]{1,0:T(8,128)(2,1)S(1)} %collective-permute-done.3.refs_4_), channel_id=1, source_target_pairs={{0,8},{2,10},{4,12},{6,14},{8,0},{10,2},{12,4},{14,6},{16,24},{18,... | collective-permute-start | bytes 589832 | tf_op jit(solution)/shard_map/ppermute | solution.py:342
  19.8 0.8 %collective-permute-start.5 = (bf16[192,512]{1,0:T(8,128)(2,1)S(1)}, bf16[192,512]{1,0:T(8,128)(2,1)S(1)}, u32[]{:S(2)}, u32[]{:S(2)}) collective-permute-start(bf16[192,512]{1,0:T(8,128)(2,1)S(1)} %collective-permute-done.3.refs_4_), channel_id=1, source_target_pairs={{0,4},{2,6},{4,0},{6,2},{8,12},{10,14},{12,8},{14,10},{16,20},{18,... | collective-permute-start | bytes 589832 | tf_op jit(solution)/shard_map/ppermute | solution.py:342
  20.7 1.6 %collective-permute-start.20 = (bf16[512,1024]{1,0:T(8,128)(2,1)S(1)}, bf16[512,1024]{1,0:T(8,128)(2,1)S(1)}, u32[]{:S(2)}, u32[]{:S(2)}) collective-permute-start(bf16[512,1024]{1,0:T(8,128)(2,1)S(1)} %stage.3), channel_id=1, source_target_pairs={{0,1},{1,0},{2,3},{3,2},{4,5},{5,4},{6,7},{7,6},{8,9},{9,8},{10,11... | collective-permute-start | bytes 3145736 | tf_op jit(solution)/shard_map/ppermute | solution.py:345
  22.3 5.7 %attend_early.2 = (f32[768,128]{1,0:T(8,128)S(1)}, f32[768,128]{1,0:T(8,128)S(1)}, f32[768,128]{1,0:T(8,128)S(1)}, f32[768,256]{1,0:T(8,128)S(1)}, f32[768,128]{1,0:T(8,128)S(1)}) custom-call(s32[20]{0:T(128)S(1)} %pad_add_fusion.meta, bf16[192,512]{1,0:T(8,128)(2,1)S(1)} %copy-done, bf16[192,512]{1,0:T(8,128)(2,1)S(1)} %copy-done.1, ...), custom_call_target="tpu_custom_call" | custom-call | flops 1 | bytes 1 | tf_op jit(solution)/shard_map/attend_early/pallas_call | solution.py:154
  28.1 1.8 %fusion.3 = (bf16[512,256]{1,0:T(8,128)(2,1)}, bf16[512,256]{1,0:T(8,128)(2,1)}) fusion(bf16[512,512]{1,0:T(8,128)(2,1)} %collective-permute-done.7.refs_0_), kind=kLoop, calls=%fused_computation.22 | loop fusion | bytes 1048576 | tf_op jit(solution)/shard_map/slice | solution.py:378
  29.9 0.1 collective-permute-start.12
  30.0 0.5 collective-permute-start.14
  30.5 0.1 collective-permute-start.13
  30.6 1.2 %collective-permute-start.11 = (bf16[192,512]{1,0:T(8,128)(2,1)S(1)}, bf16[192,512]{1,0:T(8,128)(2,1)S(1)}, u32[]{:S(2)}, u32[]{:S(2)}) collective-permute-start(bf16[192,512]{1,0:T(8,128)(2,1)S(1)} %collective-permute-done.6.refs_1_), channel_id=1, source_target_pairs={{0,4},{2,6},{4,0},{6,2},{8,12},{10,14},{12,8},{14,10},{16,20},{18,... | collective-permute-start | bytes 589832 | tf_op jit(solution)/shard_map/ppermute | solution.py:342
  31.7 0.2 collective-permute-done.13.refs_4_
  32.0 3.6 %attend_early.3 = (f32[768,128]{1,0:T(8,128)S(1)}, f32[768,128]{1,0:T(8,128)S(1)}, f32[768,128]{1,0:T(8,128)S(1)}, f32[768,256]{1,0:T(8,128)S(1)}, f32[768,128]{1,0:T(8,128)S(1)}) custom-call(s32[16]{0:T(128)S(1)} %pad_add_fusion.1.meta, bf16[192,512]{1,0:T(8,128)(2,1)S(1)} %copy-done, bf16[192,512]{1,0:T(8,128)(2,1)S(1)} %copy-done.1, ...), custom_call_target="tpu_custom_call" | custom-call | flops 1 | bytes 1 | tf_op jit(solution)/shard_map/attend_early/pallas_call | solution.py:154
  35.6 2.2 %collective-permute-done.11.refs_0_ = bf16[192,512]{1,0:T(8,128)(2,1)S(1)} collective-permute-done((bf16[192,512]{1,0:T(8,128)(2,1)S(1)}, bf16[192,512]{1,0:T(8,128)(2,1)S(1)}, u32[]{:S(2)}, u32[]{:S(2)}) %collective-permute-start.11) | collective-permute-done | bytes 196640 | tf_op jit(solution)/shard_map/ppermute | solution.py:342
  37.8 0.5 collective-permute-start.15
  38.3 0.6 %collective-permute-start.18 = (bf16[512,256]{1,0:T(8,128)(2,1)}, bf16[512,256]{1,0:T(8,128)(2,1)S(1)}, u32[]{:S(2)}, u32[]{:S(2)}) collective-permute-start(bf16[512,256]{1,0:T(8,128)(2,1)} %get-tuple-element.97), channel_id=1, source_target_pairs={{0,8},{2,10},{4,12},{6,14},{8,0},{10,2},{12,4},{14,6},{16,24},{18,... | collective-permute-start | bytes 786440 | tf_op jit(solution)/shard_map/ppermute | solution.py:342
  38.9 1.2 %collective-permute-start.19 = (bf16[512,256]{1,0:T(8,128)(2,1)}, bf16[512,256]{1,0:T(8,128)(2,1)S(1)}, u32[]{:S(2)}, u32[]{:S(2)}) collective-permute-start(bf16[512,256]{1,0:T(8,128)(2,1)} %get-tuple-element.98), channel_id=1, source_target_pairs={{0,4},{2,6},{4,0},{6,2},{8,12},{10,14},{12,8},{14,10},{16,20},{18,... | collective-permute-start | bytes 786440 | tf_op jit(solution)/shard_map/ppermute | solution.py:342
  40.1 0.1 collective-permute-done.16.refs_1_
  40.2 2.6 %attend_last.1 = (bf16[192,512]{1,0:T(8,128)(2,1)S(1)}, bf16[192,512]{1,0:T(8,128)(2,1)S(1)}) custom-call(s32[8]{0:T(128)S(1)} %pad_add_fusion.2.meta, bf16[192,512]{1,0:T(8,128)(2,1)S(1)} %copy-done, bf16[192,512]{1,0:T(8,128)(2,1)S(1)} %copy-done.1, bf16[192,512]{1,0:T(8,128)(2,1)S(1)} %collective-permute-done.11.refs_0_, ...), custom_call_target="tpu_custom_call" | custom-call | flops 1 | bytes 1 | tf_op jit(solution)/shard_map/attend_last/pallas_call | solution.py:154
  42.8 1.2 %collective-permute-start.17 = (bf16[192,512]{1,0:T(8,128)(2,1)S(1)}, bf16[192,512]{1,0:T(8,128)(2,1)S(1)}, u32[]{:S(2)}, u32[]{:S(2)}) collective-permute-start(bf16[192,512]{1,0:T(8,128)(2,1)S(1)} %get-tuple-element.95), channel_id=1, source_target_pairs={{0,1},{1,0},{2,3},{3,2},{4,5},{5,4},{6,7},{7,6},{8,9},{9,8},{10,11... | collective-permute-start | bytes 589832 | tf_op jit(solution)/shard_map/ppermute | solution.py:345
  44.0 0.1 stack.67.starts
  44.1 0.1 stack.64.starts
  44.2 3.3 %project_own.1.partial = bf16[192,4096]{1,0:T(8,128)(2,1)S(1)} custom-call(bf16[192,512]{1,0:T(8,128)(2,1)S(1)} %get-tuple-element.96.left, bf16[512,4096]{1,0:T(8,128)(2,1)} %weight.5), custom_call_target="tpu_custom_call" | custom-call | flops 1 | bytes 1 | tf_op jit(solution)/shard_map/project_own/pallas_call | solution.py:186
  47.5 0.1 collective-permute-start.22
  47.6 0.5 collective-permute-start.23
  48.1 0.1 collective-permute-start.21
  48.2 2.6 %collective-permute-done.17.left = bf16[192,512]{1,0:T(8,128)(2,1)S(1)} collective-permute-done((bf16[192,512]{1,0:T(8,128)(2,1)S(1)}, bf16[192,512]{1,0:T(8,128)(2,1)S(1)}, u32[]{:S(2)}, u32[]{:S(2)}) %collective-permute-start.17) | collective-permute-done | bytes 196640 | tf_op jit(solution)/shard_map/ppermute | solution.py:345
  50.7 2.6 %project_other.1 = (bf16[192,512]{1,0:T(8,128)(2,1)S(1)}, bf16[192,512]{1,0:T(8,128)(2,1)S(1)}, bf16[192,256]{1,0:T(8,128)(2,1)S(1)}, bf16[192,256]{1,0:T(8,128)(2,1)S(1)}, bf16[192,1024]{1,0:T(8,128)(2,1)S(1)}) custom-call(s32[7]{0:T(128)S(1)} %stack.67.starts, bf16[192,512]{1,0:T(8,128)(2,1)S(1)} %collective-permute-done.17.left, ...), custom_call_target="tpu_custom_call" | custom-call | flops 99999997952 | bytes 1 | tf_op jit(solution)/shard_map/project_other/pallas_call | solution.py:267
  53.3 2.2 %project_last.1 = (bf16[96,4096]{1,0:T(8,128)(2,1)}, bf16[96,4096]{1,0:T(8,128)(2,1)}) custom-call(s32[10]{0:T(128)S(1)} %stack.64.starts, bf16[192,512]{1,0:T(8,128)(2,1)S(1)} %collective-permute-done.17.left, bf16[192,4096]{1,0:T(8,128)(2,1)S(1)} %project_own.1.partial, bf16[192,512]{1,0:T(8,128)(2,1)S(1)} %get-tuple-element.105.refs_0_, ...), custom_call_target="tpu_custom_call" | custom-call | flops 1 | bytes 1 | tf_op jit(solution)/shard_map/project_last/pallas_call | solution.py:267
  (47 shorter events, 0.1 us)
Async XLA Ops:
  0.6 10.8 %copy-start.13 = (s32[8]{0:T(128)S(1)}, s32[8]{0:T(128)}, u32[]{:S(2)}) copy-start(s32[8]{0:T(128)} %constant.12.clone) | copy-start | bytes 100
  0.6 10.8 %copy-start.12 = (s32[6]{0:T(128)S(1)}, s32[6]{0:T(128)}, u32[]{:S(2)}) copy-start(s32[6]{0:T(128)} %constant.13.clone) | copy-start | bytes 76
  0.7 12.8 %copy-start.11 = (s32[2]{0:T(128)S(1)}, s32[2]{0:T(128)}, u32[]{:S(2)}) copy-start(s32[2]{0:T(128)} %constant.14.clone) | copy-start | bytes 28
  0.7 10.6 %copy-start.9 = (s32[32]{0:T(128)S(1)}, s32[32]{0:T(128)}, u32[]{:S(2)}) copy-start(s32[32]{0:T(128)} %param.18) | copy-start | bytes 388
  0.8 21.5 %copy-start = (bf16[192,512]{1,0:T(8,128)(2,1)S(1)}, bf16[192,512]{1,0:T(8,128)(2,1)}, u32[]{:S(2)}) copy-start(bf16[192,512]{1,0:T(8,128)(2,1)} %query.5) | copy-start | bytes 589828
  0.8 21.5 %copy-start.1 = (bf16[192,512]{1,0:T(8,128)(2,1)S(1)}, bf16[192,512]{1,0:T(8,128)(2,1)}, u32[]{:S(2)}) copy-start(bf16[192,512]{1,0:T(8,128)(2,1)} %tangent_query.5) | copy-start | bytes 589828
  2.5 19.8 %copy-start.2 = (bf16[192,512]{1,0:T(8,128)(2,1)}, bf16[192,512]{1,0:T(8,128)(2,1)S(1)}, u32[]{:S(2)}) copy-start(bf16[192,512]{1,0:T(8,128)(2,1)S(1)} %get-tuple-element.62.refs_0_) | copy-start | bytes 589828
  2.5 13.5 %collective-permute-start.3 = (bf16[192,512]{1,0:T(8,128)(2,1)S(1)}, bf16[192,512]{1,0:T(8,128)(2,1)S(1)}, u32[]{:S(2)}, u32[]{:S(2)}) collective-permute-start(bf16[192,512]{1,0:T(8,128)(2,1)S(1)} %get-tuple-element.62.refs_0_), channel_id=1, source_target_pairs={{0,16},{2,18},{4,20},{6,22},{8,24},{10,26},{12,28},{14,30},{16,0},... | collective-permute-start | bytes 589832 | tf_op jit(solution)/shard_map/ppermute | solution.py:342
  6.6 9.5 %collective-permute-start.2 = (bf16[192,512]{1,0:T(8,128)(2,1)S(1)}, bf16[192,512]{1,0:T(8,128)(2,1)}, u32[]{:S(2)}, u32[]{:S(2)}) collective-permute-start(bf16[192,512]{1,0:T(8,128)(2,1)S(1)} %get-tuple-element.62.refs_0_), channel_id=1, source_target_pairs={{0,8},{2,10},{4,12},{6,14},{8,0},{10,2},{12,4},{14,6},{16,24},{18,... | collective-permute-start | bytes 589832 | tf_op jit(solution)/shard_map/ppermute | solution.py:342
  8.2 7.9 %collective-permute-start.1 = (bf16[192,512]{1,0:T(8,128)(2,1)S(1)}, bf16[192,512]{1,0:T(8,128)(2,1)S(1)}, u32[]{:S(2)}, u32[]{:S(2)}) collective-permute-start(bf16[192,512]{1,0:T(8,128)(2,1)S(1)} %get-tuple-element.62.refs_0_), channel_id=1, source_target_pairs={{0,4},{2,6},{4,0},{6,2},{8,12},{10,14},{12,8},{14,10},{16,20},{18,... | collective-permute-start | bytes 589832 | tf_op jit(solution)/shard_map/ppermute | solution.py:342
  9.7 6.5 %collective-permute-start = (bf16[192,512]{1,0:T(8,128)(2,1)S(1)}, bf16[192,512]{1,0:T(8,128)(2,1)S(1)}, u32[]{:S(2)}, u32[]{:S(2)}) collective-permute-start(bf16[192,512]{1,0:T(8,128)(2,1)S(1)} %get-tuple-element.62.refs_0_), channel_id=1, source_target_pairs={{0,2},{2,0},{4,6},{6,4},{8,10},{10,8},{12,14},{14,12},{16,18},{18,... | collective-permute-start | bytes 589832 | tf_op jit(solution)/shard_map/ppermute | solution.py:342
  9.7 18.3 %collective-permute-start.7 = (bf16[512,512]{1,0:T(8,128)(2,1)S(1)}, bf16[512,512]{1,0:T(8,128)(2,1)}, u32[]{:S(2)}, u32[]{:S(2)}) collective-permute-start(bf16[512,512]{1,0:T(8,128)(2,1)S(1)} %get-tuple-element.60), channel_id=1, source_target_pairs={{0,1},{1,0},{2,3},{3,2},{4,5},{5,4},{6,7},{7,6},{8,9},{9,8},{10,11... | collective-permute-start | bytes 1572872 | tf_op jit(solution)/shard_map/ppermute | solution.py:345
  16.0 6.3 %copy-start.3 = (bf16[192,512]{1,0:T(8,128)(2,1)}, bf16[192,512]{1,0:T(8,128)(2,1)S(1)}, u32[]{:S(2)}) copy-start(bf16[192,512]{1,0:T(8,128)(2,1)S(1)} %collective-permute-done.3.refs_4_) | copy-start | bytes 589828
  16.2 4.5 %copy-start.4 = (bf16[192,512]{1,0:T(8,128)(2,1)}, bf16[192,512]{1,0:T(8,128)(2,1)S(1)}, u32[]{:S(2)}) copy-start(bf16[192,512]{1,0:T(8,128)(2,1)S(1)} %collective-permute-done.1.refs_2_) | copy-start | bytes 589828
  16.2 4.5 %copy-start.5 = (bf16[192,512]{1,0:T(8,128)(2,1)}, bf16[192,512]{1,0:T(8,128)(2,1)S(1)}, u32[]{:S(2)}) copy-start(bf16[192,512]{1,0:T(8,128)(2,1)S(1)} %collective-permute-done.refs_1_) | copy-start | bytes 589828
  16.2 2.2 %collective-permute-start.8 = (bf16[192,512]{1,0:T(8,128)(2,1)S(1)}, bf16[192,512]{1,0:T(8,128)(2,1)S(1)}, u32[]{:S(2)}, u32[]{:S(2)}) collective-permute-start(bf16[192,512]{1,0:T(8,128)(2,1)S(1)} %collective-permute-done.1.refs_2_), channel_id=1, source_target_pairs={{0,2},{2,0},{4,6},{6,4},{8,10},{10,8},{12,14},{14,12},{16,18},{18,... | collective-permute-start | bytes 589832 | tf_op jit(solution)/shard_map/ppermute | solution.py:342
  16.3 3.5 %collective-permute-start.9 = (bf16[192,512]{1,0:T(8,128)(2,1)}, bf16[192,512]{1,0:T(8,128)(2,1)S(1)}, u32[]{:S(2)}, u32[]{:S(2)}) collective-permute-start(bf16[192,512]{1,0:T(8,128)(2,1)} %collective-permute-done.2.refs_3_), channel_id=1, source_target_pairs={{0,2},{2,0},{4,6},{6,4},{8,10},{10,8},{12,14},{14,12},{16,18},{18,... | collective-permute-start | bytes 589832 | tf_op jit(solution)/shard_map/ppermute | solution.py:342
  16.8 3.9 %collective-permute-start.10 = (bf16[192,512]{1,0:T(8,128)(2,1)S(1)}, bf16[192,512]{1,0:T(8,128)(2,1)S(1)}, u32[]{:S(2)}, u32[]{:S(2)}) collective-permute-start(bf16[192,512]{1,0:T(8,128)(2,1)S(1)} %collective-permute-done.3.refs_4_), channel_id=1, source_target_pairs={{0,2},{2,0},{4,6},{6,4},{8,10},{10,8},{12,14},{14,12},{16,18},{18,... | collective-permute-start | bytes 589832 | tf_op jit(solution)/shard_map/ppermute | solution.py:342
  16.8 13.1 %collective-permute-start.4 = (bf16[192,512]{1,0:T(8,128)(2,1)}, bf16[192,512]{1,0:T(8,128)(2,1)S(1)}, u32[]{:S(2)}, u32[]{:S(2)}) collective-permute-start(bf16[192,512]{1,0:T(8,128)(2,1)} %collective-permute-done.2.refs_3_), channel_id=1, source_target_pairs={{0,4},{2,6},{4,0},{6,2},{8,12},{10,14},{12,8},{14,10},{16,20},{18,... | collective-permute-start | bytes 589832 | tf_op jit(solution)/shard_map/ppermute | solution.py:342
  18.4 3.9 %copy-start.6 = (bf16[192,512]{1,0:T(8,128)(2,1)}, bf16[192,512]{1,0:T(8,128)(2,1)S(1)}, u32[]{:S(2)}) copy-start(bf16[192,512]{1,0:T(8,128)(2,1)S(1)} %collective-permute-done.8.refs_5_) | copy-start | bytes 589828
  18.4 11.5 %collective-permute-start.6 = (bf16[192,512]{1,0:T(8,128)(2,1)S(1)}, bf16[192,512]{1,0:T(8,128)(2,1)S(1)}, u32[]{:S(2)}, u32[]{:S(2)}) collective-permute-start(bf16[192,512]{1,0:T(8,128)(2,1)S(1)} %collective-permute-done.3.refs_4_), channel_id=1, source_target_pairs={{0,8},{2,10},{4,12},{6,14},{8,0},{10,2},{12,4},{14,6},{16,24},{18,... | collective-permute-start | bytes 589832 | tf_op jit(solution)/shard_map/ppermute | solution.py:342
  19.8 2.5 %copy-start.7 = (bf16[192,512]{1,0:T(8,128)(2,1)}, bf16[192,512]{1,0:T(8,128)(2,1)S(1)}, u32[]{:S(2)}) copy-start(bf16[192,512]{1,0:T(8,128)(2,1)S(1)} %collective-permute-done.9.refs_6_) | copy-start | bytes 589828
  19.8 10.1 %collective-permute-start.5 = (bf16[192,512]{1,0:T(8,128)(2,1)S(1)}, bf16[192,512]{1,0:T(8,128)(2,1)S(1)}, u32[]{:S(2)}, u32[]{:S(2)}) collective-permute-start(bf16[192,512]{1,0:T(8,128)(2,1)S(1)} %collective-permute-done.3.refs_4_), channel_id=1, source_target_pairs={{0,4},{2,6},{4,0},{6,2},{8,12},{10,14},{12,8},{14,10},{16,20},{18,... | collective-permute-start | bytes 589832 | tf_op jit(solution)/shard_map/ppermute | solution.py:342
  20.7 1.6 %copy-start.8 = (bf16[192,512]{1,0:T(8,128)(2,1)}, bf16[192,512]{1,0:T(8,128)(2,1)S(1)}, u32[]{:S(2)}) copy-start(bf16[192,512]{1,0:T(8,128)(2,1)S(1)} %collective-permute-done.10.refs_7_) | copy-start | bytes 589828
  20.7 26.8 %collective-permute-start.20 = (bf16[512,1024]{1,0:T(8,128)(2,1)S(1)}, bf16[512,1024]{1,0:T(8,128)(2,1)S(1)}, u32[]{:S(2)}, u32[]{:S(2)}) collective-permute-start(bf16[512,1024]{1,0:T(8,128)(2,1)S(1)} %stage.3), channel_id=1, source_target_pairs={{0,1},{1,0},{2,3},{3,2},{4,5},{5,4},{6,7},{7,6},{8,9},{9,8},{10,11... | collective-permute-start | bytes 3145736 | tf_op jit(solution)/shard_map/ppermute | solution.py:345
  29.9 1.8 %collective-permute-start.12 = (bf16[192,512]{1,0:T(8,128)(2,1)S(1)}, bf16[192,512]{1,0:T(8,128)(2,1)S(1)}, u32[]{:S(2)}, u32[]{:S(2)}) collective-permute-start(bf16[192,512]{1,0:T(8,128)(2,1)S(1)} %collective-permute-done.4.refs_0_), channel_id=1, source_target_pairs={{0,2},{2,0},{4,6},{6,4},{8,10},{10,8},{12,14},{14,12},{16,18},{18,... | collective-permute-start | bytes 589832 | tf_op jit(solution)/shard_map/ppermute | solution.py:342
  30.0 1.8 %collective-permute-start.14 = (bf16[192,512]{1,0:T(8,128)(2,1)S(1)}, bf16[192,512]{1,0:T(8,128)(2,1)S(1)}, u32[]{:S(2)}, u32[]{:S(2)}) collective-permute-start(bf16[192,512]{1,0:T(8,128)(2,1)S(1)} %collective-permute-done.5.refs_2_), channel_id=1, source_target_pairs={{0,2},{2,0},{4,6},{6,4},{8,10},{10,8},{12,14},{14,12},{16,18},{18,... | collective-permute-start | bytes 589832 | tf_op jit(solution)/shard_map/ppermute | solution.py:342
  30.5 1.5 %collective-permute-start.13 = (bf16[192,512]{1,0:T(8,128)(2,1)S(1)}, bf16[192,512]{1,0:T(8,128)(2,1)S(1)}, u32[]{:S(2)}, u32[]{:S(2)}) collective-permute-start(bf16[192,512]{1,0:T(8,128)(2,1)S(1)} %collective-permute-done.6.refs_1_), channel_id=1, source_target_pairs={{0,2},{2,0},{4,6},{6,4},{8,10},{10,8},{12,14},{14,12},{16,18},{18,... | collective-permute-start | bytes 589832 | tf_op jit(solution)/shard_map/ppermute | solution.py:342
  30.6 7.3 %collective-permute-start.11 = (bf16[192,512]{1,0:T(8,128)(2,1)S(1)}, bf16[192,512]{1,0:T(8,128)(2,1)S(1)}, u32[]{:S(2)}, u32[]{:S(2)}) collective-permute-start(bf16[192,512]{1,0:T(8,128)(2,1)S(1)} %collective-permute-done.6.refs_1_), channel_id=1, source_target_pairs={{0,4},{2,6},{4,0},{6,2},{8,12},{10,14},{12,8},{14,10},{16,20},{18,... | collective-permute-start | bytes 589832 | tf_op jit(solution)/shard_map/ppermute | solution.py:342
  37.8 2.4 %collective-permute-start.16 = (bf16[512,512]{1,0:T(8,128)(2,1)}, bf16[512,512]{1,0:T(8,128)(2,1)S(1)}, u32[]{:S(2)}, u32[]{:S(2)}) collective-permute-start(bf16[512,512]{1,0:T(8,128)(2,1)} %collective-permute-done.7.refs_0_), channel_id=1, source_target_pairs={{0,2},{2,0},{4,6},{6,4},{8,10},{10,8},{12,14},{14,12},{16,18},{18,... | collective-permute-start | bytes 1572872 | tf_op jit(solution)/shard_map/ppermute | solution.py:342
  37.8 2.3 %collective-permute-start.15 = (bf16[192,512]{1,0:T(8,128)(2,1)S(1)}, bf16[192,512]{1,0:T(8,128)(2,1)S(1)}, u32[]{:S(2)}, u32[]{:S(2)}) collective-permute-start(bf16[192,512]{1,0:T(8,128)(2,1)S(1)} %collective-permute-done.11.refs_0_), channel_id=1, source_target_pairs={{0,2},{2,0},{4,6},{6,4},{8,10},{10,8},{12,14},{14,12},{16,18},{18,... | collective-permute-start | bytes 589832 | tf_op jit(solution)/shard_map/ppermute | solution.py:342
  38.3 9.1 %collective-permute-start.18 = (bf16[512,256]{1,0:T(8,128)(2,1)}, bf16[512,256]{1,0:T(8,128)(2,1)S(1)}, u32[]{:S(2)}, u32[]{:S(2)}) collective-permute-start(bf16[512,256]{1,0:T(8,128)(2,1)} %get-tuple-element.97), channel_id=1, source_target_pairs={{0,8},{2,10},{4,12},{6,14},{8,0},{10,2},{12,4},{14,6},{16,24},{18,... | collective-permute-start | bytes 786440 | tf_op jit(solution)/shard_map/ppermute | solution.py:342
  38.9 8.6 %collective-permute-start.19 = (bf16[512,256]{1,0:T(8,128)(2,1)}, bf16[512,256]{1,0:T(8,128)(2,1)S(1)}, u32[]{:S(2)}, u32[]{:S(2)}) collective-permute-start(bf16[512,256]{1,0:T(8,128)(2,1)} %get-tuple-element.98), channel_id=1, source_target_pairs={{0,4},{2,6},{4,0},{6,2},{8,12},{10,14},{12,8},{14,10},{16,20},{18,... | collective-permute-start | bytes 786440 | tf_op jit(solution)/shard_map/ppermute | solution.py:342
  40.2 2.6 %copy-start.10 = (bf16[512,512]{1,0:T(8,128)(2,1)}, bf16[512,512]{1,0:T(8,128)(2,1)S(1)}, u32[]{:S(2)}) copy-start(bf16[512,512]{1,0:T(8,128)(2,1)S(1)} %collective-permute-done.16.refs_1_) | copy-start | bytes 1572868
  42.8 7.9 %collective-permute-start.17 = (bf16[192,512]{1,0:T(8,128)(2,1)S(1)}, bf16[192,512]{1,0:T(8,128)(2,1)S(1)}, u32[]{:S(2)}, u32[]{:S(2)}) collective-permute-start(bf16[192,512]{1,0:T(8,128)(2,1)S(1)} %get-tuple-element.95), channel_id=1, source_target_pairs={{0,1},{1,0},{2,3},{3,2},{4,5},{5,4},{6,7},{7,6},{8,9},{9,8},{10,11... | collective-permute-start | bytes 589832 | tf_op jit(solution)/shard_map/ppermute | solution.py:345
  47.5 5.8 %collective-permute-start.22 = (bf16[512,256]{1,0:T(8,128)(2,1)S(1)}, bf16[512,256]{1,0:T(8,128)(2,1)S(1)}, u32[]{:S(2)}, u32[]{:S(2)}) collective-permute-start(bf16[512,256]{1,0:T(8,128)(2,1)S(1)} %collective-permute-done.18.refs_2_), channel_id=1, source_target_pairs={{0,2},{2,0},{4,6},{6,4},{8,10},{10,8},{12,14},{14,12},{16,18},{18,... | collective-permute-start | bytes 786440 | tf_op jit(solution)/shard_map/ppermute | solution.py:342
  47.6 5.7 %collective-permute-start.23 = (bf16[512,256]{1,0:T(8,128)(2,1)S(1)}, bf16[512,256]{1,0:T(8,128)(2,1)S(1)}, u32[]{:S(2)}, u32[]{:S(2)}) collective-permute-start(bf16[512,256]{1,0:T(8,128)(2,1)S(1)} %collective-permute-done.19.refs_3_), channel_id=1, source_target_pairs={{0,2},{2,0},{4,6},{6,4},{8,10},{10,8},{12,14},{14,12},{16,18},{18,... | collective-permute-start | bytes 786440 | tf_op jit(solution)/shard_map/ppermute | solution.py:342
  48.1 5.3 %collective-permute-start.21 = (bf16[512,1024]{1,0:T(8,128)(2,1)S(1)}, bf16[512,1024]{1,0:T(8,128)(2,1)S(1)}, u32[]{:S(2)}, u32[]{:S(2)}) collective-permute-start(bf16[512,1024]{1,0:T(8,128)(2,1)S(1)} %collective-permute-done.20.refs_4_), channel_id=1, source_target_pairs={{0,2},{2,0},{4,6},{6,4},{8,10},{10,8},{12,14},{14,12},{16,18},{18,... | collective-permute-start | bytes 3145736 | tf_op jit(solution)/shard_map/ppermute | solution.py:342

commit v4 on v3

--- a/solution.py
+++ b/solution.py
@@ -30,15 +30,22 @@
 
 
 def attend_kernel(sizes, meta, query, tangent_query, *refs):
-    packs, carried, last, held, run, group, chunk = sizes
+    packs, carried, last, held, cuts, run, group, chunk = sizes
     height = group * run
     pack_refs, refs = refs[:packs], refs[packs:]
     before, refs = refs[: 5 * carried], refs[5 * carried :]
+    whole_ref, refs = (refs[0], refs[1:]) if cuts else (None, refs)
     outs, refs = (refs[:2], refs[2:]) if last else (refs[:5], refs[5:])
-    line, top, total, shift, both, mixed, sems = refs
+    cut_refs, (line, top, total, shift, both, mixed, sems) = refs[:cuts], refs[cuts:]
     state = (top, total, shift, both, mixed)
     scale = HD ** (-0.5)
 
+    aside, at = [], 0
+    for n, ref in enumerate(cut_refs):
+        source = whole_ref.at[:, at : at + ref.shape[1]]
+        aside.append(pltpu.make_async_copy(source, ref, sems.at[line.shape[0] // run + n]))
+        aside[-1].start()
+        at += ref.shape[1]
     copies = []
     blocks = [(ref, begin) for ref in pack_refs for begin in range(0, ref.shape[0], run)]
     for n, (ref, begin) in enumerate(blocks):
@@ -129,6 +136,75 @@
             head = slice(h * run, (h + 1) * run)
             out[0:run, cols] = context[head].astype(out.dtype)
             out[run : 2 * run, cols] = tangent[head].astype(out.dtype)
+    for copy in aside:
+        copy.wait()
+
+
+def finish_kernel(run, group, meta, query, tangent_query, *refs):
+    height = group * run
+    packs, before, outs, line = refs[:-8], refs[-8:-3], refs[-3:-1], refs[-1]
+    scale = HD ** (-0.5)
+    blocks = [(ref, begin) for ref in packs for begin in range(0, ref.shape[0], run)]
+    for n, (ref, begin) in enumerate(blocks):
+        place = pl.ds(pl.multiple_of(meta[4 + n] * run, run), run)
+        line[place, :] = ref[begin : begin + run, :]
+    chunk = line.shape[0]
+    for step, out in enumerate(outs):
+        half = meta[0] if step == 0 else 1 - meta[0]
+        mine = slice(step * height, (step + 1) * height)
+        rows = pl.ds(pl.multiple_of(half * run, run), run)
+        ahead = meta[2 + half]
+        q = [query[rows, h * HD : (h + 1) * HD] for h in range(group)]
+        tq = [tangent_query[rows, h * HD : (h + 1) * HD] for h in range(group)]
+        q = jnp.concatenate(q, axis=0)
+        tq_q = jnp.concatenate([jnp.concatenate(tq, axis=0), q], axis=1)
+        scores = lax.dot_general(q, line[:, 0:HD], NT, preferred_element_type=jnp.float32)
+        slopes = lax.dot_general(
+            tq_q, line[:, 0 : 2 * HD], NT, preferred_element_type=jnp.float32
+        )
+        col = lax.broadcasted_iota(jnp.int32, (height, chunk), 1)
+        scores = jnp.where(col < ahead * run, scores * (scale * LOG2E), LOWEST)
+        old, total, shift, both, mixed = (ref[mine, :] for ref in before)
+        new = jnp.maximum(old, lanes(jnp.max(scores, axis=1, keepdims=True), HD))
+        factor = jnp.exp2(old - new)
+        weights = jnp.exp2(scores - jnp.tile(new, (1, chunk // HD)))
+        product = weights * slopes
+        total, shift = total * factor, shift * factor
+        for k in range(chunk // HD):
+            total = total + weights[:, k * HD : (k + 1) * HD]
+            shift = shift + product[:, k * HD : (k + 1) * HD]
+        weights_b, product_b = weights.astype(jnp.bfloat16), product.astype(jnp.bfloat16)
+        both = both * jnp.tile(factor, (1, 2)) + jnp.dot(
+            weights_b, line[:, 2 * HD : 4 * HD], preferred_element_type=jnp.float32
+        )
+        mixed = mixed * factor + jnp.dot(
+            product_b, line[:, 2 * HD : 3 * HD], preferred_element_type=jnp.float32
+        )
+        inverse = lanes(1.0 / jnp.sum(total, axis=1, keepdims=True), HD)
+        shifted = lanes(jnp.sum(shift, axis=1, keepdims=True), HD) * (scale * inverse)
+        context = both[:, 0:HD] * inverse
+        tangent = (mixed * scale + both[:, HD : 2 * HD]) * inverse - shifted * context
+        for h in range(group):
+            cols = slice(h * HD, (h + 1) * HD)
+            head = slice(h * run, (h + 1) * run)
+            out[0:run, cols] = context[head].astype(out.dtype)
+            out[run : 2 * run, cols] = tangent[head].astype(out.dtype)
+
+
+def finish(meta, query, tangent_query, packs, before):
+    rows, width = query.shape
+    count = sum(pack.shape[0] for pack in packs)
+    out = jax.ShapeDtypeStruct((rows, width), jnp.bfloat16)
+    return pl.pallas_call(
+        functools.partial(finish_kernel, rows // 2, width // HD),
+        out_shape=(out, out),
+        in_specs=[SMEM] + [VMEM] * (2 + len(packs) + len(before)),
+        out_specs=(VMEM,) * 2,
+        scratch_shapes=[pltpu.VMEM((count, 4 * HD), jnp.bfloat16)],
+        compiler_params=pltpu.CompilerParams(vmem_limit_bytes=16 * 2**20),
+        cost_estimate=SMALL,
+        name="finish",
+    )(meta, query, tangent_query, *packs, *before)
 
 
 def ranks(order, first, me, sources, own):
@@ -139,7 +215,7 @@
     return jnp.concatenate([jnp.stack([first, jnp.int32(own)]), ahead, rank])
 
 
-def attend(meta, query, tangent_query, packs, before=(), last=True, held=False):
+def attend(meta, query, tangent_query, packs, before=(), last=True, held=False, cut=()):
     rows, width = query.shape
     run, group = rows // 2, width // HD
     count = sum(pack.shape[0] for pack in packs)
@@ -150,19 +226,24 @@
         outs = (jax.ShapeDtypeStruct((rows, width), jnp.bfloat16),) * 2
     else:
         outs = tuple(jax.ShapeDtypeStruct((2 * height, w), jnp.float32) for w in widths)
-    sizes = (len(packs), len(before) // 5, last, held, run, group, chunk)
+    whole, parts = cut[:1], cut[1:]
+    outs += tuple(jax.ShapeDtypeStruct((whole[0].shape[0], w), whole[0].dtype) for w in parts)
+    sizes = (len(packs), len(before) // 5, last, held, len(parts), run, group, chunk)
     return pl.pallas_call(
         functools.partial(attend_kernel, sizes),
         out_shape=outs,
-        in_specs=[SMEM, VMEM, VMEM] + [VMEM if held else ANY] * len(packs) + [VMEM] * len(before),
-        out_specs=(VMEM,) * len(outs),
+        in_specs=[SMEM, VMEM, VMEM]
+        + [VMEM if held else ANY] * len(packs)
+        + [VMEM] * len(before)
+        + [ANY] * len(whole),
+        out_specs=(VMEM,) * (len(outs) - len(parts)) + (ANY,) * len(parts),
         scratch_shapes=[pltpu.VMEM((count, 4 * HD), jnp.bfloat16)]
         + [pltpu.VMEM((height, w), jnp.float32) for w in widths]
-        + [pltpu.SemaphoreType.DMA((count // run,))],
+        + [pltpu.SemaphoreType.DMA((count // run + len(parts),))],
         compiler_params=pltpu.CompilerParams(vmem_limit_bytes=16 * 2**20),
         cost_estimate=SMALL,
         name="attend_last" if last else "attend_early",
-    )(meta, query, tangent_query, *(packs if held else in_hbm(packs)), *before)
+    )(meta, query, tangent_query, *(packs if held else in_hbm(packs)), *before, *whole)
 
 
 def project_own_kernel(tile, left, weight, out, held, sems):
@@ -361,32 +442,35 @@
     pack, shared = stage(places, out_weight, ((part, part),), fields)
     (direct,) = stage([by_core(core)], out_weight, ((4 * part,),))
     tie = lax.optimization_barrier
-    bits = ([0, 1, 2, 4, 8, 3, 5, 9], [6, 12, 10, 7, 13, 11], [14, 15])
+    bits = ([0, 1, 2, 4, 8, 3], [6, 12, 10, 7, 13, 11, 5, 9], [14, 15])
     metas = [
         ranks(block_order, 1 - side, me, me ^ jnp.array(some, jnp.int32), int(0 in some))
         for some in bits
     ]
 
-    c0, x0, z1, z2 = swap(pack, 1), swap(pack, 2), swap(pack, 4), swap(pack, 8)
+    x0, z1, z2 = swap(pack, 2), swap(pack, 4), swap(pack, 8)
     shared = cross(shared)
-    metas, pack, c0, x0, z1, z2, direct = tie((metas, pack, c0, x0, z1, z2, direct))
+    x0, pack = tie((x0, pack))
+    c0, cx0 = swap(pack, 1), swap(x0, 1)
+    metas, pack, c0, x0, cx0, z1, z2, direct = tie((metas, pack, c0, x0, cx0, z1, z2, direct))
+    x1, x2, z3 = swap(z1, 2), swap(z2, 2), swap(z2, 4)
     direct = cross(direct)
-    cx0, cz1, cz2 = swap(x0, 1), swap(z1, 1), swap(z2, 1)
-    x1, z3, x2 = swap(z1, 2), swap(z2, 4), swap(z2, 2)
-    packs = [pack, c0, x0, z1, z2, cx0, cz1, cz2]
-    state = attend(metas[0], query, tangent_query, packs, last=False)
-    level_part, column_part = shared[:, :part], shared[:, part:]
-    x1, x2, z3, shared, level_part, column_part, state = tie(
-        (x1, x2, z3, shared, level_part, column_part, state)
+    cz1, cz2 = swap(z1, 1), swap(z2, 1)
+    packs = [pack, c0, x0, z1, z2, cx0]
+    *state, level_part, column_part = attend(
+        metas[0], query, tangent_query, packs, last=False, cut=(shared, part, part)
+    )
+    x1, x2, z3, cz1, cz2, shared, level_part, column_part, state = tie(
+        (x1, x2, z3, cz1, cz2, shared, level_part, column_part, state)
     )
     x3 = swap(z3, 2)
     cx1, cz3, cx2 = swap(x1, 1), swap(z3, 1), swap(x2, 1)
-    packs = [x1, z3, x2, cx1, cz3, cx2]
+    packs = [x1, z3, x2, cx1, cz3, cx2, cz1, cz2]
     state = attend(metas[1], query, tangent_query, packs, state, last=False, held=True)
     x3, shared, level_part, column_part, state = tie((x3, shared, level_part, column_part, state))
     level_part, column_part = swap(level_part, 4), swap(column_part, 2)
     cx3, shared_core = tie((swap(x3, 1), swap(shared, 1)))
-    theirs, mine = attend(metas[2], query, tangent_query, [x3, cx3], state, held=True)
+    theirs, mine = finish(metas[2], query, tangent_query, [x3, cx3], state)
 
     other = cross(theirs)
     partial, level_part, column_part, direct = tie(

time: 56 us -> 55.8 us (level)
  waiting for transfers between devices: 5.31 us -> 9.04 us
  local copies, waits for them, and re-layouts: 4.15 us -> 2.29 us
  starting transfers between devices: 20.7 us -> 19.1 us
    ppermute x3, waiting for transfers between devices: 2.58 us -> 5.9 us  [cross(): return lax.ppermute(array, 'head', [(0, 1), (1, 0)])]
    pallas_call x3 -> x2, Pallas kernels: 11.9 us -> 8.77 us  [attend(): pl.pallas_call(functools.partial(attend_kernel, sizes), out_shape=outs, i...]
    pallas_call x0 -> x1, Pallas kernels: none -> 2.32 us  [finish(): pl.pallas_call(functools.partial(finish_kernel, rows // 2, width // HD),...]
    slice x1 -> x0, local copies, waits for them, and re-layouts: 1.85 us -> none  [paired_program(): level_part, column_part = (shared[:, :part], shared[:, part:])]
    ppermute x21, starting transfers between devices: 16.4 us -> 15.3 us  [swap(): return lax.ppermute(array, 'ctx', [(i, i ^ bits) for i in range(count)])]
  transfers between devices with their start and end apart: 24 -> 24, of which waited for: 5 -> 5; matrix products, arithmetic and copies ran while one was open for 10% -> 6% of each run, Pallas kernels for 34% -> 34%
where the time goes in v4:
time: 55.8 us; the launch traced here: 55.5 us
  Pallas kernels  22.6 us (41%)
  starting transfers between devices  19.1 us (34%)
  waiting for transfers between devices  9.04 us (16%)
  local copies, waits for them, and re-layouts  2.29 us (4%)
  other arithmetic  1.43 us (3%)
  between operations  0.94 us (2%)
    ppermute x21, starting transfers between devices, swap(): return lax.ppermute(array, 'ctx', [(i, i ^ bits) for i in range(count)])  15.3 us
    pallas_call x2, Pallas kernels, attend(): pl.pallas_call(functools.partial(attend_kernel, sizes), out_shape=outs, i...  8.77 us
    ppermute x3, waiting for transfers between devices, cross(): return lax.ppermute(array, 'head', [(0, 1), (1, 0)])  5.9 us
    pallas_call x2, Pallas kernels, project_other(): pl.pallas_call(functools.partial(project_other_kernel, counts, len(early)...  5.31 us
    ppermute x3, starting transfers between devices, cross(): return lax.ppermute(array, 'head', [(0, 1), (1, 0)])  3.81 us
    pallas_call x1, Pallas kernels, project_own(): pl.pallas_call(functools.partial(project_own_kernel, tile), out_shape=jax...  3.27 us
    ppermute x21, waiting for transfers between devices, swap(): return lax.ppermute(array, 'ctx', [(i, i ^ bits) for i in range(count)])  3.14 us
    pallas_call x2, Pallas kernels, stage(): pl.pallas_call(functools.partial(stage_kernel, widths, len(fields)), out_...  2.98 us
  transfers between devices with their start and end apart: 24, of which 5 were waited for; matrix products, arithmetic and copies ran while one was open for 6% of the time, Pallas kernels for 34%

profile of v4, /device:TPU:0, one launch (start us, length us, event | category | flops | bytes accessed | tf_op | source)
XLA Modules:
  0.0 55.5 jit_solution(17919636286473912506)
XLA Ops:
  0.6 0.0 copy-start.10
  0.6 0.0 copy-start.9
  0.7 0.0 copy-start.8
  0.7 0.1 pad_add_fusion.3.starts
  0.8 1.7 %stage.2 = (bf16[192,512]{1,0:T(8,128)(2,1)S(1)}, bf16[512,512]{1,0:T(8,128)(2,1)S(1)}) custom-call(s32[2]{0:T(128)S(1)} %pad_add_fusion.3.starts, bf16[512,4096]{1,0:T(8,128)(2,1)} %weight.5, bf16[192,128]{1,0:T(8,128)(2,1)} %refs_0_.1, bf16[192,128]{1,0:T(8,128)(2,1)} %refs_1_.1, bf16[192,128]{1,0:T(8,128)(2,1)} %refs_2_.1, bf16[192,128]{1,0:T(8,128)(2,1)} %refs_3_.1), custom_call_target="tpu_custom_call" | custom-call | flops 1 | bytes 1 | tf_op jit(solution)/shard_map/stage/pallas_call | solution.py:400
  2.5 4.1 %collective-permute-start.4 = (bf16[192,512]{1,0:T(8,128)(2,1)S(1)}, bf16[192,512]{1,0:T(8,128)(2,1)}, u32[]{:S(2)}, u32[]{:S(2)}) collective-permute-start(bf16[192,512]{1,0:T(8,128)(2,1)S(1)} %get-tuple-element.71.refs_0_), channel_id=1, source_target_pairs={{0,16},{2,18},{4,20},{6,22},{8,24},{10,26},{12,28},{14,30},{16,0},... | collective-permute-start | bytes 589832 | tf_op jit(solution)/shard_map/ppermute | solution.py:423
  6.6 1.6 %collective-permute-start.3 = (bf16[192,512]{1,0:T(8,128)(2,1)S(1)}, bf16[192,512]{1,0:T(8,128)(2,1)}, u32[]{:S(2)}, u32[]{:S(2)}) collective-permute-start(bf16[192,512]{1,0:T(8,128)(2,1)S(1)} %get-tuple-element.71.refs_0_), channel_id=1, source_target_pairs={{0,8},{2,10},{4,12},{6,14},{8,0},{10,2},{12,4},{14,6},{16,24},{18,... | collective-permute-start | bytes 589832 | tf_op jit(solution)/shard_map/ppermute | solution.py:423
  8.2 1.5 %collective-permute-start = (bf16[192,512]{1,0:T(8,128)(2,1)S(1)}, bf16[192,512]{1,0:T(8,128)(2,1)S(1)}, u32[]{:S(2)}, u32[]{:S(2)}) collective-permute-start(bf16[192,512]{1,0:T(8,128)(2,1)S(1)} %get-tuple-element.71.refs_0_), channel_id=1, source_target_pairs={{0,4},{2,6},{4,0},{6,2},{8,12},{10,14},{12,8},{14,10},{16,20},{18,... | collective-permute-start | bytes 589832 | tf_op jit(solution)/shard_map/ppermute | solution.py:423
  9.7 1.5 %collective-permute-start.10 = (bf16[512,512]{1,0:T(8,128)(2,1)S(1)}, bf16[512,512]{1,0:T(8,128)(2,1)S(1)}, u32[]{:S(2)}, u32[]{:S(2)}) collective-permute-start(bf16[512,512]{1,0:T(8,128)(2,1)S(1)} %get-tuple-element.69), channel_id=1, source_target_pairs={{0,1},{1,0},{2,3},{3,2},{4,5},{5,4},{6,7},{7,6},{8,9},{9,8},{10,11... | collective-permute-start | bytes 1572872 | tf_op jit(solution)/shard_map/ppermute | solution.py:426
  11.2 0.1 reshape.16
  11.3 0.1 dynamic_slice.2
  11.4 0.0 copy-done.9
  11.4 0.6 %gather_fusion.1 = s32[8,2]{1,0:T(8,128)S(1)} fusion(s32[16,2]{1,0:T(8,128)S(1)} %reshape.16, s32[1024]{0:T(1024)S(1)} %pad_clamp_fusion.1), kind=kCustom, calls=%fused_computation.1 | custom fusion | bytes 160 | tf_op jit(solution)/shard_map/gather | solution.py:211
  12.0 0.6 gather_fusion
  12.6 0.1 lt.99
  12.6 0.1 lt.108
  12.7 0.2 convert_reduce_fusion
  12.9 0.2 fusion.1
  13.1 0.2 convert_reduce_fusion.1
  13.3 0.2 fusion
  13.5 0.6 %gather_fusion.2 = s32[2,2]{1,0:T(2,128)S(1)} fusion(s32[16,2]{1,0:T(8,128)S(1)} %reshape.16, s32[1024]{0:T(1024)S(1)} %pad_clamp_fusion), kind=kCustom, calls=%fused_computation.2 | custom fusion | bytes 40 | tf_op jit(solution)/shard_map/gather | solution.py:211
  14.1 0.1 lt.116
  14.1 0.2 fusion.2
  14.3 1.2 %stage.3 = bf16[512,1024]{1,0:T(8,128)(2,1)S(1)} custom-call(s32[1]{0:T(128)} %bitcast.6.starts, bf16[512,4096]{1,0:T(8,128)(2,1)} %weight.5), custom_call_target="tpu_custom_call" | custom-call | flops 1 | bytes 1 | tf_op jit(solution)/shard_map/stage/pallas_call | solution.py:400
  15.6 0.1 pad_add_fusion.1.meta
  15.6 0.2 convert_reduce_fusion.2
  15.8 0.0 collective-permute-done.refs_2_
  15.8 0.1 collective-permute-start.1
  15.9 0.5 collective-permute-start.2
  16.4 0.1 pad_add_fusion.2.meta
  16.5 0.1 pad_add_fusion.meta
  16.6 0.8 %collective-permute-done.1.refs_1_ = bf16[192,512]{1,0:T(8,128)(2,1)S(1)} collective-permute-done((bf16[192,512]{1,0:T(8,128)(2,1)S(1)}, bf16[192,512]{1,0:T(8,128)(2,1)S(1)}, u32[]{:S(2)}, u32[]{:S(2)}) %collective-permute-start.1) | collective-permute-done | bytes 196640 | tf_op jit(solution)/shard_map/ppermute | solution.py:423
  17.4 0.3 collective-permute-done.2.refs_5_
  17.6 0.2 collective-permute-start.8
  17.9 0.5 collective-permute-start.5
  18.4 1.1 %collective-permute-start.7 = (bf16[192,512]{1,0:T(8,128)(2,1)}, bf16[192,512]{1,0:T(8,128)(2,1)S(1)}, u32[]{:S(2)}, u32[]{:S(2)}) collective-permute-start(bf16[192,512]{1,0:T(8,128)(2,1)} %collective-permute-done.4.refs_4_), channel_id=1, source_target_pairs={{0,8},{2,10},{4,12},{6,14},{8,0},{10,2},{12,4},{14,6},{16,24},{18,... | collective-permute-start | bytes 589832 | tf_op jit(solution)/shard_map/ppermute | solution.py:423
  19.5 3.1 %collective-permute-done.10.refs_6_.refs_0_ = bf16[512,512]{1,0:T(8,128)(2,1)S(1)} collective-permute-done((bf16[512,512]{1,0:T(8,128)(2,1)S(1)}, bf16[512,512]{1,0:T(8,128)(2,1)S(1)}, u32[]{:S(2)}, u32[]{:S(2)}) %collective-permute-start.10) | collective-permute-done | bytes 524320 | tf_op jit(solution)/shard_map/ppermute | solution.py:426
  22.5 0.5 collective-permute-start.6
  23.1 0.0 collective-permute-done.8.refs_6_
  23.1 1.5 %collective-permute-start.20 = (bf16[512,1024]{1,0:T(8,128)(2,1)S(1)}, bf16[512,1024]{1,0:T(8,128)(2,1)S(1)}, u32[]{:S(2)}, u32[]{:S(2)}) collective-permute-start(bf16[512,1024]{1,0:T(8,128)(2,1)S(1)} %stage.3), channel_id=1, source_target_pairs={{0,1},{1,0},{2,3},{3,2},{4,5},{5,4},{6,7},{7,6},{8,9},{9,8},{10,11... | collective-permute-start | bytes 3145736 | tf_op jit(solution)/shard_map/ppermute | solution.py:426
  24.6 5.0 %attend_early.2 = (f32[768,128]{1,0:T(8,128)S(1)}, f32[768,128]{1,0:T(8,128)S(1)}, f32[768,128]{1,0:T(8,128)S(1)}, f32[768,256]{1,0:T(8,128)S(1)}, f32[768,128]{...) custom-call(s32[16]{0:T(128)S(1)} %pad_add_fusion.meta, bf16[192,512]{1,0:T(8,128)(2,1)S(1)} %copy-done, ...), custom_call_target="tpu_custom_call" | custom-call | flops 1 | bytes 1 | tf_op jit(solution)/shard_map/attend_early/pallas_call | solution.py:232
  29.7 0.0 collective-permute-done.5.refs_0_
  29.7 0.0 collective-permute-done.7.refs_1_
  29.7 0.1 collective-permute-start.12
  29.8 0.5 collective-permute-start.14
  30.3 0.1 collective-permute-start.13
  30.4 1.5 %collective-permute-start.11 = (bf16[192,512]{1,0:T(8,128)(2,1)S(1)}, bf16[192,512]{1,0:T(8,128)(2,1)S(1)}, u32[]{:S(2)}, u32[]{:S(2)}) collective-permute-start(bf16[192,512]{1,0:T(8,128)(2,1)S(1)} %collective-permute-done.7.refs_1_), channel_id=1, source_target_pairs={{0,4},{2,6},{4,0},{6,2},{8,12},{10,14},{12,8},{14,10},{16,20},{18,... | collective-permute-start | bytes 589832 | tf_op jit(solution)/shard_map/ppermute | solution.py:423
  31.9 3.7 %attend_early.3 = (f32[768,128]{1,0:T(8,128)S(1)}, f32[768,128]{1,0:T(8,128)S(1)}, f32[768,128]{1,0:T(8,128)S(1)}, f32[768,256]{1,0:T(8,128)S(1)}, f32[768,128]{1,0:T(8,128)S(1)}) custom-call(s32[20]{0:T(128)S(1)} %pad_add_fusion.1.meta, bf16[192,512]{1,0:T(8,128)(2,1)S(1)} %copy-done, bf16[192,512]{1,0:T(8,128)(2,1)S(1)} %copy-done.1, ...), custom_call_target="tpu_custom_call" | custom-call | flops 1 | bytes 1 | tf_op jit(solution)/shard_map/attend_early/pallas_call | solution.py:232
  35.6 2.0 %collective-permute-done.11.refs_0_ = bf16[192,512]{1,0:T(8,128)(2,1)S(1)} collective-permute-done((bf16[192,512]{1,0:T(8,128)(2,1)S(1)}, bf16[192,512]{1,0:T(8,128)(2,1)S(1)}, u32[]{:S(2)}, u32[]{:S(2)}) %collective-permute-start.11) | collective-permute-done | bytes 196640 | tf_op jit(solution)/shard_map/ppermute | solution.py:423
  37.6 0.5 collective-permute-start.15
  38.1 0.4 collective-permute-start.18
  38.6 1.5 %collective-permute-start.19 = (bf16[512,256]{1,0:T(8,128)(2,1)S(1)}, bf16[512,256]{1,0:T(8,128)(2,1)}, u32[]{:S(2)}, u32[]{:S(2)}) collective-permute-start(bf16[512,256]{1,0:T(8,128)(2,1)S(1)} %get-tuple-element.112), channel_id=1, source_target_pairs={{0,4},{2,6},{4,0},{6,2},{8,12},{10,14},{12,8},{14,10},{16,20},{18,... | collective-permute-start | bytes 786440 | tf_op jit(solution)/shard_map/ppermute | solution.py:423
  40.1 2.3 %finish.1 = (bf16[192,512]{1,0:T(8,128)(2,1)}, bf16[192,512]{1,0:T(8,128)(2,1)S(1)}) custom-call(s32[8]{0:T(128)S(1)} %pad_add_fusion.2.meta, bf16[192,512]{1,0:T(8,128)(2,1)S(1)} %copy-done, bf16[192,512]{1,0:T(8,128)(2,1)S(1)} %copy-done.1, bf16[192,512]{1,0:T(8,128)(2,1)S(1)} %collective-permute-done.11.refs_0_, ...), custom_call_target="tpu_custom_call" | custom-call | flops 1 | bytes 1 | tf_op jit(solution)/shard_map/finish/pallas_call | solution.py:198
  42.4 0.8 %collective-permute-start.17 = (bf16[192,512]{1,0:T(8,128)(2,1)}, bf16[192,512]{1,0:T(8,128)(2,1)S(1)}, u32[]{:S(2)}, u32[]{:S(2)}) collective-permute-start(bf16[192,512]{1,0:T(8,128)(2,1)} %get-tuple-element.109), channel_id=1, source_target_pairs={{0,1},{1,0},{2,3},{3,2},{4,5},{5,4},{6,7},{7,6},{8,9},{9,8},{10,11... | collective-permute-start | bytes 589832 | tf_op jit(solution)/shard_map/ppermute | solution.py:426
  43.2 0.1 stack.67.starts
  43.2 0.1 stack.64.starts
  43.3 3.3 %project_own.1.partial = bf16[192,4096]{1,0:T(8,128)(2,1)S(1)} custom-call(bf16[192,512]{1,0:T(8,128)(2,1)S(1)} %get-tuple-element.110.left, bf16[512,4096]{1,0:T(8,128)(2,1)} %weight.5), custom_call_target="tpu_custom_call" | custom-call | flops 1 | bytes 1 | tf_op jit(solution)/shard_map/project_own/pallas_call | solution.py:267
  46.6 0.0 collective-permute-done.18.refs_2_
  46.7 0.1 collective-permute-start.22
  46.7 0.5 collective-permute-start.23
  47.2 0.1 collective-permute-start.21
  47.3 2.8 %collective-permute-done.17.left = bf16[192,512]{1,0:T(8,128)(2,1)S(1)} collective-permute-done((bf16[192,512]{1,0:T(8,128)(2,1)}, bf16[192,512]{1,0:T(8,128)(2,1)S(1)}, u32[]{:S(2)}, u32[]{:S(2)}) %collective-permute-start.17) | collective-permute-done | bytes 196640 | tf_op jit(solution)/shard_map/ppermute | solution.py:426
  50.1 3.1 %project_other.1 = (bf16[192,512]{1,0:T(8,128)(2,1)S(1)}, bf16[192,512]{1,0:T(8,128)(2,1)S(1)}, bf16[192,256]{1,0:T(8,128)(2,1)S(1)}, bf16[192,256]{1,0:T(8,128)(2,1)S(1)}, bf16[192,1024]{1,0:T(8,128)(2,1)S(1)}) custom-call(s32[7]{0:T(128)S(1)} %stack.67.starts, bf16[192,512]{1,0:T(8,128)(2,1)S(1)} %collective-permute-done.17.left, ...), custom_call_target="tpu_custom_call" | custom-call | flops 99999997952 | bytes 1 | tf_op jit(solution)/shard_map/project_other/pallas_call | solution.py:348
  53.2 2.2 %project_last.1 = (bf16[96,4096]{1,0:T(8,128)(2,1)}, bf16[96,4096]{1,0:T(8,128)(2,1)}) custom-call(s32[10]{0:T(128)S(1)} %stack.64.starts, bf16[192,512]{1,0:T(8,128)(2,1)S(1)} %collective-permute-done.17.left, bf16[192,4096]{1,0:T(8,128)(2,1)S(1)} %project_own.1.partial, bf16[192,512]{1,0:T(8,128)(2,1)S(1)} %get-tuple-element.119.refs_0_, ...), custom_call_target="tpu_custom_call" | custom-call | flops 1 | bytes 1 | tf_op jit(solution)/shard_map/project_last/pallas_call | solution.py:348
  (40 shorter events, 0.1 us)
Async XLA Ops:
  0.6 10.8 %copy-start.10 = (s32[6]{0:T(128)S(1)}, s32[6]{0:T(128)}, u32[]{:S(2)}) copy-start(s32[6]{0:T(128)} %constant.12.clone) | copy-start | bytes 76
  0.6 10.8 %copy-start.9 = (s32[8]{0:T(128)S(1)}, s32[8]{0:T(128)}, u32[]{:S(2)}) copy-start(s32[8]{0:T(128)} %constant.13.clone) | copy-start | bytes 100
  0.7 12.8 %copy-start.8 = (s32[2]{0:T(128)S(1)}, s32[2]{0:T(128)}, u32[]{:S(2)}) copy-start(s32[2]{0:T(128)} %constant.14.clone) | copy-start | bytes 28
  0.7 10.6 %copy-start.7 = (s32[32]{0:T(128)S(1)}, s32[32]{0:T(128)}, u32[]{:S(2)}) copy-start(s32[32]{0:T(128)} %param.18) | copy-start | bytes 388
  0.8 23.8 %copy-start = (bf16[192,512]{1,0:T(8,128)(2,1)S(1)}, bf16[192,512]{1,0:T(8,128)(2,1)}, u32[]{:S(2)}) copy-start(bf16[192,512]{1,0:T(8,128)(2,1)} %query.5) | copy-start | bytes 589828
  0.8 23.8 %copy-start.1 = (bf16[192,512]{1,0:T(8,128)(2,1)S(1)}, bf16[192,512]{1,0:T(8,128)(2,1)}, u32[]{:S(2)}) copy-start(bf16[192,512]{1,0:T(8,128)(2,1)} %tangent_query.5) | copy-start | bytes 589828
  2.5 22.1 %copy-start.3 = (bf16[192,512]{1,0:T(8,128)(2,1)}, bf16[192,512]{1,0:T(8,128)(2,1)S(1)}, u32[]{:S(2)}) copy-start(bf16[192,512]{1,0:T(8,128)(2,1)S(1)} %get-tuple-element.71.refs_0_) | copy-start | bytes 589828
  2.5 14.0 %collective-permute-start.4 = (bf16[192,512]{1,0:T(8,128)(2,1)S(1)}, bf16[192,512]{1,0:T(8,128)(2,1)}, u32[]{:S(2)}, u32[]{:S(2)}) collective-permute-start(bf16[192,512]{1,0:T(8,128)(2,1)S(1)} %get-tuple-element.71.refs_0_), channel_id=1, source_target_pairs={{0,16},{2,18},{4,20},{6,22},{8,24},{10,26},{12,28},{14,30},{16,0},... | collective-permute-start | bytes 589832 | tf_op jit(solution)/shard_map/ppermute | solution.py:423
  6.6 9.9 %collective-permute-start.3 = (bf16[192,512]{1,0:T(8,128)(2,1)S(1)}, bf16[192,512]{1,0:T(8,128)(2,1)}, u32[]{:S(2)}, u32[]{:S(2)}) collective-permute-start(bf16[192,512]{1,0:T(8,128)(2,1)S(1)} %get-tuple-element.71.refs_0_), channel_id=1, source_target_pairs={{0,8},{2,10},{4,12},{6,14},{8,0},{10,2},{12,4},{14,6},{16,24},{18,... | collective-permute-start | bytes 589832 | tf_op jit(solution)/shard_map/ppermute | solution.py:423
  8.2 7.6 %collective-permute-start = (bf16[192,512]{1,0:T(8,128)(2,1)S(1)}, bf16[192,512]{1,0:T(8,128)(2,1)S(1)}, u32[]{:S(2)}, u32[]{:S(2)}) collective-permute-start(bf16[192,512]{1,0:T(8,128)(2,1)S(1)} %get-tuple-element.71.refs_0_), channel_id=1, source_target_pairs={{0,4},{2,6},{4,0},{6,2},{8,12},{10,14},{12,8},{14,10},{16,20},{18,... | collective-permute-start | bytes 589832 | tf_op jit(solution)/shard_map/ppermute | solution.py:423
  9.7 12.8 %collective-permute-start.10 = (bf16[512,512]{1,0:T(8,128)(2,1)S(1)}, bf16[512,512]{1,0:T(8,128)(2,1)S(1)}, u32[]{:S(2)}, u32[]{:S(2)}) collective-permute-start(bf16[512,512]{1,0:T(8,128)(2,1)S(1)} %get-tuple-element.69), channel_id=1, source_target_pairs={{0,1},{1,0},{2,3},{3,2},{4,5},{5,4},{6,7},{7,6},{8,9},{9,8},{10,11... | collective-permute-start | bytes 1572872 | tf_op jit(solution)/shard_map/ppermute | solution.py:426
  15.8 7.2 %copy-start.4 = (bf16[192,512]{1,0:T(8,128)(2,1)}, bf16[192,512]{1,0:T(8,128)(2,1)S(1)}, u32[]{:S(2)}) copy-start(bf16[192,512]{1,0:T(8,128)(2,1)S(1)} %collective-permute-done.refs_2_) | copy-start | bytes 589828
  15.8 1.5 %collective-permute-start.1 = (bf16[192,512]{1,0:T(8,128)(2,1)S(1)}, bf16[192,512]{1,0:T(8,128)(2,1)S(1)}, u32[]{:S(2)}, u32[]{:S(2)}) collective-permute-start(bf16[192,512]{1,0:T(8,128)(2,1)S(1)} %get-tuple-element.71.refs_0_), channel_id=1, source_target_pairs={{0,2},{2,0},{4,6},{6,4},{8,10},{10,8},{12,14},{14,12},{16,18},{18,... | collective-permute-start | bytes 589832 | tf_op jit(solution)/shard_map/ppermute | solution.py:423
  15.9 1.7 %collective-permute-start.2 = (bf16[192,512]{1,0:T(8,128)(2,1)S(1)}, bf16[192,512]{1,0:T(8,128)(2,1)S(1)}, u32[]{:S(2)}, u32[]{:S(2)}) collective-permute-start(bf16[192,512]{1,0:T(8,128)(2,1)S(1)} %collective-permute-done.refs_2_), channel_id=1, source_target_pairs={{0,2},{2,0},{4,6},{6,4},{8,10},{10,8},{12,14},{14,12},{16,18},{18,... | collective-permute-start | bytes 589832 | tf_op jit(solution)/shard_map/ppermute | solution.py:423
  17.4 7.2 %copy-start.5 = (bf16[192,512]{1,0:T(8,128)(2,1)}, bf16[192,512]{1,0:T(8,128)(2,1)S(1)}, u32[]{:S(2)}) copy-start(bf16[192,512]{1,0:T(8,128)(2,1)S(1)} %collective-permute-done.1.refs_1_) | copy-start | bytes 589828
  17.6 7.0 %copy-start.6 = (bf16[192,512]{1,0:T(8,128)(2,1)}, bf16[192,512]{1,0:T(8,128)(2,1)S(1)}, u32[]{:S(2)}) copy-start(bf16[192,512]{1,0:T(8,128)(2,1)S(1)} %collective-permute-done.2.refs_5_) | copy-start | bytes 589828
  17.6 5.4 %collective-permute-start.8 = (bf16[192,512]{1,0:T(8,128)(2,1)}, bf16[192,512]{1,0:T(8,128)(2,1)S(1)}, u32[]{:S(2)}, u32[]{:S(2)}) collective-permute-start(bf16[192,512]{1,0:T(8,128)(2,1)} %collective-permute-done.3.refs_3_), channel_id=1, source_target_pairs={{0,2},{2,0},{4,6},{6,4},{8,10},{10,8},{12,14},{14,12},{16,18},{18,... | collective-permute-start | bytes 589832 | tf_op jit(solution)/shard_map/ppermute | solution.py:423
  17.9 11.8 %collective-permute-start.5 = (bf16[192,512]{1,0:T(8,128)(2,1)}, bf16[192,512]{1,0:T(8,128)(2,1)S(1)}, u32[]{:S(2)}, u32[]{:S(2)}) collective-permute-start(bf16[192,512]{1,0:T(8,128)(2,1)} %collective-permute-done.3.refs_3_), channel_id=1, source_target_pairs={{0,4},{2,6},{4,0},{6,2},{8,12},{10,14},{12,8},{14,10},{16,20},{18,... | collective-permute-start | bytes 589832 | tf_op jit(solution)/shard_map/ppermute | solution.py:423
  18.4 11.3 %collective-permute-start.9 = (bf16[192,512]{1,0:T(8,128)(2,1)}, bf16[192,512]{1,0:T(8,128)(2,1)S(1)}, u32[]{:S(2)}, u32[]{:S(2)}) collective-permute-start(bf16[192,512]{1,0:T(8,128)(2,1)} %collective-permute-done.4.refs_4_), channel_id=1, source_target_pairs={{0,2},{2,0},{4,6},{6,4},{8,10},{10,8},{12,14},{14,12},{16,18},{18,... | collective-permute-start | bytes 589832 | tf_op jit(solution)/shard_map/ppermute | solution.py:423
  18.4 11.3 %collective-permute-start.7 = (bf16[192,512]{1,0:T(8,128)(2,1)}, bf16[192,512]{1,0:T(8,128)(2,1)S(1)}, u32[]{:S(2)}, u32[]{:S(2)}) collective-permute-start(bf16[192,512]{1,0:T(8,128)(2,1)} %collective-permute-done.4.refs_4_), channel_id=1, source_target_pairs={{0,8},{2,10},{4,12},{6,14},{8,0},{10,2},{12,4},{14,6},{16,24},{18,... | collective-permute-start | bytes 589832 | tf_op jit(solution)/shard_map/ppermute | solution.py:423
  22.5 19.9 %copy-start.2 = (bf16[512,512]{1,0:T(8,128)(2,1)}, bf16[512,512]{1,0:T(8,128)(2,1)S(1)}, u32[]{:S(2)}) copy-start(bf16[512,512]{1,0:T(8,128)(2,1)S(1)} %collective-permute-done.10.refs_6_.refs_0_) | copy-start | bytes 1572868
  22.5 7.2 %collective-permute-start.6 = (bf16[192,512]{1,0:T(8,128)(2,1)}, bf16[192,512]{1,0:T(8,128)(2,1)S(1)}, u32[]{:S(2)}, u32[]{:S(2)}) collective-permute-start(bf16[192,512]{1,0:T(8,128)(2,1)} %collective-permute-done.4.refs_4_), channel_id=1, source_target_pairs={{0,4},{2,6},{4,0},{6,2},{8,12},{10,14},{12,8},{14,10},{16,20},{18,... | collective-permute-start | bytes 589832 | tf_op jit(solution)/shard_map/ppermute | solution.py:423
  23.1 23.6 %collective-permute-start.20 = (bf16[512,1024]{1,0:T(8,128)(2,1)S(1)}, bf16[512,1024]{1,0:T(8,128)(2,1)S(1)}, u32[]{:S(2)}, u32[]{:S(2)}) collective-permute-start(bf16[512,1024]{1,0:T(8,128)(2,1)S(1)} %stage.3), channel_id=1, source_target_pairs={{0,1},{1,0},{2,3},{3,2},{4,5},{5,4},{6,7},{7,6},{8,9},{9,8},{10,11... | collective-permute-start | bytes 3145736 | tf_op jit(solution)/shard_map/ppermute | solution.py:426
  29.7 2.1 %collective-permute-start.12 = (bf16[192,512]{1,0:T(8,128)(2,1)S(1)}, bf16[192,512]{1,0:T(8,128)(2,1)S(1)}, u32[]{:S(2)}, u32[]{:S(2)}) collective-permute-start(bf16[192,512]{1,0:T(8,128)(2,1)S(1)} %collective-permute-done.5.refs_0_), channel_id=1, source_target_pairs={{0,2},{2,0},{4,6},{6,4},{8,10},{10,8},{12,14},{14,12},{16,18},{18,... | collective-permute-start | bytes 589832 | tf_op jit(solution)/shard_map/ppermute | solution.py:423
  29.8 2.1 %collective-permute-start.14 = (bf16[192,512]{1,0:T(8,128)(2,1)S(1)}, bf16[192,512]{1,0:T(8,128)(2,1)S(1)}, u32[]{:S(2)}, u32[]{:S(2)}) collective-permute-start(bf16[192,512]{1,0:T(8,128)(2,1)S(1)} %collective-permute-done.6.refs_2_), channel_id=1, source_target_pairs={{0,2},{2,0},{4,6},{6,4},{8,10},{10,8},{12,14},{14,12},{16,18},{18,... | collective-permute-start | bytes 589832 | tf_op jit(solution)/shard_map/ppermute | solution.py:423
  30.3 1.6 %collective-permute-start.13 = (bf16[192,512]{1,0:T(8,128)(2,1)S(1)}, bf16[192,512]{1,0:T(8,128)(2,1)S(1)}, u32[]{:S(2)}, u32[]{:S(2)}) collective-permute-start(bf16[192,512]{1,0:T(8,128)(2,1)S(1)} %collective-permute-done.7.refs_1_), channel_id=1, source_target_pairs={{0,2},{2,0},{4,6},{6,4},{8,10},{10,8},{12,14},{14,12},{16,18},{18,... | collective-permute-start | bytes 589832 | tf_op jit(solution)/shard_map/ppermute | solution.py:423
  30.4 7.3 %collective-permute-start.11 = (bf16[192,512]{1,0:T(8,128)(2,1)S(1)}, bf16[192,512]{1,0:T(8,128)(2,1)S(1)}, u32[]{:S(2)}, u32[]{:S(2)}) collective-permute-start(bf16[192,512]{1,0:T(8,128)(2,1)S(1)} %collective-permute-done.7.refs_1_), channel_id=1, source_target_pairs={{0,4},{2,6},{4,0},{6,2},{8,12},{10,14},{12,8},{14,10},{16,20},{18,... | collective-permute-start | bytes 589832 | tf_op jit(solution)/shard_map/ppermute | solution.py:423
  37.6 2.5 %collective-permute-start.16 = (bf16[512,512]{1,0:T(8,128)(2,1)S(1)}, bf16[512,512]{1,0:T(8,128)(2,1)}, u32[]{:S(2)}, u32[]{:S(2)}) collective-permute-start(bf16[512,512]{1,0:T(8,128)(2,1)S(1)} %collective-permute-done.10.refs_6_.refs_0_), channel_id=1, source_target_pairs={{0,2},{2,0},{4,6},{6,4},{8,10},{10,8},{12,14},{14,12},{16,18},{18,... | collective-permute-start | bytes 1572872 | tf_op jit(solution)/shard_map/ppermute | solution.py:423
  37.6 2.5 %collective-permute-start.15 = (bf16[192,512]{1,0:T(8,128)(2,1)S(1)}, bf16[192,512]{1,0:T(8,128)(2,1)S(1)}, u32[]{:S(2)}, u32[]{:S(2)}) collective-permute-start(bf16[192,512]{1,0:T(8,128)(2,1)S(1)} %collective-permute-done.11.refs_0_), channel_id=1, source_target_pairs={{0,2},{2,0},{4,6},{6,4},{8,10},{10,8},{12,14},{14,12},{16,18},{18,... | collective-permute-start | bytes 589832 | tf_op jit(solution)/shard_map/ppermute | solution.py:423
  38.1 8.5 %collective-permute-start.18 = (bf16[512,256]{1,0:T(8,128)(2,1)}, bf16[512,256]{1,0:T(8,128)(2,1)}, u32[]{:S(2)}, u32[]{:S(2)}) collective-permute-start(bf16[512,256]{1,0:T(8,128)(2,1)} %get-tuple-element.111), channel_id=1, source_target_pairs={{0,8},{2,10},{4,12},{6,14},{8,0},{10,2},{12,4},{14,6},{16,24},{18,... | collective-permute-start | bytes 786440 | tf_op jit(solution)/shard_map/ppermute | solution.py:423
  38.6 8.1 %collective-permute-start.19 = (bf16[512,256]{1,0:T(8,128)(2,1)S(1)}, bf16[512,256]{1,0:T(8,128)(2,1)}, u32[]{:S(2)}, u32[]{:S(2)}) collective-permute-start(bf16[512,256]{1,0:T(8,128)(2,1)S(1)} %get-tuple-element.112), channel_id=1, source_target_pairs={{0,4},{2,6},{4,0},{6,2},{8,12},{10,14},{12,8},{14,10},{16,20},{18,... | collective-permute-start | bytes 786440 | tf_op jit(solution)/shard_map/ppermute | solution.py:423
  42.4 7.7 %collective-permute-start.17 = (bf16[192,512]{1,0:T(8,128)(2,1)}, bf16[192,512]{1,0:T(8,128)(2,1)S(1)}, u32[]{:S(2)}, u32[]{:S(2)}) collective-permute-start(bf16[192,512]{1,0:T(8,128)(2,1)} %get-tuple-element.109), channel_id=1, source_target_pairs={{0,1},{1,0},{2,3},{3,2},{4,5},{5,4},{6,7},{7,6},{8,9},{9,8},{10,11... | collective-permute-start | bytes 589832 | tf_op jit(solution)/shard_map/ppermute | solution.py:426
  46.7 6.6 %collective-permute-start.22 = (bf16[512,256]{1,0:T(8,128)(2,1)}, bf16[512,256]{1,0:T(8,128)(2,1)S(1)}, u32[]{:S(2)}, u32[]{:S(2)}) collective-permute-start(bf16[512,256]{1,0:T(8,128)(2,1)} %collective-permute-done.18.refs_2_), channel_id=1, source_target_pairs={{0,2},{2,0},{4,6},{6,4},{8,10},{10,8},{12,14},{14,12},{16,18},{18,... | collective-permute-start | bytes 786440 | tf_op jit(solution)/shard_map/ppermute | solution.py:423
  46.7 6.5 %collective-permute-start.23 = (bf16[512,256]{1,0:T(8,128)(2,1)}, bf16[512,256]{1,0:T(8,128)(2,1)S(1)}, u32[]{:S(2)}, u32[]{:S(2)}) collective-permute-start(bf16[512,256]{1,0:T(8,128)(2,1)} %collective-permute-done.19.refs_3_), channel_id=1, source_target_pairs={{0,2},{2,0},{4,6},{6,4},{8,10},{10,8},{12,14},{14,12},{16,18},{18,... | collective-permute-start | bytes 786440 | tf_op jit(solution)/shard_map/ppermute | solution.py:423
  47.2 6.0 %collective-permute-start.21 = (bf16[512,1024]{1,0:T(8,128)(2,1)S(1)}, bf16[512,1024]{1,0:T(8,128)(2,1)S(1)}, u32[]{:S(2)}, u32[]{:S(2)}) collective-permute-start(bf16[512,1024]{1,0:T(8,128)(2,1)S(1)} %collective-permute-done.20.refs_4_), channel_id=1, source_target_pairs={{0,2},{2,0},{4,6},{6,4},{8,10},{10,8},{12,14},{14,12},{16,18},{18,... | collective-permute-start | bytes 3145736 | tf_op jit(solution)/shard_map/ppermute | solution.py:423

commit v5 on v4

--- a/solution.py
+++ b/solution.py
@@ -246,12 +246,17 @@
     )(meta, query, tangent_query, *(packs if held else in_hbm(packs)), *before, *whole)
 
 
-def project_own_kernel(tile, left, weight, out, held, sems):
+def project_own_kernel(tile, relayed, left, weight, *refs):
+    sources, out, targets = refs[:relayed], refs[relayed], refs[relayed + 1 : -2]
+    held, sems = refs[-2:]
     count = weight.shape[1] // tile
     copies = []
     for n in range(count):
         cols = slice(n * tile, (n + 1) * tile)
         copies.append(pltpu.make_async_copy(weight.at[:, cols], held.at[n], sems.at[n]))
+        copies[-1].start()
+    for n, (source, target) in enumerate(zip(sources, targets)):
+        copies.append(pltpu.make_async_copy(source, target, sems.at[count + n]))
         copies[-1].start()
     rows = left[...]
     for n in range(count):
@@ -259,24 +264,27 @@
         out[:, n * tile : (n + 1) * tile] = jnp.dot(
             rows, held[n], preferred_element_type=jnp.float32
         ).astype(out.dtype)
-
-
-def project_own(left, weight, tile=512):
+    for copy in copies[count:]:
+        copy.wait()
+
+
+def project_own(left, weight, pieces=(), tile=512):
     rows, depth = left.shape
     width = weight.shape[1]
+    shapes = [(rows, width)] + [piece.shape for piece in pieces]
     return pl.pallas_call(
-        functools.partial(project_own_kernel, tile),
-        out_shape=jax.ShapeDtypeStruct((rows, width), jnp.bfloat16),
-        in_specs=[VMEM, HBM],
-        out_specs=VMEM,
+        functools.partial(project_own_kernel, tile, len(pieces)),
+        out_shape=[jax.ShapeDtypeStruct(shape, jnp.bfloat16) for shape in shapes],
+        in_specs=[VMEM, HBM] + [ANY] * len(pieces),
+        out_specs=[VMEM] * len(shapes),
         scratch_shapes=[
             pltpu.VMEM((width // tile, depth, tile), jnp.bfloat16),
-            pltpu.SemaphoreType.DMA((width // tile,)),
+            pltpu.SemaphoreType.DMA((width // tile + len(pieces),)),
         ],
-        compiler_params=pltpu.CompilerParams(vmem_limit_bytes=8 * 2**20),
+        compiler_params=pltpu.CompilerParams(vmem_limit_bytes=12 * 2**20),
         cost_estimate=SMALL,
         name="project_own",
-    )(left, *in_hbm([weight]))
+    )(left, *in_hbm([weight, *pieces]))
 
 
 def columns_at(starts, counts, n, width):
@@ -369,7 +377,7 @@
     meta = ranks(block_order, jnp.int32(0), me, jnp.arange(axes["ctx"], dtype=jnp.int32), 1)
     first, second = attend(meta, query, tangent_query, [gathered])
     left = jnp.concatenate([first[:run], second[:run], first[run:], second[run:]], axis=0)
-    partial = project_own(left, out_weight)
+    (partial,) = project_own(left, out_weight)
     both = jnp.concatenate([partial[: 2 * run], partial[2 * run :]], axis=1)
     summed = lax.psum_scatter(both, "head", scatter_dimension=0, tiled=True)
     width = out_weight.shape[1]
@@ -473,9 +481,9 @@
     theirs, mine = finish(metas[2], query, tangent_query, [x3, cx3], state)
 
     other = cross(theirs)
-    partial, level_part, column_part, direct = tie(
-        (project_own(mine, out_weight), level_part, column_part, direct)
-    )
+    held = project_own(mine, out_weight, [shared, shared_core])
+    held, level_part, column_part, direct = tie((held, level_part, column_part, direct))
+    partial, shared, shared_core = held
     far = [swap(p, 1) for p in (direct, level_part, column_part)]
     near = [
         [by_level(level, core), by_column(column, core)],
@@ -485,7 +493,7 @@
         [by_core(core)],
     ]
     sums = project_other(
-        near, other, partial, [shared, shared_core], [level_part, column_part, direct]
+        near, other, partial, [], [shared, shared_core, level_part, column_part, direct]
     )
     rest = [[by_core(1 - core)], [by_level(1 - level, 1 - core)], [by_column(1 - column, 1 - core)]]
     return tuple(project_other(near + rest, other, partial, [], far, sums))

time: 55.8 us -> 54.6 us (0.978)
  waiting for transfers between devices: 9.04 us -> 8.35 us
    pallas_call x2, Pallas kernels: 5.31 us -> 4.12 us  [project_other(): pl.pallas_call(functools.partial(project_other_kernel, counts, len(early)...]
    ppermute x21, waiting for transfers between devices: 3.14 us -> 2.47 us  [swap(): return lax.ppermute(array, 'ctx', [(i, i ^ bits) for i in range(count)])]
    pallas_call x2, Pallas kernels: 8.77 us -> 9.41 us  [attend(): pl.pallas_call(functools.partial(attend_kernel, sizes), out_shape=outs, i...]
  transfers between devices with their start and end apart: 24 -> 24, of which waited for: 5 -> 5; matrix products, arithmetic and copies ran while one was open for 6% -> 7% of each run, Pallas kernels for 34% -> 33%
where the time goes in v5:
time: 54.6 us; the launch traced here: 54.3 us
  Pallas kernels  22.1 us (40%)
  starting transfers between devices  19.1 us (35%)
  waiting for transfers between devices  8.35 us (15%)
  local copies, waits for them, and re-layouts  2.29 us (4%)
  other arithmetic  1.43 us (3%)
  between operations  0.96 us (2%)
    ppermute x21, starting transfers between devices, swap(): return lax.ppermute(array, 'ctx', [(i, i ^ bits) for i in range(count)])  15.3 us
    pallas_call x2, Pallas kernels, attend(): pl.pallas_call(functools.partial(attend_kernel, sizes), out_shape=outs, i...  9.41 us
    ppermute x3, waiting for transfers between devices, cross(): return lax.ppermute(array, 'head', [(0, 1), (1, 0)])  5.88 us
    pallas_call x2, Pallas kernels, project_other(): pl.pallas_call(functools.partial(project_other_kernel, counts, len(early)...  4.12 us
    ppermute x3, starting transfers between devices, cross(): return lax.ppermute(array, 'head', [(0, 1), (1, 0)])  3.81 us
    pallas_call x1, Pallas kernels, project_own(): pl.pallas_call(functools.partial(project_own_kernel, tile, len(pieces)),...  3.29 us
    pallas_call x2, Pallas kernels, stage(): pl.pallas_call(functools.partial(stage_kernel, widths, len(fields)), out_...  2.98 us
    ppermute x21, waiting for transfers between devices, swap(): return lax.ppermute(array, 'ctx', [(i, i ^ bits) for i in range(count)])  2.47 us
  transfers between devices with their start and end apart: 24, of which 5 were waited for; matrix products, arithmetic and copies ran while one was open for 7% of the time, Pallas kernels for 33%

profile of v5, /device:TPU:0, one launch (start us, length us, event | category | flops | bytes accessed | tf_op | source)
XLA Modules:
  0.0 54.3 jit_solution(10757502991786188439)
XLA Ops:
  0.6 0.0 copy-start.10
  0.6 0.0 copy-start.9
  0.7 0.0 copy-start.8
  0.7 0.1 pad_add_fusion.3.starts
  0.8 1.7 %stage.2 = (bf16[192,512]{1,0:T(8,128)(2,1)S(1)}, bf16[512,512]{1,0:T(8,128)(2,1)S(1)}) custom-call(s32[2]{0:T(128)S(1)} %pad_add_fusion.3.starts, bf16[512,4096]{1,0:T(8,128)(2,1)} %weight.5, bf16[192,128]{1,0:T(8,128)(2,1)} %refs_0_.1, bf16[192,128]{1,0:T(8,128)(2,1)} %refs_1_.1, bf16[192,128]{1,0:T(8,128)(2,1)} %refs_2_.1, bf16[192,128]{1,0:T(8,128)(2,1)} %refs_3_.1), custom_call_target="tpu_custom_call" | custom-call | flops 1 | bytes 1 | tf_op jit(solution)/shard_map/stage/pallas_call | solution.py:408
  2.5 4.1 %collective-permute-start.4 = (bf16[192,512]{1,0:T(8,128)(2,1)S(1)}, bf16[192,512]{1,0:T(8,128)(2,1)}, u32[]{:S(2)}, u32[]{:S(2)}) collective-permute-start(bf16[192,512]{1,0:T(8,128)(2,1)S(1)} %get-tuple-element.76.refs_0_), channel_id=1, source_target_pairs={{0,16},{2,18},{4,20},{6,22},{8,24},{10,26},{12,28},{14,30},{16,0},... | collective-permute-start | bytes 589832 | tf_op jit(solution)/shard_map/ppermute | solution.py:431
  6.6 1.6 %collective-permute-start.3 = (bf16[192,512]{1,0:T(8,128)(2,1)S(1)}, bf16[192,512]{1,0:T(8,128)(2,1)}, u32[]{:S(2)}, u32[]{:S(2)}) collective-permute-start(bf16[192,512]{1,0:T(8,128)(2,1)S(1)} %get-tuple-element.76.refs_0_), channel_id=1, source_target_pairs={{0,8},{2,10},{4,12},{6,14},{8,0},{10,2},{12,4},{14,6},{16,24},{18,... | collective-permute-start | bytes 589832 | tf_op jit(solution)/shard_map/ppermute | solution.py:431
  8.2 1.5 %collective-permute-start = (bf16[192,512]{1,0:T(8,128)(2,1)S(1)}, bf16[192,512]{1,0:T(8,128)(2,1)S(1)}, u32[]{:S(2)}, u32[]{:S(2)}) collective-permute-start(bf16[192,512]{1,0:T(8,128)(2,1)S(1)} %get-tuple-element.76.refs_0_), channel_id=1, source_target_pairs={{0,4},{2,6},{4,0},{6,2},{8,12},{10,14},{12,8},{14,10},{16,20},{18,... | collective-permute-start | bytes 589832 | tf_op jit(solution)/shard_map/ppermute | solution.py:431
  9.7 1.5 %collective-permute-start.10 = (bf16[512,512]{1,0:T(8,128)(2,1)S(1)}, bf16[512,512]{1,0:T(8,128)(2,1)S(1)}, u32[]{:S(2)}, u32[]{:S(2)}) collective-permute-start(bf16[512,512]{1,0:T(8,128)(2,1)S(1)} %get-tuple-element.74), channel_id=1, source_target_pairs={{0,1},{1,0},{2,3},{3,2},{4,5},{5,4},{6,7},{7,6},{8,9},{9,8},{10,11... | collective-permute-start | bytes 1572872 | tf_op jit(solution)/shard_map/ppermute | solution.py:434
  11.2 0.1 reshape.16
  11.3 0.1 dynamic_slice.2
  11.4 0.0 copy-done.9
  11.4 0.6 %gather_fusion.1 = s32[8,2]{1,0:T(8,128)S(1)} fusion(s32[16,2]{1,0:T(8,128)S(1)} %reshape.16, s32[1024]{0:T(1024)S(1)} %pad_clamp_fusion.1), kind=kCustom, calls=%fused_computation.1 | custom fusion | bytes 160 | tf_op jit(solution)/shard_map/gather | solution.py:211
  12.0 0.6 %gather_fusion = s32[6,2]{1,0:T(8,128)S(1)} fusion(s32[16,2]{1,0:T(8,128)S(1)} %reshape.16, s32[1024]{0:T(1024)S(1)} %pad_clamp_fusion.2), kind=kCustom, calls=%fused_computation | custom fusion | bytes 120 | tf_op jit(solution)/shard_map/gather | solution.py:211
  12.6 0.1 lt.99
  12.6 0.1 lt.108
  12.7 0.2 convert_reduce_fusion
  12.9 0.2 fusion.1
  13.1 0.2 convert_reduce_fusion.1
  13.3 0.2 fusion
  13.5 0.6 %gather_fusion.2 = s32[2,2]{1,0:T(2,128)S(1)} fusion(s32[16,2]{1,0:T(8,128)S(1)} %reshape.16, s32[1024]{0:T(1024)S(1)} %pad_clamp_fusion), kind=kCustom, calls=%fused_computation.2 | custom fusion | bytes 40 | tf_op jit(solution)/shard_map/gather | solution.py:211
  14.1 0.1 lt.116
  14.1 0.2 fusion.2
  14.3 1.2 %stage.3 = bf16[512,1024]{1,0:T(8,128)(2,1)S(1)} custom-call(s32[1]{0:T(128)} %bitcast.6.starts, bf16[512,4096]{1,0:T(8,128)(2,1)} %weight.5), custom_call_target="tpu_custom_call" | custom-call | flops 1 | bytes 1 | tf_op jit(solution)/shard_map/stage/pallas_call | solution.py:408
  15.6 0.1 pad_add_fusion.1.meta
  15.6 0.2 convert_reduce_fusion.2
  15.8 0.1 collective-permute-start.1
  15.9 0.5 collective-permute-start.2
  16.4 0.1 pad_add_fusion.2.meta
  16.5 0.1 pad_add_fusion.meta
  16.6 0.0 collective-permute-done.4.refs_4_
  16.6 0.0 collective-permute-done.3.refs_3_
  16.6 0.8 %collective-permute-done.1.refs_1_ = bf16[192,512]{1,0:T(8,128)(2,1)S(1)} collective-permute-done((bf16[192,512]{1,0:T(8,128)(2,1)S(1)}, bf16[192,512]{1,0:T(8,128)(2,1)S(1)}, u32[]{:S(2)}, u32[]{:S(2)}) %collective-permute-start.1) | collective-permute-done | bytes 196640 | tf_op jit(solution)/shard_map/ppermute | solution.py:431
  17.4 0.3 collective-permute-done.2.refs_5_
  17.6 0.2 collective-permute-start.8
  17.9 0.5 collective-permute-start.5
  18.4 0.0 collective-permute-start.9
  18.4 1.1 %collective-permute-start.7 = (bf16[192,512]{1,0:T(8,128)(2,1)}, bf16[192,512]{1,0:T(8,128)(2,1)S(1)}, u32[]{:S(2)}, u32[]{:S(2)}) collective-permute-start(bf16[192,512]{1,0:T(8,128)(2,1)} %collective-permute-done.4.refs_4_), channel_id=1, source_target_pairs={{0,8},{2,10},{4,12},{6,14},{8,0},{10,2},{12,4},{14,6},{16,24},{18,... | collective-permute-start | bytes 589832 | tf_op jit(solution)/shard_map/ppermute | solution.py:431
  19.5 3.1 %collective-permute-done.10.refs_6_.refs_0_ = bf16[512,512]{1,0:T(8,128)(2,1)S(1)} collective-permute-done((bf16[512,512]{1,0:T(8,128)(2,1)S(1)}, bf16[512,512]{1,0:T(8,128)(2,1)S(1)}, u32[]{:S(2)}, u32[]{:S(2)}) %collective-permute-start.10) | collective-permute-done | bytes 524320 | tf_op jit(solution)/shard_map/ppermute | solution.py:434
  22.5 0.5 collective-permute-start.6
  23.1 1.5 %collective-permute-start.20 = (bf16[512,1024]{1,0:T(8,128)(2,1)S(1)}, bf16[512,1024]{1,0:T(8,128)(2,1)S(1)}, u32[]{:S(2)}, u32[]{:S(2)}) collective-permute-start(bf16[512,1024]{1,0:T(8,128)(2,1)S(1)} %stage.3), channel_id=1, source_target_pairs={{0,1},{1,0},{2,3},{3,2},{4,5},{5,4},{6,7},{7,6},{8,9},{9,8},{10,11... | collective-permute-start | bytes 3145736 | tf_op jit(solution)/shard_map/ppermute | solution.py:434
  24.6 5.0 %attend_early.2 = (f32[768,128]{1,0:T(8,128)S(1)}, f32[768,128]{1,0:T(8,128)S(1)}, f32[768,128]{1,0:T(8,128)S(1)}, f32[768,256]{1,0:T(8,128)S(1)}, f32[768,128]{...) custom-call(s32[16]{0:T(128)S(1)} %pad_add_fusion.meta, bf16[192,512]{1,0:T(8,128)(2,1)S(1)} %copy-done.1, ...), custom_call_target="tpu_custom_call" | custom-call | flops 1 | bytes 1 | tf_op jit(solution)/shard_map/attend_early/pallas_call | solution.py:232
  29.7 0.0 collective-permute-done.5.refs_0_
  29.7 0.1 collective-permute-start.12
  29.8 0.5 collective-permute-start.14
  30.3 0.1 collective-permute-start.13
  30.4 1.5 %collective-permute-start.11 = (bf16[192,512]{1,0:T(8,128)(2,1)S(1)}, bf16[192,512]{1,0:T(8,128)(2,1)S(1)}, u32[]{:S(2)}, u32[]{:S(2)}) collective-permute-start(bf16[192,512]{1,0:T(8,128)(2,1)S(1)} %collective-permute-done.7.refs_1_), channel_id=1, source_target_pairs={{0,4},{2,6},{4,0},{6,2},{8,12},{10,14},{12,8},{14,10},{16,20},{18,... | collective-permute-start | bytes 589832 | tf_op jit(solution)/shard_map/ppermute | solution.py:431
  31.9 4.4 %attend_early.3 = (f32[768,128]{1,0:T(8,128)S(1)}, f32[768,128]{1,0:T(8,128)S(1)}, f32[768,128]{1,0:T(8,128)S(1)}, f32[768,256]{1,0:T(8,128)S(1)}, f32[768,128]{1,0:T(8,128)S(1)}) custom-call(s32[20]{0:T(128)S(1)} %pad_add_fusion.1.meta, bf16[192,512]{1,0:T(8,128)(2,1)S(1)} %copy-done.1, bf16[192,512]{1,0:T(8,128)(2,1)S(1)} %copy-done.2, ...), custom_call_target="tpu_custom_call" | custom-call | flops 1 | bytes 1 | tf_op jit(solution)/shard_map/attend_early/pallas_call | solution.py:232
  36.2 1.4 %collective-permute-done.11.refs_0_ = bf16[192,512]{1,0:T(8,128)(2,1)S(1)} collective-permute-done((bf16[192,512]{1,0:T(8,128)(2,1)S(1)}, bf16[192,512]{1,0:T(8,128)(2,1)S(1)}, u32[]{:S(2)}, u32[]{:S(2)}) %collective-permute-start.11) | collective-permute-done | bytes 196640 | tf_op jit(solution)/shard_map/ppermute | solution.py:431
  37.6 0.5 collective-permute-start.15
  38.1 0.4 collective-permute-start.18
  38.6 1.5 %collective-permute-start.19 = (bf16[512,256]{1,0:T(8,128)(2,1)S(1)}, bf16[512,256]{1,0:T(8,128)(2,1)}, u32[]{:S(2)}, u32[]{:S(2)}) collective-permute-start(bf16[512,256]{1,0:T(8,128)(2,1)S(1)} %get-tuple-element.121), channel_id=1, source_target_pairs={{0,4},{2,6},{4,0},{6,2},{8,12},{10,14},{12,8},{14,10},{16,20},{18,... | collective-permute-start | bytes 786440 | tf_op jit(solution)/shard_map/ppermute | solution.py:431
  40.1 2.3 %finish.1 = (bf16[192,512]{1,0:T(8,128)(2,1)}, bf16[192,512]{1,0:T(8,128)(2,1)S(1)}) custom-call(s32[8]{0:T(128)S(1)} %pad_add_fusion.2.meta, bf16[192,512]{1,0:T(8,128)(2,1)S(1)} %copy-done.1, bf16[192,512]{1,0:T(8,128)(2,1)S(1)} %copy-done.2, bf16[192,512]{1,0:T(8,128)(2,1)S(1)} %collective-permute-done.11.refs_0_, ...), custom_call_target="tpu_custom_call" | custom-call | flops 1 | bytes 1 | tf_op jit(solution)/shard_map/finish/pallas_call | solution.py:198
  42.4 0.8 %collective-permute-start.17 = (bf16[192,512]{1,0:T(8,128)(2,1)}, bf16[192,512]{1,0:T(8,128)(2,1)S(1)}, u32[]{:S(2)}, u32[]{:S(2)}) collective-permute-start(bf16[192,512]{1,0:T(8,128)(2,1)} %get-tuple-element.114), channel_id=1, source_target_pairs={{0,1},{1,0},{2,3},{3,2},{4,5},{5,4},{6,7},{7,6},{8,9},{9,8},{10,11... | collective-permute-start | bytes 589832 | tf_op jit(solution)/shard_map/ppermute | solution.py:434
  43.2 0.1 stack.67.starts
  43.3 0.1 stack.64.starts
  43.3 3.3 %project_own.1 = (bf16[192,4096]{1,0:T(8,128)(2,1)S(1)}, bf16[512,512]{1,0:T(8,128)(2,1)S(1)}, bf16[512,512]{1,0:T(8,128)(2,1)S(1)}) custom-call(bf16[192,512]{1,0:T(8,128)(2,1)S(1)} %get-tuple-element.115.left, bf16[512,4096]{1,0:T(8,128)(2,1)} %weight.5, bf16[512,512]{1,0:T(8,128)(2,1)} %copy-done, bf16[512,512]{1,0:T(8,128)(2,1)} %collective-permute-done.16.refs_1_), custom_call_target="tpu_custom_call" | custom-call | flops 1 | bytes 1 | tf_op jit(solution)/shard_map/project_own/pallas_call | solution.py:275
  46.6 0.0 collective-permute-done.18.refs_2_
  46.7 0.1 collective-permute-start.22
  46.8 0.5 collective-permute-start.23
  47.2 0.1 collective-permute-start.21
  47.3 2.8 %collective-permute-done.17.left = bf16[192,512]{1,0:T(8,128)(2,1)S(1)} collective-permute-done((bf16[192,512]{1,0:T(8,128)(2,1)}, bf16[192,512]{1,0:T(8,128)(2,1)S(1)}, u32[]{:S(2)}, u32[]{:S(2)}) %collective-permute-start.17) | collective-permute-done | bytes 196640 | tf_op jit(solution)/shard_map/ppermute | solution.py:434
  50.1 1.9 %project_other.1 = (bf16[192,512]{1,0:T(8,128)(2,1)S(1)}, bf16[192,512]{1,0:T(8,128)(2,1)S(1)}, bf16[192,256]{1,0:T(8,128)(2,1)S(1)}, bf16[192,256]{1,0:T(8,128)(2,1)S(1)}, bf16[192,1024]{1,0:T(8,128)(2,1)S(1)}) custom-call(s32[7]{0:T(128)S(1)} %stack.67.starts, bf16[192,512]{1,0:T(8,128)(2,1)S(1)} %collective-permute-done.17.left, ...), custom_call_target="tpu_custom_call" | custom-call | flops 99999997952 | bytes 1 | tf_op jit(solution)/shard_map/project_other/pallas_call | solution.py:356
  52.1 2.2 %project_last.1 = (bf16[96,4096]{1,0:T(8,128)(2,1)}, bf16[96,4096]{1,0:T(8,128)(2,1)}) custom-call(s32[10]{0:T(128)S(1)} %stack.64.starts, bf16[192,512]{1,0:T(8,128)(2,1)S(1)} %collective-permute-done.17.left, bf16[192,4096]{1,0:T(8,128)(2,1)S(1)} %get-tuple-element.123.partial, bf16[192,512]{1,0:T(8,128)(2,1)S(1)} %get-tuple-element.129.refs_0_, ...), custom_call_target="tpu_custom_call" | custom-call | flops 1 | bytes 1 | tf_op jit(solution)/shard_map/project_last/pallas_call | solution.py:356
  (40 shorter events, 0.1 us)
Async XLA Ops:
  0.6 10.8 %copy-start.10 = (s32[6]{0:T(128)S(1)}, s32[6]{0:T(128)}, u32[]{:S(2)}) copy-start(s32[6]{0:T(128)} %constant.12.clone) | copy-start | bytes 76
  0.6 10.8 %copy-start.9 = (s32[8]{0:T(128)S(1)}, s32[8]{0:T(128)}, u32[]{:S(2)}) copy-start(s32[8]{0:T(128)} %constant.13.clone) | copy-start | bytes 100
  0.7 12.8 %copy-start.8 = (s32[2]{0:T(128)S(1)}, s32[2]{0:T(128)}, u32[]{:S(2)}) copy-start(s32[2]{0:T(128)} %constant.14.clone) | copy-start | bytes 28
  0.7 10.6 %copy-start.7 = (s32[32]{0:T(128)S(1)}, s32[32]{0:T(128)}, u32[]{:S(2)}) copy-start(s32[32]{0:T(128)} %param.18) | copy-start | bytes 388
  0.8 23.8 %copy-start.1 = (bf16[192,512]{1,0:T(8,128)(2,1)S(1)}, bf16[192,512]{1,0:T(8,128)(2,1)}, u32[]{:S(2)}) copy-start(bf16[192,512]{1,0:T(8,128)(2,1)} %query.5) | copy-start | bytes 589828
  0.8 23.8 %copy-start.2 = (bf16[192,512]{1,0:T(8,128)(2,1)S(1)}, bf16[192,512]{1,0:T(8,128)(2,1)}, u32[]{:S(2)}) copy-start(bf16[192,512]{1,0:T(8,128)(2,1)} %tangent_query.5) | copy-start | bytes 589828
  2.5 22.1 %copy-start.3 = (bf16[192,512]{1,0:T(8,128)(2,1)}, bf16[192,512]{1,0:T(8,128)(2,1)S(1)}, u32[]{:S(2)}) copy-start(bf16[192,512]{1,0:T(8,128)(2,1)S(1)} %get-tuple-element.76.refs_0_) | copy-start | bytes 589828
  2.5 14.0 %collective-permute-start.4 = (bf16[192,512]{1,0:T(8,128)(2,1)S(1)}, bf16[192,512]{1,0:T(8,128)(2,1)}, u32[]{:S(2)}, u32[]{:S(2)}) collective-permute-start(bf16[192,512]{1,0:T(8,128)(2,1)S(1)} %get-tuple-element.76.refs_0_), channel_id=1, source_target_pairs={{0,16},{2,18},{4,20},{6,22},{8,24},{10,26},{12,28},{14,30},{16,0},... | collective-permute-start | bytes 589832 | tf_op jit(solution)/shard_map/ppermute | solution.py:431
  6.6 9.9 %collective-permute-start.3 = (bf16[192,512]{1,0:T(8,128)(2,1)S(1)}, bf16[192,512]{1,0:T(8,128)(2,1)}, u32[]{:S(2)}, u32[]{:S(2)}) collective-permute-start(bf16[192,512]{1,0:T(8,128)(2,1)S(1)} %get-tuple-element.76.refs_0_), channel_id=1, source_target_pairs={{0,8},{2,10},{4,12},{6,14},{8,0},{10,2},{12,4},{14,6},{16,24},{18,... | collective-permute-start | bytes 589832 | tf_op jit(solution)/shard_map/ppermute | solution.py:431
  8.2 7.6 %collective-permute-start = (bf16[192,512]{1,0:T(8,128)(2,1)S(1)}, bf16[192,512]{1,0:T(8,128)(2,1)S(1)}, u32[]{:S(2)}, u32[]{:S(2)}) collective-permute-start(bf16[192,512]{1,0:T(8,128)(2,1)S(1)} %get-tuple-element.76.refs_0_), channel_id=1, source_target_pairs={{0,4},{2,6},{4,0},{6,2},{8,12},{10,14},{12,8},{14,10},{16,20},{18,... | collective-permute-start | bytes 589832 | tf_op jit(solution)/shard_map/ppermute | solution.py:431
  9.7 12.8 %collective-permute-start.10 = (bf16[512,512]{1,0:T(8,128)(2,1)S(1)}, bf16[512,512]{1,0:T(8,128)(2,1)S(1)}, u32[]{:S(2)}, u32[]{:S(2)}) collective-permute-start(bf16[512,512]{1,0:T(8,128)(2,1)S(1)} %get-tuple-element.74), channel_id=1, source_target_pairs={{0,1},{1,0},{2,3},{3,2},{4,5},{5,4},{6,7},{7,6},{8,9},{9,8},{10,11... | collective-permute-start | bytes 1572872 | tf_op jit(solution)/shard_map/ppermute | solution.py:434
  15.8 7.2 %copy-start.4 = (bf16[192,512]{1,0:T(8,128)(2,1)}, bf16[192,512]{1,0:T(8,128)(2,1)S(1)}, u32[]{:S(2)}) copy-start(bf16[192,512]{1,0:T(8,128)(2,1)S(1)} %collective-permute-done.refs_2_) | copy-start | bytes 589828
  15.8 1.5 %collective-permute-start.1 = (bf16[192,512]{1,0:T(8,128)(2,1)S(1)}, bf16[192,512]{1,0:T(8,128)(2,1)S(1)}, u32[]{:S(2)}, u32[]{:S(2)}) collective-permute-start(bf16[192,512]{1,0:T(8,128)(2,1)S(1)} %get-tuple-element.76.refs_0_), channel_id=1, source_target_pairs={{0,2},{2,0},{4,6},{6,4},{8,10},{10,8},{12,14},{14,12},{16,18},{18,... | collective-permute-start | bytes 589832 | tf_op jit(solution)/shard_map/ppermute | solution.py:431
  15.9 1.7 %collective-permute-start.2 = (bf16[192,512]{1,0:T(8,128)(2,1)S(1)}, bf16[192,512]{1,0:T(8,128)(2,1)S(1)}, u32[]{:S(2)}, u32[]{:S(2)}) collective-permute-start(bf16[192,512]{1,0:T(8,128)(2,1)S(1)} %collective-permute-done.refs_2_), channel_id=1, source_target_pairs={{0,2},{2,0},{4,6},{6,4},{8,10},{10,8},{12,14},{14,12},{16,18},{18,... | collective-permute-start | bytes 589832 | tf_op jit(solution)/shard_map/ppermute | solution.py:431
  17.4 7.2 %copy-start.5 = (bf16[192,512]{1,0:T(8,128)(2,1)}, bf16[192,512]{1,0:T(8,128)(2,1)S(1)}, u32[]{:S(2)}) copy-start(bf16[192,512]{1,0:T(8,128)(2,1)S(1)} %collective-permute-done.1.refs_1_) | copy-start | bytes 589828
  17.6 7.0 %copy-start.6 = (bf16[192,512]{1,0:T(8,128)(2,1)}, bf16[192,512]{1,0:T(8,128)(2,1)S(1)}, u32[]{:S(2)}) copy-start(bf16[192,512]{1,0:T(8,128)(2,1)S(1)} %collective-permute-done.2.refs_5_) | copy-start | bytes 589828
  17.6 5.4 %collective-permute-start.8 = (bf16[192,512]{1,0:T(8,128)(2,1)}, bf16[192,512]{1,0:T(8,128)(2,1)S(1)}, u32[]{:S(2)}, u32[]{:S(2)}) collective-permute-start(bf16[192,512]{1,0:T(8,128)(2,1)} %collective-permute-done.3.refs_3_), channel_id=1, source_target_pairs={{0,2},{2,0},{4,6},{6,4},{8,10},{10,8},{12,14},{14,12},{16,18},{18,... | collective-permute-start | bytes 589832 | tf_op jit(solution)/shard_map/ppermute | solution.py:431
  17.9 11.8 %collective-permute-start.5 = (bf16[192,512]{1,0:T(8,128)(2,1)}, bf16[192,512]{1,0:T(8,128)(2,1)S(1)}, u32[]{:S(2)}, u32[]{:S(2)}) collective-permute-start(bf16[192,512]{1,0:T(8,128)(2,1)} %collective-permute-done.3.refs_3_), channel_id=1, source_target_pairs={{0,4},{2,6},{4,0},{6,2},{8,12},{10,14},{12,8},{14,10},{16,20},{18,... | collective-permute-start | bytes 589832 | tf_op jit(solution)/shard_map/ppermute | solution.py:431
  18.4 11.3 %collective-permute-start.9 = (bf16[192,512]{1,0:T(8,128)(2,1)}, bf16[192,512]{1,0:T(8,128)(2,1)S(1)}, u32[]{:S(2)}, u32[]{:S(2)}) collective-permute-start(bf16[192,512]{1,0:T(8,128)(2,1)} %collective-permute-done.4.refs_4_), channel_id=1, source_target_pairs={{0,2},{2,0},{4,6},{6,4},{8,10},{10,8},{12,14},{14,12},{16,18},{18,... | collective-permute-start | bytes 589832 | tf_op jit(solution)/shard_map/ppermute | solution.py:431
  18.4 11.3 %collective-permute-start.7 = (bf16[192,512]{1,0:T(8,128)(2,1)}, bf16[192,512]{1,0:T(8,128)(2,1)S(1)}, u32[]{:S(2)}, u32[]{:S(2)}) collective-permute-start(bf16[192,512]{1,0:T(8,128)(2,1)} %collective-permute-done.4.refs_4_), channel_id=1, source_target_pairs={{0,8},{2,10},{4,12},{6,14},{8,0},{10,2},{12,4},{14,6},{16,24},{18,... | collective-permute-start | bytes 589832 | tf_op jit(solution)/shard_map/ppermute | solution.py:431
  22.5 19.9 %copy-start = (bf16[512,512]{1,0:T(8,128)(2,1)}, bf16[512,512]{1,0:T(8,128)(2,1)S(1)}, u32[]{:S(2)}) copy-start(bf16[512,512]{1,0:T(8,128)(2,1)S(1)} %collective-permute-done.10.refs_6_.refs_0_) | copy-start | bytes 1572868
  22.5 7.2 %collective-permute-start.6 = (bf16[192,512]{1,0:T(8,128)(2,1)}, bf16[192,512]{1,0:T(8,128)(2,1)S(1)}, u32[]{:S(2)}, u32[]{:S(2)}) collective-permute-start(bf16[192,512]{1,0:T(8,128)(2,1)} %collective-permute-done.4.refs_4_), channel_id=1, source_target_pairs={{0,4},{2,6},{4,0},{6,2},{8,12},{10,14},{12,8},{14,10},{16,20},{18,... | collective-permute-start | bytes 589832 | tf_op jit(solution)/shard_map/ppermute | solution.py:431
  23.1 23.6 %collective-permute-start.20 = (bf16[512,1024]{1,0:T(8,128)(2,1)S(1)}, bf16[512,1024]{1,0:T(8,128)(2,1)S(1)}, u32[]{:S(2)}, u32[]{:S(2)}) collective-permute-start(bf16[512,1024]{1,0:T(8,128)(2,1)S(1)} %stage.3), channel_id=1, source_target_pairs={{0,1},{1,0},{2,3},{3,2},{4,5},{5,4},{6,7},{7,6},{8,9},{9,8},{10,11... | collective-permute-start | bytes 3145736 | tf_op jit(solution)/shard_map/ppermute | solution.py:434
  29.7 2.2 %collective-permute-start.12 = (bf16[192,512]{1,0:T(8,128)(2,1)S(1)}, bf16[192,512]{1,0:T(8,128)(2,1)S(1)}, u32[]{:S(2)}, u32[]{:S(2)}) collective-permute-start(bf16[192,512]{1,0:T(8,128)(2,1)S(1)} %collective-permute-done.5.refs_0_), channel_id=1, source_target_pairs={{0,2},{2,0},{4,6},{6,4},{8,10},{10,8},{12,14},{14,12},{16,18},{18,... | collective-permute-start | bytes 589832 | tf_op jit(solution)/shard_map/ppermute | solution.py:431
  29.8 2.1 %collective-permute-start.14 = (bf16[192,512]{1,0:T(8,128)(2,1)S(1)}, bf16[192,512]{1,0:T(8,128)(2,1)S(1)}, u32[]{:S(2)}, u32[]{:S(2)}) collective-permute-start(bf16[192,512]{1,0:T(8,128)(2,1)S(1)} %collective-permute-done.6.refs_2_), channel_id=1, source_target_pairs={{0,2},{2,0},{4,6},{6,4},{8,10},{10,8},{12,14},{14,12},{16,18},{18,... | collective-permute-start | bytes 589832 | tf_op jit(solution)/shard_map/ppermute | solution.py:431
  30.3 1.6 %collective-permute-start.13 = (bf16[192,512]{1,0:T(8,128)(2,1)S(1)}, bf16[192,512]{1,0:T(8,128)(2,1)S(1)}, u32[]{:S(2)}, u32[]{:S(2)}) collective-permute-start(bf16[192,512]{1,0:T(8,128)(2,1)S(1)} %collective-permute-done.7.refs_1_), channel_id=1, source_target_pairs={{0,2},{2,0},{4,6},{6,4},{8,10},{10,8},{12,14},{14,12},{16,18},{18,... | collective-permute-start | bytes 589832 | tf_op jit(solution)/shard_map/ppermute | solution.py:431
  30.4 7.3 %collective-permute-start.11 = (bf16[192,512]{1,0:T(8,128)(2,1)S(1)}, bf16[192,512]{1,0:T(8,128)(2,1)S(1)}, u32[]{:S(2)}, u32[]{:S(2)}) collective-permute-start(bf16[192,512]{1,0:T(8,128)(2,1)S(1)} %collective-permute-done.7.refs_1_), channel_id=1, source_target_pairs={{0,4},{2,6},{4,0},{6,2},{8,12},{10,14},{12,8},{14,10},{16,20},{18,... | collective-permute-start | bytes 589832 | tf_op jit(solution)/shard_map/ppermute | solution.py:431
  37.6 2.5 %collective-permute-start.16 = (bf16[512,512]{1,0:T(8,128)(2,1)S(1)}, bf16[512,512]{1,0:T(8,128)(2,1)}, u32[]{:S(2)}, u32[]{:S(2)}) collective-permute-start(bf16[512,512]{1,0:T(8,128)(2,1)S(1)} %collective-permute-done.10.refs_6_.refs_0_), channel_id=1, source_target_pairs={{0,2},{2,0},{4,6},{6,4},{8,10},{10,8},{12,14},{14,12},{16,18},{18,... | collective-permute-start | bytes 1572872 | tf_op jit(solution)/shard_map/ppermute | solution.py:431
  37.6 2.4 %collective-permute-start.15 = (bf16[192,512]{1,0:T(8,128)(2,1)S(1)}, bf16[192,512]{1,0:T(8,128)(2,1)S(1)}, u32[]{:S(2)}, u32[]{:S(2)}) collective-permute-start(bf16[192,512]{1,0:T(8,128)(2,1)S(1)} %collective-permute-done.11.refs_0_), channel_id=1, source_target_pairs={{0,2},{2,0},{4,6},{6,4},{8,10},{10,8},{12,14},{14,12},{16,18},{18,... | collective-permute-start | bytes 589832 | tf_op jit(solution)/shard_map/ppermute | solution.py:431
  38.1 8.5 %collective-permute-start.18 = (bf16[512,256]{1,0:T(8,128)(2,1)}, bf16[512,256]{1,0:T(8,128)(2,1)}, u32[]{:S(2)}, u32[]{:S(2)}) collective-permute-start(bf16[512,256]{1,0:T(8,128)(2,1)} %get-tuple-element.120), channel_id=1, source_target_pairs={{0,8},{2,10},{4,12},{6,14},{8,0},{10,2},{12,4},{14,6},{16,24},{18,... | collective-permute-start | bytes 786440 | tf_op jit(solution)/shard_map/ppermute | solution.py:431
  38.6 8.1 %collective-permute-start.19 = (bf16[512,256]{1,0:T(8,128)(2,1)S(1)}, bf16[512,256]{1,0:T(8,128)(2,1)}, u32[]{:S(2)}, u32[]{:S(2)}) collective-permute-start(bf16[512,256]{1,0:T(8,128)(2,1)S(1)} %get-tuple-element.121), channel_id=1, source_target_pairs={{0,4},{2,6},{4,0},{6,2},{8,12},{10,14},{12,8},{14,10},{16,20},{18,... | collective-permute-start | bytes 786440 | tf_op jit(solution)/shard_map/ppermute | solution.py:431
  42.4 7.7 %collective-permute-start.17 = (bf16[192,512]{1,0:T(8,128)(2,1)}, bf16[192,512]{1,0:T(8,128)(2,1)S(1)}, u32[]{:S(2)}, u32[]{:S(2)}) collective-permute-start(bf16[192,512]{1,0:T(8,128)(2,1)} %get-tuple-element.114), channel_id=1, source_target_pairs={{0,1},{1,0},{2,3},{3,2},{4,5},{5,4},{6,7},{7,6},{8,9},{9,8},{10,11... | collective-permute-start | bytes 589832 | tf_op jit(solution)/shard_map/ppermute | solution.py:434
  46.7 5.4 %collective-permute-start.22 = (bf16[512,256]{1,0:T(8,128)(2,1)}, bf16[512,256]{1,0:T(8,128)(2,1)S(1)}, u32[]{:S(2)}, u32[]{:S(2)}) collective-permute-start(bf16[512,256]{1,0:T(8,128)(2,1)} %collective-permute-done.18.refs_2_), channel_id=1, source_target_pairs={{0,2},{2,0},{4,6},{6,4},{8,10},{10,8},{12,14},{14,12},{16,18},{18,... | collective-permute-start | bytes 786440 | tf_op jit(solution)/shard_map/ppermute | solution.py:431
  46.8 5.3 %collective-permute-start.23 = (bf16[512,256]{1,0:T(8,128)(2,1)}, bf16[512,256]{1,0:T(8,128)(2,1)S(1)}, u32[]{:S(2)}, u32[]{:S(2)}) collective-permute-start(bf16[512,256]{1,0:T(8,128)(2,1)} %collective-permute-done.19.refs_3_), channel_id=1, source_target_pairs={{0,2},{2,0},{4,6},{6,4},{8,10},{10,8},{12,14},{14,12},{16,18},{18,... | collective-permute-start | bytes 786440 | tf_op jit(solution)/shard_map/ppermute | solution.py:431
  47.2 4.8 %collective-permute-start.21 = (bf16[512,1024]{1,0:T(8,128)(2,1)S(1)}, bf16[512,1024]{1,0:T(8,128)(2,1)S(1)}, u32[]{:S(2)}, u32[]{:S(2)}) collective-permute-start(bf16[512,1024]{1,0:T(8,128)(2,1)S(1)} %collective-permute-done.20.refs_4_), channel_id=1, source_target_pairs={{0,2},{2,0},{4,6},{6,4},{8,10},{10,8},{12,14},{14,12},{16,18},{18,... | collective-permute-start | bytes 3145736 | tf_op jit(solution)/shard_map/ppermute | solution.py:431

commit v6 on v5

--- a/solution.py
+++ b/solution.py
@@ -149,44 +149,45 @@
         place = pl.ds(pl.multiple_of(meta[4 + n] * run, run), run)
         line[place, :] = ref[begin : begin + run, :]
     chunk = line.shape[0]
+    qs, tqs, aheads = [], [], []
+    for step in range(2):
+        half = meta[0] if step == 0 else 1 - meta[0]
+        rows = pl.ds(pl.multiple_of(half * run, run), run)
+        aheads.append(meta[2 + half])
+        qs += [query[rows, h * HD : (h + 1) * HD] for h in range(group)]
+        tqs += [tangent_query[rows, h * HD : (h + 1) * HD] for h in range(group)]
+    q = jnp.concatenate(qs, axis=0)
+    tq_q = jnp.concatenate([jnp.concatenate(tqs, axis=0), q], axis=1)
+    scores = lax.dot_general(q, line[:, 0:HD], NT, preferred_element_type=jnp.float32)
+    slopes = lax.dot_general(tq_q, line[:, 0 : 2 * HD], NT, preferred_element_type=jnp.float32)
+    col = lax.broadcasted_iota(jnp.int32, (2 * height, chunk), 1)
+    row = lax.broadcasted_iota(jnp.int32, (2 * height, chunk), 0)
+    limit = jnp.where(row < height, aheads[0] * run, aheads[1] * run)
+    scores = jnp.where(col < limit, scores * (scale * LOG2E), LOWEST)
+    old, total, shift, both, mixed = (ref[...] for ref in before)
+    new = jnp.maximum(old, lanes(jnp.max(scores, axis=1, keepdims=True), HD))
+    factor = jnp.exp2(old - new)
+    weights = jnp.exp2(scores - jnp.tile(new, (1, chunk // HD)))
+    product = weights * slopes
+    total, shift = total * factor, shift * factor
+    for k in range(chunk // HD):
+        total = total + weights[:, k * HD : (k + 1) * HD]
+        shift = shift + product[:, k * HD : (k + 1) * HD]
+    weights_b, product_b = weights.astype(jnp.bfloat16), product.astype(jnp.bfloat16)
+    both = both * jnp.tile(factor, (1, 2)) + jnp.dot(
+        weights_b, line[:, 2 * HD : 4 * HD], preferred_element_type=jnp.float32
+    )
+    mixed = mixed * factor + jnp.dot(
+        product_b, line[:, 2 * HD : 3 * HD], preferred_element_type=jnp.float32
+    )
+    inverse = lanes(1.0 / jnp.sum(total, axis=1, keepdims=True), HD)
+    shifted = lanes(jnp.sum(shift, axis=1, keepdims=True), HD) * (scale * inverse)
+    context = both[:, 0:HD] * inverse
+    tangent = (mixed * scale + both[:, HD : 2 * HD]) * inverse - shifted * context
     for step, out in enumerate(outs):
-        half = meta[0] if step == 0 else 1 - meta[0]
-        mine = slice(step * height, (step + 1) * height)
-        rows = pl.ds(pl.multiple_of(half * run, run), run)
-        ahead = meta[2 + half]
-        q = [query[rows, h * HD : (h + 1) * HD] for h in range(group)]
-        tq = [tangent_query[rows, h * HD : (h + 1) * HD] for h in range(group)]
-        q = jnp.concatenate(q, axis=0)
-        tq_q = jnp.concatenate([jnp.concatenate(tq, axis=0), q], axis=1)
-        scores = lax.dot_general(q, line[:, 0:HD], NT, preferred_element_type=jnp.float32)
-        slopes = lax.dot_general(
-            tq_q, line[:, 0 : 2 * HD], NT, preferred_element_type=jnp.float32
-        )
-        col = lax.broadcasted_iota(jnp.int32, (height, chunk), 1)
-        scores = jnp.where(col < ahead * run, scores * (scale * LOG2E), LOWEST)
-        old, total, shift, both, mixed = (ref[mine, :] for ref in before)
-        new = jnp.maximum(old, lanes(jnp.max(scores, axis=1, keepdims=True), HD))
-        factor = jnp.exp2(old - new)
-        weights = jnp.exp2(scores - jnp.tile(new, (1, chunk // HD)))
-        product = weights * slopes
-        total, shift = total * factor, shift * factor
-        for k in range(chunk // HD):
-            total = total + weights[:, k * HD : (k + 1) * HD]
-            shift = shift + product[:, k * HD : (k + 1) * HD]
-        weights_b, product_b = weights.astype(jnp.bfloat16), product.astype(jnp.bfloat16)
-        both = both * jnp.tile(factor, (1, 2)) + jnp.dot(
-            weights_b, line[:, 2 * HD : 4 * HD], preferred_element_type=jnp.float32
-        )
-        mixed = mixed * factor + jnp.dot(
-            product_b, line[:, 2 * HD : 3 * HD], preferred_element_type=jnp.float32
-        )
-        inverse = lanes(1.0 / jnp.sum(total, axis=1, keepdims=True), HD)
-        shifted = lanes(jnp.sum(shift, axis=1, keepdims=True), HD) * (scale * inverse)
-        context = both[:, 0:HD] * inverse
-        tangent = (mixed * scale + both[:, HD : 2 * HD]) * inverse - shifted * context
         for h in range(group):
             cols = slice(h * HD, (h + 1) * HD)
-            head = slice(h * run, (h + 1) * run)
+            head = slice(step * height + h * run, step * height + (h + 1) * run)
             out[0:run, cols] = context[head].astype(out.dtype)
             out[run : 2 * run, cols] = tangent[head].astype(out.dtype)
 

time: 54.6 us -> 54.6 us (level)
    pallas_call x2, Pallas kernels: 9.41 us -> 8.77 us  [attend(): pl.pallas_call(functools.partial(attend_kernel, sizes), out_shape=outs, i...]
    ppermute x21, waiting for transfers between devices: 2.47 us -> 3.09 us  [swap(): return lax.ppermute(array, 'ctx', [(i, i ^ bits) for i in range(count)])]
where the time goes in v6:
time: 54.6 us; the launch traced here: 54.3 us
  Pallas kernels  21.7 us (40%)
  starting transfers between devices  19.1 us (35%)
  waiting for transfers between devices  8.81 us (16%)
  local copies, waits for them, and re-layouts  2.29 us (4%)
  other arithmetic  1.43 us (3%)
  between operations  0.97 us (2%)
    ppermute x21, starting transfers between devices, swap(): return lax.ppermute(array, 'ctx', [(i, i ^ bits) for i in range(count)])  15.3 us
    pallas_call x2, Pallas kernels, attend(): pl.pallas_call(functools.partial(attend_kernel, sizes), out_shape=outs, i...  8.77 us
    ppermute x3, waiting for transfers between devices, cross(): return lax.ppermute(array, 'head', [(0, 1), (1, 0)])  5.71 us
    pallas_call x2, Pallas kernels, project_other(): pl.pallas_call(functools.partial(project_other_kernel, counts, len(early)...  4.12 us
    ppermute x3, starting transfers between devices, cross(): return lax.ppermute(array, 'head', [(0, 1), (1, 0)])  3.81 us
    pallas_call x1, Pallas kernels, project_own(): pl.pallas_call(functools.partial(project_own_kernel, tile, len(pieces)),...  3.29 us
    ppermute x21, waiting for transfers between devices, swap(): return lax.ppermute(array, 'ctx', [(i, i ^ bits) for i in range(count)])  3.09 us
    pallas_call x2, Pallas kernels, stage(): pl.pallas_call(functools.partial(stage_kernel, widths, len(fields)), out_...  2.98 us
  transfers between devices with their start and end apart: 24, of which 5 were waited for; matrix products, arithmetic and copies ran while one was open for 7% of the time, Pallas kernels for 33%

profile of v6, /device:TPU:0, one launch (start us, length us, event | category | flops | bytes accessed | tf_op | source)
XLA Modules:
  0.0 54.3 jit_solution(2163446870087481982)
XLA Ops:
  0.6 0.0 copy-start.10
  0.6 0.0 copy-start.9
  0.7 0.0 copy-start.8
  0.7 0.1 pad_add_fusion.3.starts
  0.8 1.7 %stage.2 = (bf16[192,512]{1,0:T(8,128)(2,1)S(1)}, bf16[512,512]{1,0:T(8,128)(2,1)S(1)}) custom-call(s32[2]{0:T(128)S(1)} %pad_add_fusion.3.starts, bf16[512,4096]{1,0:T(8,128)(2,1)} %weight.5, bf16[192,128]{1,0:T(8,128)(2,1)} %refs_0_.1, bf16[192,128]{1,0:T(8,128)(2,1)} %refs_1_.1, bf16[192,128]{1,0:T(8,128)(2,1)} %refs_2_.1, bf16[192,128]{1,0:T(8,128)(2,1)} %refs_3_.1), custom_call_target="tpu_custom_call" | custom-call | flops 1 | bytes 1 | tf_op jit(solution)/shard_map/stage/pallas_call | solution.py:409
  2.5 4.1 %collective-permute-start.4 = (bf16[192,512]{1,0:T(8,128)(2,1)S(1)}, bf16[192,512]{1,0:T(8,128)(2,1)}, u32[]{:S(2)}, u32[]{:S(2)}) collective-permute-start(bf16[192,512]{1,0:T(8,128)(2,1)S(1)} %get-tuple-element.76.refs_0_), channel_id=1, source_target_pairs={{0,16},{2,18},{4,20},{6,22},{8,24},{10,26},{12,28},{14,30},{16,0},... | collective-permute-start | bytes 589832 | tf_op jit(solution)/shard_map/ppermute | solution.py:432
  6.6 1.6 %collective-permute-start.3 = (bf16[192,512]{1,0:T(8,128)(2,1)S(1)}, bf16[192,512]{1,0:T(8,128)(2,1)}, u32[]{:S(2)}, u32[]{:S(2)}) collective-permute-start(bf16[192,512]{1,0:T(8,128)(2,1)S(1)} %get-tuple-element.76.refs_0_), channel_id=1, source_target_pairs={{0,8},{2,10},{4,12},{6,14},{8,0},{10,2},{12,4},{14,6},{16,24},{18,... | collective-permute-start | bytes 589832 | tf_op jit(solution)/shard_map/ppermute | solution.py:432
  8.2 1.5 %collective-permute-start = (bf16[192,512]{1,0:T(8,128)(2,1)S(1)}, bf16[192,512]{1,0:T(8,128)(2,1)S(1)}, u32[]{:S(2)}, u32[]{:S(2)}) collective-permute-start(bf16[192,512]{1,0:T(8,128)(2,1)S(1)} %get-tuple-element.76.refs_0_), channel_id=1, source_target_pairs={{0,4},{2,6},{4,0},{6,2},{8,12},{10,14},{12,8},{14,10},{16,20},{18,... | collective-permute-start | bytes 589832 | tf_op jit(solution)/shard_map/ppermute | solution.py:432
  9.7 1.5 %collective-permute-start.10 = (bf16[512,512]{1,0:T(8,128)(2,1)S(1)}, bf16[512,512]{1,0:T(8,128)(2,1)S(1)}, u32[]{:S(2)}, u32[]{:S(2)}) collective-permute-start(bf16[512,512]{1,0:T(8,128)(2,1)S(1)} %get-tuple-element.74), channel_id=1, source_target_pairs={{0,1},{1,0},{2,3},{3,2},{4,5},{5,4},{6,7},{7,6},{8,9},{9,8},{10,11... | collective-permute-start | bytes 1572872 | tf_op jit(solution)/shard_map/ppermute | solution.py:435
  11.2 0.1 reshape.16
  11.3 0.1 dynamic_slice.2
  11.4 0.0 copy-done.9
  11.4 0.6 %gather_fusion.1 = s32[8,2]{1,0:T(8,128)S(1)} fusion(s32[16,2]{1,0:T(8,128)S(1)} %reshape.16, s32[1024]{0:T(1024)S(1)} %pad_clamp_fusion.1), kind=kCustom, calls=%fused_computation.1 | custom fusion | bytes 160 | tf_op jit(solution)/shard_map/gather | solution.py:212
  12.0 0.6 %gather_fusion = s32[6,2]{1,0:T(8,128)S(1)} fusion(s32[16,2]{1,0:T(8,128)S(1)} %reshape.16, s32[1024]{0:T(1024)S(1)} %pad_clamp_fusion.2), kind=kCustom, calls=%fused_computation | custom fusion | bytes 120 | tf_op jit(solution)/shard_map/gather | solution.py:212
  12.6 0.1 lt.99
  12.6 0.1 lt.108
  12.7 0.2 convert_reduce_fusion
  12.9 0.2 fusion.1
  13.1 0.2 convert_reduce_fusion.1
  13.3 0.2 fusion
  13.5 0.6 %gather_fusion.2 = s32[2,2]{1,0:T(2,128)S(1)} fusion(s32[16,2]{1,0:T(8,128)S(1)} %reshape.16, s32[1024]{0:T(1024)S(1)} %pad_clamp_fusion), kind=kCustom, calls=%fused_computation.2 | custom fusion | bytes 40 | tf_op jit(solution)/shard_map/gather | solution.py:212
  14.1 0.1 lt.116
  14.1 0.2 fusion.2
  14.3 1.2 %stage.3 = bf16[512,1024]{1,0:T(8,128)(2,1)S(1)} custom-call(s32[1]{0:T(128)} %bitcast.6.starts, bf16[512,4096]{1,0:T(8,128)(2,1)} %weight.5), custom_call_target="tpu_custom_call" | custom-call | flops 1 | bytes 1 | tf_op jit(solution)/shard_map/stage/pallas_call | solution.py:409
  15.6 0.1 pad_add_fusion.1.meta
  15.6 0.2 convert_reduce_fusion.2
  15.8 0.1 collective-permute-start.1
  15.9 0.5 collective-permute-start.2
  16.4 0.1 pad_add_fusion.2.meta
  16.5 0.1 pad_add_fusion.meta
  16.6 0.0 collective-permute-done.4.refs_4_
  16.6 0.0 collective-permute-done.3.refs_3_
  16.6 0.8 %collective-permute-done.1.refs_1_ = bf16[192,512]{1,0:T(8,128)(2,1)S(1)} collective-permute-done((bf16[192,512]{1,0:T(8,128)(2,1)S(1)}, bf16[192,512]{1,0:T(8,128)(2,1)S(1)}, u32[]{:S(2)}, u32[]{:S(2)}) %collective-permute-start.1) | collective-permute-done | bytes 196640 | tf_op jit(solution)/shard_map/ppermute | solution.py:432
  17.4 0.3 collective-permute-done.2.refs_5_
  17.6 0.2 collective-permute-start.8
  17.9 0.5 collective-permute-start.5
  18.4 0.0 collective-permute-start.9
  18.4 1.1 %collective-permute-start.7 = (bf16[192,512]{1,0:T(8,128)(2,1)}, bf16[192,512]{1,0:T(8,128)(2,1)S(1)}, u32[]{:S(2)}, u32[]{:S(2)}) collective-permute-start(bf16[192,512]{1,0:T(8,128)(2,1)} %collective-permute-done.4.refs_4_), channel_id=1, source_target_pairs={{0,8},{2,10},{4,12},{6,14},{8,0},{10,2},{12,4},{14,6},{16,24},{18,... | collective-permute-start | bytes 589832 | tf_op jit(solution)/shard_map/ppermute | solution.py:432
  19.5 3.1 %collective-permute-done.10.refs_6_.refs_0_ = bf16[512,512]{1,0:T(8,128)(2,1)S(1)} collective-permute-done((bf16[512,512]{1,0:T(8,128)(2,1)S(1)}, bf16[512,512]{1,0:T(8,128)(2,1)S(1)}, u32[]{:S(2)}, u32[]{:S(2)}) %collective-permute-start.10) | collective-permute-done | bytes 524320 | tf_op jit(solution)/shard_map/ppermute | solution.py:435
  22.5 0.5 collective-permute-start.6
  23.1 1.5 %collective-permute-start.20 = (bf16[512,1024]{1,0:T(8,128)(2,1)S(1)}, bf16[512,1024]{1,0:T(8,128)(2,1)S(1)}, u32[]{:S(2)}, u32[]{:S(2)}) collective-permute-start(bf16[512,1024]{1,0:T(8,128)(2,1)S(1)} %stage.3), channel_id=1, source_target_pairs={{0,1},{1,0},{2,3},{3,2},{4,5},{5,4},{6,7},{7,6},{8,9},{9,8},{10,11... | collective-permute-start | bytes 3145736 | tf_op jit(solution)/shard_map/ppermute | solution.py:435
  24.6 5.0 %attend_early.2 = (f32[768,128]{1,0:T(8,128)S(1)}, f32[768,128]{1,0:T(8,128)S(1)}, f32[768,128]{1,0:T(8,128)S(1)}, f32[768,256]{1,0:T(8,128)S(1)}, f32[768,128]{...) custom-call(s32[16]{0:T(128)S(1)} %pad_add_fusion.meta, bf16[192,512]{1,0:T(8,128)(2,1)S(1)} %copy-done.1, ...), custom_call_target="tpu_custom_call" | custom-call | flops 1 | bytes 1 | tf_op jit(solution)/shard_map/attend_early/pallas_call | solution.py:233
  29.7 0.0 collective-permute-done.5.refs_0_
  29.7 0.0 collective-permute-done.9.refs_7_
  29.7 0.1 collective-permute-start.12
  29.8 0.5 collective-permute-start.14
  30.3 0.1 collective-permute-start.13
  30.4 1.5 %collective-permute-start.11 = (bf16[192,512]{1,0:T(8,128)(2,1)S(1)}, bf16[192,512]{1,0:T(8,128)(2,1)S(1)}, u32[]{:S(2)}, u32[]{:S(2)}) collective-permute-start(bf16[192,512]{1,0:T(8,128)(2,1)S(1)} %collective-permute-done.7.refs_1_), channel_id=1, source_target_pairs={{0,4},{2,6},{4,0},{6,2},{8,12},{10,14},{12,8},{14,10},{16,20},{18,... | collective-permute-start | bytes 589832 | tf_op jit(solution)/shard_map/ppermute | solution.py:432
  31.9 3.7 %attend_early.3 = (f32[768,128]{1,0:T(8,128)S(1)}, f32[768,128]{1,0:T(8,128)S(1)}, f32[768,128]{1,0:T(8,128)S(1)}, f32[768,256]{1,0:T(8,128)S(1)}, f32[768,128]{1,0:T(8,128)S(1)}) custom-call(s32[20]{0:T(128)S(1)} %pad_add_fusion.1.meta, bf16[192,512]{1,0:T(8,128)(2,1)S(1)} %copy-done.1, bf16[192,512]{1,0:T(8,128)(2,1)S(1)} %copy-done.2, ...), custom_call_target="tpu_custom_call" | custom-call | flops 1 | bytes 1 | tf_op jit(solution)/shard_map/attend_early/pallas_call | solution.py:233
  35.6 2.0 %collective-permute-done.11.refs_0_ = bf16[192,512]{1,0:T(8,128)(2,1)S(1)} collective-permute-done((bf16[192,512]{1,0:T(8,128)(2,1)S(1)}, bf16[192,512]{1,0:T(8,128)(2,1)S(1)}, u32[]{:S(2)}, u32[]{:S(2)}) %collective-permute-start.11) | collective-permute-done | bytes 196640 | tf_op jit(solution)/shard_map/ppermute | solution.py:432
  37.6 0.5 collective-permute-start.15
  38.1 0.4 collective-permute-start.18
  38.6 1.5 %collective-permute-start.19 = (bf16[512,256]{1,0:T(8,128)(2,1)S(1)}, bf16[512,256]{1,0:T(8,128)(2,1)}, u32[]{:S(2)}, u32[]{:S(2)}) collective-permute-start(bf16[512,256]{1,0:T(8,128)(2,1)S(1)} %get-tuple-element.121), channel_id=1, source_target_pairs={{0,4},{2,6},{4,0},{6,2},{8,12},{10,14},{12,8},{14,10},{16,20},{18,... | collective-permute-start | bytes 786440 | tf_op jit(solution)/shard_map/ppermute | solution.py:432
  40.1 2.5 %finish.1 = (bf16[192,512]{1,0:T(8,128)(2,1)}, bf16[192,512]{1,0:T(8,128)(2,1)S(1)}) custom-call(s32[8]{0:T(128)S(1)} %pad_add_fusion.2.meta, bf16[192,512]{1,0:T(8,128)(2,1)S(1)} %copy-done.1, bf16[192,512]{1,0:T(8,128)(2,1)S(1)} %copy-done.2, bf16[192,512]{1,0:T(8,128)(2,1)S(1)} %collective-permute-done.11.refs_0_, ...), custom_call_target="tpu_custom_call" | custom-call | flops 1 | bytes 1 | tf_op jit(solution)/shard_map/finish/pallas_call | solution.py:199
  42.6 0.8 %collective-permute-start.17 = (bf16[192,512]{1,0:T(8,128)(2,1)}, bf16[192,512]{1,0:T(8,128)(2,1)S(1)}, u32[]{:S(2)}, u32[]{:S(2)}) collective-permute-start(bf16[192,512]{1,0:T(8,128)(2,1)} %get-tuple-element.114), channel_id=1, source_target_pairs={{0,1},{1,0},{2,3},{3,2},{4,5},{5,4},{6,7},{7,6},{8,9},{9,8},{10,11... | collective-permute-start | bytes 589832 | tf_op jit(solution)/shard_map/ppermute | solution.py:435
  43.3 0.1 stack.67.starts
  43.4 0.1 stack.64.starts
  43.5 3.3 %project_own.1 = (bf16[192,4096]{1,0:T(8,128)(2,1)S(1)}, bf16[512,512]{1,0:T(8,128)(2,1)S(1)}, bf16[512,512]{1,0:T(8,128)(2,1)S(1)}) custom-call(bf16[192,512]{1,0:T(8,128)(2,1)S(1)} %get-tuple-element.115.left, bf16[512,4096]{1,0:T(8,128)(2,1)} %weight.5, bf16[512,512]{1,0:T(8,128)(2,1)} %copy-done, bf16[512,512]{1,0:T(8,128)(2,1)} %collective-permute-done.16.refs_1_), custom_call_target="tpu_custom_call" | custom-call | flops 1 | bytes 1 | tf_op jit(solution)/shard_map/project_own/pallas_call | solution.py:276
  46.8 0.1 collective-permute-start.22
  46.9 0.5 collective-permute-start.23
  47.4 0.1 collective-permute-start.21
  47.5 2.6 %collective-permute-done.17.left = bf16[192,512]{1,0:T(8,128)(2,1)S(1)} collective-permute-done((bf16[192,512]{1,0:T(8,128)(2,1)}, bf16[192,512]{1,0:T(8,128)(2,1)S(1)}, u32[]{:S(2)}, u32[]{:S(2)}) %collective-permute-start.17) | collective-permute-done | bytes 196640 | tf_op jit(solution)/shard_map/ppermute | solution.py:435
  50.1 1.9 %project_other.1 = (bf16[192,512]{1,0:T(8,128)(2,1)S(1)}, bf16[192,512]{1,0:T(8,128)(2,1)S(1)}, bf16[192,256]{1,0:T(8,128)(2,1)S(1)}, bf16[192,256]{1,0:T(8,128)(2,1)S(1)}, bf16[192,1024]{1,0:T(8,128)(2,1)S(1)}) custom-call(s32[7]{0:T(128)S(1)} %stack.67.starts, bf16[192,512]{1,0:T(8,128)(2,1)S(1)} %collective-permute-done.17.left, ...), custom_call_target="tpu_custom_call" | custom-call | flops 99999997952 | bytes 1 | tf_op jit(solution)/shard_map/project_other/pallas_call | solution.py:357
  52.1 2.2 %project_last.1 = (bf16[96,4096]{1,0:T(8,128)(2,1)}, bf16[96,4096]{1,0:T(8,128)(2,1)}) custom-call(s32[10]{0:T(128)S(1)} %stack.64.starts, bf16[192,512]{1,0:T(8,128)(2,1)S(1)} %collective-permute-done.17.left, bf16[192,4096]{1,0:T(8,128)(2,1)S(1)} %get-tuple-element.123.partial, bf16[192,512]{1,0:T(8,128)(2,1)S(1)} %get-tuple-element.129.refs_0_, ...), custom_call_target="tpu_custom_call" | custom-call | flops 1 | bytes 1 | tf_op jit(solution)/shard_map/project_last/pallas_call | solution.py:357
  (40 shorter events, 0.1 us)
Async XLA Ops:
  0.6 10.8 %copy-start.10 = (s32[6]{0:T(128)S(1)}, s32[6]{0:T(128)}, u32[]{:S(2)}) copy-start(s32[6]{0:T(128)} %constant.12.clone) | copy-start | bytes 76
  0.6 10.8 %copy-start.9 = (s32[8]{0:T(128)S(1)}, s32[8]{0:T(128)}, u32[]{:S(2)}) copy-start(s32[8]{0:T(128)} %constant.13.clone) | copy-start | bytes 100
  0.7 12.8 %copy-start.8 = (s32[2]{0:T(128)S(1)}, s32[2]{0:T(128)}, u32[]{:S(2)}) copy-start(s32[2]{0:T(128)} %constant.14.clone) | copy-start | bytes 28
  0.7 10.6 %copy-start.7 = (s32[32]{0:T(128)S(1)}, s32[32]{0:T(128)}, u32[]{:S(2)}) copy-start(s32[32]{0:T(128)} %param.18) | copy-start | bytes 388
  0.8 23.8 %copy-start.1 = (bf16[192,512]{1,0:T(8,128)(2,1)S(1)}, bf16[192,512]{1,0:T(8,128)(2,1)}, u32[]{:S(2)}) copy-start(bf16[192,512]{1,0:T(8,128)(2,1)} %query.5) | copy-start | bytes 589828
  0.8 23.8 %copy-start.2 = (bf16[192,512]{1,0:T(8,128)(2,1)S(1)}, bf16[192,512]{1,0:T(8,128)(2,1)}, u32[]{:S(2)}) copy-start(bf16[192,512]{1,0:T(8,128)(2,1)} %tangent_query.5) | copy-start | bytes 589828
  2.5 22.1 %copy-start.3 = (bf16[192,512]{1,0:T(8,128)(2,1)}, bf16[192,512]{1,0:T(8,128)(2,1)S(1)}, u32[]{:S(2)}) copy-start(bf16[192,512]{1,0:T(8,128)(2,1)S(1)} %get-tuple-element.76.refs_0_) | copy-start | bytes 589828
  2.5 14.0 %collective-permute-start.4 = (bf16[192,512]{1,0:T(8,128)(2,1)S(1)}, bf16[192,512]{1,0:T(8,128)(2,1)}, u32[]{:S(2)}, u32[]{:S(2)}) collective-permute-start(bf16[192,512]{1,0:T(8,128)(2,1)S(1)} %get-tuple-element.76.refs_0_), channel_id=1, source_target_pairs={{0,16},{2,18},{4,20},{6,22},{8,24},{10,26},{12,28},{14,30},{16,0},... | collective-permute-start | bytes 589832 | tf_op jit(solution)/shard_map/ppermute | solution.py:432
  6.6 9.9 %collective-permute-start.3 = (bf16[192,512]{1,0:T(8,128)(2,1)S(1)}, bf16[192,512]{1,0:T(8,128)(2,1)}, u32[]{:S(2)}, u32[]{:S(2)}) collective-permute-start(bf16[192,512]{1,0:T(8,128)(2,1)S(1)} %get-tuple-element.76.refs_0_), channel_id=1, source_target_pairs={{0,8},{2,10},{4,12},{6,14},{8,0},{10,2},{12,4},{14,6},{16,24},{18,... | collective-permute-start | bytes 589832 | tf_op jit(solution)/shard_map/ppermute | solution.py:432
  8.2 7.6 %collective-permute-start = (bf16[192,512]{1,0:T(8,128)(2,1)S(1)}, bf16[192,512]{1,0:T(8,128)(2,1)S(1)}, u32[]{:S(2)}, u32[]{:S(2)}) collective-permute-start(bf16[192,512]{1,0:T(8,128)(2,1)S(1)} %get-tuple-element.76.refs_0_), channel_id=1, source_target_pairs={{0,4},{2,6},{4,0},{6,2},{8,12},{10,14},{12,8},{14,10},{16,20},{18,... | collective-permute-start | bytes 589832 | tf_op jit(solution)/shard_map/ppermute | solution.py:432
  9.7 12.8 %collective-permute-start.10 = (bf16[512,512]{1,0:T(8,128)(2,1)S(1)}, bf16[512,512]{1,0:T(8,128)(2,1)S(1)}, u32[]{:S(2)}, u32[]{:S(2)}) collective-permute-start(bf16[512,512]{1,0:T(8,128)(2,1)S(1)} %get-tuple-element.74), channel_id=1, source_target_pairs={{0,1},{1,0},{2,3},{3,2},{4,5},{5,4},{6,7},{7,6},{8,9},{9,8},{10,11... | collective-permute-start | bytes 1572872 | tf_op jit(solution)/shard_map/ppermute | solution.py:435
  15.8 7.2 %copy-start.4 = (bf16[192,512]{1,0:T(8,128)(2,1)}, bf16[192,512]{1,0:T(8,128)(2,1)S(1)}, u32[]{:S(2)}) copy-start(bf16[192,512]{1,0:T(8,128)(2,1)S(1)} %collective-permute-done.refs_2_) | copy-start | bytes 589828
  15.8 1.5 %collective-permute-start.1 = (bf16[192,512]{1,0:T(8,128)(2,1)S(1)}, bf16[192,512]{1,0:T(8,128)(2,1)S(1)}, u32[]{:S(2)}, u32[]{:S(2)}) collective-permute-start(bf16[192,512]{1,0:T(8,128)(2,1)S(1)} %get-tuple-element.76.refs_0_), channel_id=1, source_target_pairs={{0,2},{2,0},{4,6},{6,4},{8,10},{10,8},{12,14},{14,12},{16,18},{18,... | collective-permute-start | bytes 589832 | tf_op jit(solution)/shard_map/ppermute | solution.py:432
  15.9 1.7 %collective-permute-start.2 = (bf16[192,512]{1,0:T(8,128)(2,1)S(1)}, bf16[192,512]{1,0:T(8,128)(2,1)S(1)}, u32[]{:S(2)}, u32[]{:S(2)}) collective-permute-start(bf16[192,512]{1,0:T(8,128)(2,1)S(1)} %collective-permute-done.refs_2_), channel_id=1, source_target_pairs={{0,2},{2,0},{4,6},{6,4},{8,10},{10,8},{12,14},{14,12},{16,18},{18,... | collective-permute-start | bytes 589832 | tf_op jit(solution)/shard_map/ppermute | solution.py:432
  17.4 7.2 %copy-start.5 = (bf16[192,512]{1,0:T(8,128)(2,1)}, bf16[192,512]{1,0:T(8,128)(2,1)S(1)}, u32[]{:S(2)}) copy-start(bf16[192,512]{1,0:T(8,128)(2,1)S(1)} %collective-permute-done.1.refs_1_) | copy-start | bytes 589828
  17.6 7.0 %copy-start.6 = (bf16[192,512]{1,0:T(8,128)(2,1)}, bf16[192,512]{1,0:T(8,128)(2,1)S(1)}, u32[]{:S(2)}) copy-start(bf16[192,512]{1,0:T(8,128)(2,1)S(1)} %collective-permute-done.2.refs_5_) | copy-start | bytes 589828
  17.6 5.4 %collective-permute-start.8 = (bf16[192,512]{1,0:T(8,128)(2,1)}, bf16[192,512]{1,0:T(8,128)(2,1)S(1)}, u32[]{:S(2)}, u32[]{:S(2)}) collective-permute-start(bf16[192,512]{1,0:T(8,128)(2,1)} %collective-permute-done.3.refs_3_), channel_id=1, source_target_pairs={{0,2},{2,0},{4,6},{6,4},{8,10},{10,8},{12,14},{14,12},{16,18},{18,... | collective-permute-start | bytes 589832 | tf_op jit(solution)/shard_map/ppermute | solution.py:432
  17.9 11.8 %collective-permute-start.5 = (bf16[192,512]{1,0:T(8,128)(2,1)}, bf16[192,512]{1,0:T(8,128)(2,1)S(1)}, u32[]{:S(2)}, u32[]{:S(2)}) collective-permute-start(bf16[192,512]{1,0:T(8,128)(2,1)} %collective-permute-done.3.refs_3_), channel_id=1, source_target_pairs={{0,4},{2,6},{4,0},{6,2},{8,12},{10,14},{12,8},{14,10},{16,20},{18,... | collective-permute-start | bytes 589832 | tf_op jit(solution)/shard_map/ppermute | solution.py:432
  18.4 11.3 %collective-permute-start.9 = (bf16[192,512]{1,0:T(8,128)(2,1)}, bf16[192,512]{1,0:T(8,128)(2,1)S(1)}, u32[]{:S(2)}, u32[]{:S(2)}) collective-permute-start(bf16[192,512]{1,0:T(8,128)(2,1)} %collective-permute-done.4.refs_4_), channel_id=1, source_target_pairs={{0,2},{2,0},{4,6},{6,4},{8,10},{10,8},{12,14},{14,12},{16,18},{18,... | collective-permute-start | bytes 589832 | tf_op jit(solution)/shard_map/ppermute | solution.py:432
  18.4 11.3 %collective-permute-start.7 = (bf16[192,512]{1,0:T(8,128)(2,1)}, bf16[192,512]{1,0:T(8,128)(2,1)S(1)}, u32[]{:S(2)}, u32[]{:S(2)}) collective-permute-start(bf16[192,512]{1,0:T(8,128)(2,1)} %collective-permute-done.4.refs_4_), channel_id=1, source_target_pairs={{0,8},{2,10},{4,12},{6,14},{8,0},{10,2},{12,4},{14,6},{16,24},{18,... | collective-permute-start | bytes 589832 | tf_op jit(solution)/shard_map/ppermute | solution.py:432
  22.5 20.0 %copy-start = (bf16[512,512]{1,0:T(8,128)(2,1)}, bf16[512,512]{1,0:T(8,128)(2,1)S(1)}, u32[]{:S(2)}) copy-start(bf16[512,512]{1,0:T(8,128)(2,1)S(1)} %collective-permute-done.10.refs_6_.refs_0_) | copy-start | bytes 1572868
  22.5 7.2 %collective-permute-start.6 = (bf16[192,512]{1,0:T(8,128)(2,1)}, bf16[192,512]{1,0:T(8,128)(2,1)S(1)}, u32[]{:S(2)}, u32[]{:S(2)}) collective-permute-start(bf16[192,512]{1,0:T(8,128)(2,1)} %collective-permute-done.4.refs_4_), channel_id=1, source_target_pairs={{0,4},{2,6},{4,0},{6,2},{8,12},{10,14},{12,8},{14,10},{16,20},{18,... | collective-permute-start | bytes 589832 | tf_op jit(solution)/shard_map/ppermute | solution.py:432
  23.1 23.8 %collective-permute-start.20 = (bf16[512,1024]{1,0:T(8,128)(2,1)S(1)}, bf16[512,1024]{1,0:T(8,128)(2,1)S(1)}, u32[]{:S(2)}, u32[]{:S(2)}) collective-permute-start(bf16[512,1024]{1,0:T(8,128)(2,1)S(1)} %stage.3), channel_id=1, source_target_pairs={{0,1},{1,0},{2,3},{3,2},{4,5},{5,4},{6,7},{7,6},{8,9},{9,8},{10,11... | collective-permute-start | bytes 3145736 | tf_op jit(solution)/shard_map/ppermute | solution.py:435
  29.7 2.2 %collective-permute-start.12 = (bf16[192,512]{1,0:T(8,128)(2,1)S(1)}, bf16[192,512]{1,0:T(8,128)(2,1)S(1)}, u32[]{:S(2)}, u32[]{:S(2)}) collective-permute-start(bf16[192,512]{1,0:T(8,128)(2,1)S(1)} %collective-permute-done.5.refs_0_), channel_id=1, source_target_pairs={{0,2},{2,0},{4,6},{6,4},{8,10},{10,8},{12,14},{14,12},{16,18},{18,... | collective-permute-start | bytes 589832 | tf_op jit(solution)/shard_map/ppermute | solution.py:432
  29.8 2.1 %collective-permute-start.14 = (bf16[192,512]{1,0:T(8,128)(2,1)S(1)}, bf16[192,512]{1,0:T(8,128)(2,1)S(1)}, u32[]{:S(2)}, u32[]{:S(2)}) collective-permute-start(bf16[192,512]{1,0:T(8,128)(2,1)S(1)} %collective-permute-done.6.refs_2_), channel_id=1, source_target_pairs={{0,2},{2,0},{4,6},{6,4},{8,10},{10,8},{12,14},{14,12},{16,18},{18,... | collective-permute-start | bytes 589832 | tf_op jit(solution)/shard_map/ppermute | solution.py:432
  30.3 1.6 %collective-permute-start.13 = (bf16[192,512]{1,0:T(8,128)(2,1)S(1)}, bf16[192,512]{1,0:T(8,128)(2,1)S(1)}, u32[]{:S(2)}, u32[]{:S(2)}) collective-permute-start(bf16[192,512]{1,0:T(8,128)(2,1)S(1)} %collective-permute-done.7.refs_1_), channel_id=1, source_target_pairs={{0,2},{2,0},{4,6},{6,4},{8,10},{10,8},{12,14},{14,12},{16,18},{18,... | collective-permute-start | bytes 589832 | tf_op jit(solution)/shard_map/ppermute | solution.py:432
  30.4 7.3 %collective-permute-start.11 = (bf16[192,512]{1,0:T(8,128)(2,1)S(1)}, bf16[192,512]{1,0:T(8,128)(2,1)S(1)}, u32[]{:S(2)}, u32[]{:S(2)}) collective-permute-start(bf16[192,512]{1,0:T(8,128)(2,1)S(1)} %collective-permute-done.7.refs_1_), channel_id=1, source_target_pairs={{0,4},{2,6},{4,0},{6,2},{8,12},{10,14},{12,8},{14,10},{16,20},{18,... | collective-permute-start | bytes 589832 | tf_op jit(solution)/shard_map/ppermute | solution.py:432
  37.6 2.5 %collective-permute-start.16 = (bf16[512,512]{1,0:T(8,128)(2,1)S(1)}, bf16[512,512]{1,0:T(8,128)(2,1)}, u32[]{:S(2)}, u32[]{:S(2)}) collective-permute-start(bf16[512,512]{1,0:T(8,128)(2,1)S(1)} %collective-permute-done.10.refs_6_.refs_0_), channel_id=1, source_target_pairs={{0,2},{2,0},{4,6},{6,4},{8,10},{10,8},{12,14},{14,12},{16,18},{18,... | collective-permute-start | bytes 1572872 | tf_op jit(solution)/shard_map/ppermute | solution.py:432
  37.6 2.5 %collective-permute-start.15 = (bf16[192,512]{1,0:T(8,128)(2,1)S(1)}, bf16[192,512]{1,0:T(8,128)(2,1)S(1)}, u32[]{:S(2)}, u32[]{:S(2)}) collective-permute-start(bf16[192,512]{1,0:T(8,128)(2,1)S(1)} %collective-permute-done.11.refs_0_), channel_id=1, source_target_pairs={{0,2},{2,0},{4,6},{6,4},{8,10},{10,8},{12,14},{14,12},{16,18},{18,... | collective-permute-start | bytes 589832 | tf_op jit(solution)/shard_map/ppermute | solution.py:432
  38.1 8.7 %collective-permute-start.18 = (bf16[512,256]{1,0:T(8,128)(2,1)}, bf16[512,256]{1,0:T(8,128)(2,1)}, u32[]{:S(2)}, u32[]{:S(2)}) collective-permute-start(bf16[512,256]{1,0:T(8,128)(2,1)} %get-tuple-element.120), channel_id=1, source_target_pairs={{0,8},{2,10},{4,12},{6,14},{8,0},{10,2},{12,4},{14,6},{16,24},{18,... | collective-permute-start | bytes 786440 | tf_op jit(solution)/shard_map/ppermute | solution.py:432
  38.6 8.3 %collective-permute-start.19 = (bf16[512,256]{1,0:T(8,128)(2,1)S(1)}, bf16[512,256]{1,0:T(8,128)(2,1)}, u32[]{:S(2)}, u32[]{:S(2)}) collective-permute-start(bf16[512,256]{1,0:T(8,128)(2,1)S(1)} %get-tuple-element.121), channel_id=1, source_target_pairs={{0,4},{2,6},{4,0},{6,2},{8,12},{10,14},{12,8},{14,10},{16,20},{18,... | collective-permute-start | bytes 786440 | tf_op jit(solution)/shard_map/ppermute | solution.py:432
  42.6 7.6 %collective-permute-start.17 = (bf16[192,512]{1,0:T(8,128)(2,1)}, bf16[192,512]{1,0:T(8,128)(2,1)S(1)}, u32[]{:S(2)}, u32[]{:S(2)}) collective-permute-start(bf16[192,512]{1,0:T(8,128)(2,1)} %get-tuple-element.114), channel_id=1, source_target_pairs={{0,1},{1,0},{2,3},{3,2},{4,5},{5,4},{6,7},{7,6},{8,9},{9,8},{10,11... | collective-permute-start | bytes 589832 | tf_op jit(solution)/shard_map/ppermute | solution.py:435
  46.8 5.2 %collective-permute-start.22 = (bf16[512,256]{1,0:T(8,128)(2,1)}, bf16[512,256]{1,0:T(8,128)(2,1)S(1)}, u32[]{:S(2)}, u32[]{:S(2)}) collective-permute-start(bf16[512,256]{1,0:T(8,128)(2,1)} %collective-permute-done.18.refs_2_), channel_id=1, source_target_pairs={{0,2},{2,0},{4,6},{6,4},{8,10},{10,8},{12,14},{14,12},{16,18},{18,... | collective-permute-start | bytes 786440 | tf_op jit(solution)/shard_map/ppermute | solution.py:432
  46.9 5.1 %collective-permute-start.23 = (bf16[512,256]{1,0:T(8,128)(2,1)}, bf16[512,256]{1,0:T(8,128)(2,1)S(1)}, u32[]{:S(2)}, u32[]{:S(2)}) collective-permute-start(bf16[512,256]{1,0:T(8,128)(2,1)} %collective-permute-done.19.refs_3_), channel_id=1, source_target_pairs={{0,2},{2,0},{4,6},{6,4},{8,10},{10,8},{12,14},{14,12},{16,18},{18,... | collective-permute-start | bytes 786440 | tf_op jit(solution)/shard_map/ppermute | solution.py:432
  47.4 4.7 %collective-permute-start.21 = (bf16[512,1024]{1,0:T(8,128)(2,1)S(1)}, bf16[512,1024]{1,0:T(8,128)(2,1)S(1)}, u32[]{:S(2)}, u32[]{:S(2)}) collective-permute-start(bf16[512,1024]{1,0:T(8,128)(2,1)S(1)} %collective-permute-done.20.refs_4_), channel_id=1, source_target_pairs={{0,2},{2,0},{4,6},{6,4},{8,10},{10,8},{12,14},{14,12},{16,18},{18,... | collective-permute-start | bytes 3145736 | tf_op jit(solution)/shard_map/ppermute | solution.py:432
